TPU v7x, 128 devices: a whole 4x4x4 slice. The times are simulated.
128 devices in a mesh: gz: 16 (over y, x), gy: 8 (over z, core).
Axes of the slice: x: 4, y: 4, z: 4, core: 2. Of those that a mesh axis runs over, the one named last changes fastest.
Arguments:
- density: float32 [256, 128, 1024], P('gz', 'gy'), may hold values from 0.1 to 10
Outputs:
- coefficients: float32 [256, 128, 1024], P('gz', 'gy')
All inputs are finite; a program needn't handle non-finite values.
Results may differ from a plain program's by a relative error of at most 0.00002.
Values sent between devices are 32-bit elements; how exact they have to be, the bound alone decides.
No kernel may reach another device: no remote copies, remote signals or barrier semaphores. Data moves between devices by JAX's collectives and lax.ppermute only.
A program may use at most 192 MiB of HBM per device.

v0:
```python
import functools

import jax
import jax.numpy as jnp
import numpy as np
from jax import lax
from jax.experimental import pallas as pl
from jax.experimental.pallas import tpu as pltpu
from jax.sharding import PartitionSpec as P

A1 = -1.586134342059924
B1 = -0.052980118572961
A2 = 0.882911075530934
B2 = 0.443506852043971
GAIN = 1.230174104914001

WIDE = 1024
LANES = 128
TILES = WIDE // LANES
HIGH = lax.Precision.HIGHEST


def lift(rows, left, right, first, last, choose):
    p, q = left
    s_next, r = right
    smooth, detail = rows[0::2], rows[1::2]
    m = len(smooth)
    s_next = choose(last, smooth[-1], s_next)
    d1 = [detail[i] + A1 * (smooth[i] + (smooth[i + 1] if i + 1 < m else s_next)) for i in range(m)]
    d1_before = choose(first, d1[0], p + A1 * smooth[0])
    s1 = [smooth[i] + B1 * ((d1[i - 1] if i else d1_before) + d1[i]) for i in range(m)]
    s1_after = choose(last, s1[-1], r + B1 * d1[-1])
    d2 = [d1[i] + A2 * (s1[i] + (s1[i + 1] if i + 1 < m else s1_after)) for i in range(m)]
    d2_before = choose(first, d2[0], d1_before + A2 * (q + B1 * d1_before + s1[0]))
    s2 = [s1[i] + B2 * ((d2[i - 1] if i else d2_before) + d2[i]) for i in range(m)]
    return [v * (1.0 / GAIN) for v in s2], [v * (GAIN / 2.0) for v in d2]


def lift_alone(rows):
    zero = jnp.zeros_like(rows[0])
    return lift(rows, (zero, zero), (zero, zero), False, False, lambda c, a, b: a if c else b)[0]


def edges(rows):
    s, d = rows[0::2], rows[1::2]
    to_right = (d[-1] + A1 * s[-1], s[-1] + B1 * (d[-2] + A1 * (s[-2] + s[-1])))
    to_left = (s[0], s[0] + B1 * (d[0] + A1 * (s[0] + s[1])))
    return to_right, to_left


def own_left(to_left):
    s, r = to_left
    c2 = (B2 * A2 * B1 * A1 / GAIN) * s
    c1 = ((B1 * A1 + B2 * A1 + 3 * B2 * A2 * B1 * A1) / GAIN) * s + (B2 * A2 / GAIN) * r
    return c1 + A1 * c2, (1 + B1 * A1) * c2


def own_right(to_right):
    p, q = to_right
    c0 = ((B1 + B2 + 3 * B2 * A2 * B1) / GAIN) * p + (B2 * A2 / GAIN) * q
    c1 = (B2 * A2 * B1 / GAIN) * p
    return c0, c0 + B1 * (c1 + A1 * c0)


def add_pairs(a, b):
    return a[0] + b[0], a[1] + b[1]


def mix(flag, a, b):
    return jnp.where(flag, a, b)


def interleave(smooth, detail):
    return [v for pair in zip(smooth, detail) for v in pair]


def lane_factors(stride):
    lane = np.arange(WIDE)
    odd = (lane % (2 * stride)) == stride
    even = (lane % (2 * stride)) == 0
    table = np.zeros((16, WIDE), np.float64)
    for k, a in enumerate((A1, B1, A2, B2)):
        at = even if k % 2 else odd
        table[k] = np.where(at, a, 0.0)
        table[4 + k] = np.where(at, a, 0.0)
        if k % 2:
            table[k, 0] = 0.0
            table[4 + k, 0] = 2 * a
        else:
            table[k, WIDE - stride] = 2 * a
            table[4 + k, WIDE - stride] = 0.0
    table[8] = np.where(even, 1.0 / GAIN, np.where(odd, GAIN / 2.0, 1.0))
    return table.astype(np.float32)


def lift_lanes(v, table, stride):
    for k in range(4):
        before = pltpu.roll(v, stride, 1)
        after = pltpu.roll(v, WIDE - stride, 1)
        v = v + table[k : k + 1, :] * before + table[4 + k : 5 + k, :] * after
    return v * table[8:9, :]


def lane_id(shape):
    return lax.broadcasted_iota(jnp.int32, shape, len(shape) - 1)


def pack_two(a, b, even):
    return jnp.where(even, a, pltpu.roll(b, 1, 1))


def unpack_two(w):
    return w, pltpu.roll(w, LANES - 1, 1)


def gather_tiles(ref, at):
    return jnp.concatenate([ref[t, at, :] for t in range(TILES)], axis=1)


def tile(t):
    return slice(t * LANES, (t + 1) * LANES)


def along_x(table, x, out, pay_e, pay_o):
    def plane(z, carry):
        at = pl.ds(pl.multiple_of(z * 16, 16), 16)
        v = lift_lanes(x[at, :], table, 1)
        for t in range(TILES):
            out[t, at, :] = v[:, tile(t)]
        return carry

    lax.fori_loop(0, 16, plane, 0)
    flip = lax.axis_index("gy") % 2 == 1
    even = lane_id((8, LANES)) % 2 == 0
    for half in range(2):
        for t in range(TILES):
            lanes = pl.ds(t * LANES, LANES)
            rows = [out[t, pl.ds(half * 128 + y, 8, stride=16), :] for y in range(16)]
            to_right, to_left = edges(rows)
            next_right, next_left = edges(lift_alone(rows))
            going_right = to_right + (pack_two(*next_right, even),)
            going_left = to_left + (pack_two(*next_left, even),)
            for c in range(3):
                pay_e[c, pl.ds(half * 8, 8), lanes] = mix(flip, going_left[c], going_right[c])
                pay_o[c, pl.ds(half * 8, 8), lanes] = mix(flip, going_right[c], going_left[c])


def along_y(x, got_e, got_o, one, two, pay_e, pay_o):
    me = lax.axis_index("gy")
    first, last, flip = me == 0, me == lax.axis_size("gy") - 1, me % 2 == 1
    even = lane_id((8, LANES)) % 2 == 0
    for half in range(2):
        for t in range(TILES):
            lanes = pl.ds(t * LANES, LANES)
            rows = [x[t, pl.ds(half * 128 + y, 8, stride=16), :] for y in range(16)]
            e = [got_e[c, pl.ds(half * 8, 8), lanes] for c in range(3)]
            o = [got_o[c, pl.ds(half * 8, 8), lanes] for c in range(3)]
            left = [mix(flip, e[c], o[c]) for c in range(3)]
            right = [mix(flip, o[c], e[c]) for c in range(3)]
            to_right, to_left = edges(rows)
            smooth, detail = lift(rows, left[:2], right[:2], first, last, mix)
            for y, v in enumerate(interleave(smooth, detail)):
                one[t, pl.ds(half * 128 + y, 8, stride=16), :] = v
            left2 = add_pairs(unpack_two(left[2]), own_left(to_left))
            right2 = add_pairs(unpack_two(right[2]), own_right(to_right))
            smooth, detail = lift(smooth, left2, right2, first, last, mix)
            for y, v in enumerate(interleave(smooth, detail)):
                two[t, pl.ds(half * 64 + y, 8, stride=8), :] = v
    flip = lax.axis_index("gz") % 2 == 1
    for t in range(TILES):
        lanes = pl.ds(t * LANES, LANES)
        going_right, going_left = [None] * 6, [None] * 6
        for half in range(2):
            rows = [one[t, pl.ds(z * 16 + half * 8, 8), :] for z in range(16)]
            to_right, to_left = edges(rows)
            for c in range(2):
                going_right[2 * c + half] = to_right[c]
                going_left[2 * c + half] = to_left[c]
        rows = [two[t, pl.ds(z * 8, 8), :] for z in range(16)]
        to_right, to_left = edges(rows)
        next_right, next_left = edges(lift_alone(rows))
        going_right[4:] = pack_two(*to_right, even), pack_two(*next_right, even)
        going_left[4:] = pack_two(*to_left, even), pack_two(*next_left, even)
        for c in range(6):
            pay_e[c, :, lanes] = mix(flip, going_left[c], going_right[c])
            pay_o[c, :, lanes] = mix(flip, going_right[c], going_left[c])


def along_z(table2, table3, one, two, got_e, got_o, out, pay, fine, spread):
    me = lax.axis_index("gz")
    first, last, flip = me == 0, me == lax.axis_size("gz") - 1, me % 2 == 1
    for t in range(TILES):
        lanes = pl.ds(t * LANES, LANES)
        e = [got_e[c, :, lanes] for c in range(6)]
        o = [got_o[c, :, lanes] for c in range(6)]
        left = [mix(flip, e[c], o[c]) for c in range(6)]
        right = [mix(flip, o[c], e[c]) for c in range(6)]
        for half in range(2):
            rows = [one[t, pl.ds(z * 16 + half * 8, 8), :] for z in range(16)]
            smooth, detail = lift(rows, left[half:4:2], right[half:4:2], first, last, mix)
            for z, v in enumerate(interleave(smooth, detail)):
                out[pl.ds(z * 16 + half * 8, 8), lanes] = v
        rows = [two[t, pl.ds(z * 8, 8), :] for z in range(16)]
        to_right, to_left = edges(rows)
        smooth, _ = lift(rows, unpack_two(left[4]), unpack_two(right[4]), first, last, mix)
        left2 = add_pairs(unpack_two(left[5]), own_left(to_left))
        right2 = add_pairs(unpack_two(right[5]), own_right(to_right))
        smooth, detail = lift(smooth, left2, right2, first, last, mix)
        for z, v in enumerate(interleave(smooth, detail)):
            fine[t, pl.ds(z * 8, 8), :] = v
    row = lax.broadcasted_iota(jnp.int32, (16, LANES), 0)
    here = (row % 2 == 0) & (lane_id((16, LANES)) % 2 == 0)
    for z in range(8):
        v = lift_lanes(gather_tiles(fine, pl.ds(z * 8, 8)), table2, 2)
        for t in range(TILES):
            part = v[:, tile(t)]
            if z % 2 == 0:
                fine[t, pl.ds(z * 8, 8), :] = part
            spread[t, pl.ds(z * 16, 8, stride=2), :] = part
            at, lanes = pl.ds(z * 32, 16), pl.ds(t * LANES, LANES)
            out[at, lanes] = jnp.where(here, spread[t, pl.ds(z * 16, 16), :], out[at, lanes])
    lane = lane_id((4, WIDE))
    packed = None
    for z in range(4):
        v = lift_lanes(gather_tiles(fine, pl.ds(z * 16, 4, stride=2)), table3, 4)
        packed = jnp.where(lane % 4 == z, pltpu.roll(v, z, 1), packed) if z else v
    for to in range(pay.shape[0]):
        pay[to, pl.ds(0, 4), :] = packed[:, : WIDE // 2]
        pay[to, pl.ds(4, 4), :] = packed[:, WIDE // 2 :]


def coarse_y(weights, got, pay, held):
    me = lax.axis_index("gy")
    rows = got[...].reshape(64, WIDE // 2)
    held[...] = jnp.dot(weights[me], rows, precision=HIGH, preferred_element_type=jnp.float32)
    lane = lane_id((2, WIDE // 2))
    four = jnp.where(lane % 8 < 4, held[pl.ds(8, 2), :], pltpu.roll(held[pl.ds(10, 2), :], 4, 1))
    three = held[pl.ds(0, 8), :]
    for to in range(pay.shape[0]):
        pay[to, :, pl.ds(0, WIDE // 2)] = three
        for part in range(4):
            pay[to, pl.ds(2 * part, 2), pl.ds(WIDE // 2, LANES)] = four[:, tile(part)]


def coarse_z(table4, weights3, weights4, got, base, out, planes, three, four, spread, sem):
    loads = [pltpu.make_async_copy(base.at[4 * i], planes.at[i], sem.at[i]) for i in range(4)]
    for load in loads:
        load.start()
    me = lax.axis_index("gz")
    half = WIDE // 2
    g3 = jnp.dot(
        weights3[me], got[:, :, pl.ds(0, half)].reshape(128, half), precision=HIGH, preferred_element_type=jnp.float32
    )
    g4 = jnp.dot(
        weights4[me], got[:, :, pl.ds(half, LANES)].reshape(128, LANES), precision=HIGH, preferred_element_type=jnp.float32
    )
    sum3 = g3[0:32]
    for j in range(1, 4):
        sum3 = sum3 + pltpu.roll(g3[j * 32 : j * 32 + 32], half - j, 1)
    for o in range(4):
        for h in range(2):
            part = sum3[o * 8 + h * 4 : o * 8 + h * 4 + 4]
            for t in range(TILES // 2):
                three[h * (TILES // 2) + t, pl.ds(o * 4, 4), :] = part[:, tile(t)]
    for h in range(2):
        sum4 = g4[0:16] if h == 0 else pltpu.roll(g4[0:16], LANES - 4, 1)
        for j in range(1, 4):
            sum4 = sum4 + pltpu.roll(g4[j * 16 : j * 16 + 16], LANES - 4 * h - j, 1)
        for o in range(2):
            for part in range(4):
                at = o * 8 + part * 2
                four[pl.ds(o * 2, 2), pl.ds(h * half + part * LANES, LANES)] = sum4[at : at + 2]
    last = lift_lanes(four[...], table4, 8)
    lane = lane_id((2, LANES))
    for o in range(2):
        at = pl.ds(o * 8, 2, stride=2)
        for t in range(TILES):
            three[t, at, :] = jnp.where(lane % 8 == 0, last[o * 2 : o * 2 + 2, tile(t)], three[t, at, :])
    for load in loads:
        load.wait()
    row = lax.broadcasted_iota(jnp.int32, (16, LANES), 0)
    here = (row % 4 == 0) & (lane_id((16, LANES)) % 4 == 0)
    stores = []
    for i in range(4):
        for t in range(TILES):
            spread[t, pl.ds(i * 16, 4, stride=4), :] = three[t, pl.ds(i * 4, 4), :]
            lanes = pl.ds(t * LANES, LANES)
            planes[i, :, lanes] = jnp.where(here, spread[t, pl.ds(i * 16, 16), :], planes[i, :, lanes])
        stores.append(pltpu.make_async_copy(planes.at[i], out.at[4 * i], sem.at[i]))
        stores[-1].start()
    for store in stores:
        store.wait()


def two_levels(n):
    fixed = lambda c, a, b: a if c else b
    none = (0.0, 0.0)
    cells = list(np.eye(n))
    smooth, detail = lift(cells, none, none, True, True, fixed)
    upper = np.stack(interleave(smooth, detail))
    smooth, detail = lift(smooth, none, none, True, True, fixed)
    return upper, np.stack(interleave(smooth, detail))


def weights_y(devices):
    upper, lower = two_levels(4 * devices)
    out = np.zeros((devices, 16, devices, 2, 4), np.float64)
    for b in range(devices):
        for h in range(2):
            out[b, 4 * h : 4 * h + 4, :, h, :] = upper[4 * b : 4 * b + 4].reshape(4, devices, 4)
            out[b, 8 + 2 * h : 10 + 2 * h, :, h, :] = lower[2 * b : 2 * b + 2].reshape(2, devices, 4)
    return out.reshape(devices, 16, devices * 8).astype(np.float32)


def weights_z(devices):
    upper, lower = two_levels(4 * devices)
    w3 = np.zeros((devices, 4, 4, 8, devices, 8), np.float64)
    w4 = np.zeros((devices, 4, 2, 8, devices, 8), np.float64)
    for a in range(devices):
        u = upper[4 * a : 4 * a + 4].reshape(4, devices, 4)
        v = lower[2 * a : 2 * a + 2].reshape(2, devices, 4)
        for j in range(4):
            for r in range(8):
                w3[a, j, :, r, :, r] = u[:, :, j]
                w4[a, j, :, r, :, r] = v[:, :, j]
    return (
        w3.reshape(devices, 128, devices * 8).astype(np.float32),
        w4.reshape(devices, 64, devices * 8).astype(np.float32),
    )


def swap(values, axis, start):
    devices = lax.axis_size(axis)
    pairs = []
    for i in range(start, devices - 1, 2):
        pairs += [(i, i + 1), (i + 1, i)]
    return lax.ppermute(values, axis, pairs)


def f32(*shape):
    return jax.ShapeDtypeStruct(shape, jnp.float32)


def call(body, out, scratch=(), **more):
    return pl.pallas_call(
        body,
        out_shape=out,
        scratch_shapes=list(scratch),
        compiler_params=pltpu.CompilerParams(vmem_limit_bytes=24 * 1024 * 1024),
        **more,
    )


def per_device(density):
    planes, rows, cells = density.shape
    ny, nz = lax.axis_size("gy"), lax.axis_size("gz")
    tables = [jnp.asarray(lane_factors(s)) for s in (1, 2, 4, 8)]
    flat = density.reshape(planes * rows, cells)
    tiled = f32(TILES, planes * rows, LANES)
    payload = f32(3, 16, cells)
    x, pay_e, pay_o = call(along_x, [tiled, payload, payload])(tables[0], flat)
    got_e, got_o = swap(pay_e, "gy", 0), swap(pay_o, "gy", 1)
    payload = f32(6, 8, cells)
    one, two, pay_e, pay_o = call(along_y, [tiled, f32(TILES, planes * rows // 2, LANES), payload, payload])(
        x, got_e, got_o
    )
    got_e, got_o = swap(pay_e, "gz", 0), swap(pay_o, "gz", 1)
    base, pay = call(
        along_z,
        [f32(planes * rows, cells), f32(ny, 8, cells // 2)],
        [pltpu.VMEM((TILES, 64, LANES), jnp.float32), pltpu.VMEM((TILES, 128, LANES), jnp.float32)],
    )(tables[1], tables[2], one, two, got_e, got_o)
    got = lax.all_to_all(pay, "gy", 0, 0, tiled=True)
    pay = call(coarse_y, f32(nz, 8, cells // 2 + LANES), [pltpu.VMEM((16, cells // 2), jnp.float32)])(
        jnp.asarray(weights_y(ny)), got
    )
    got = lax.all_to_all(pay, "gz", 0, 0, tiled=True)
    w3, w4 = weights_z(nz)
    whole = pl.BlockSpec(memory_space=pltpu.VMEM)
    return call(
        coarse_z,
        f32(planes, rows, cells),
        [
            pltpu.VMEM((4, rows, cells), jnp.float32),
            pltpu.VMEM((TILES, 16, LANES), jnp.float32),
            pltpu.VMEM((4, cells), jnp.float32),
            pltpu.VMEM((TILES, 64, LANES), jnp.float32),
            pltpu.SemaphoreType.DMA((4,)),
        ],
        in_specs=[whole] * 4 + [pl.BlockSpec(memory_space=pl.ANY)],
        out_specs=pl.BlockSpec(memory_space=pl.ANY),
        input_output_aliases={4: 0},
    )(tables[3], jnp.asarray(w3), jnp.asarray(w4), got, base.reshape(planes, rows, cells))


def solution(mesh):
    return jax.shard_map(
        per_device, mesh=mesh, in_specs=(P("gz", "gy", None),), out_specs=P("gz", "gy", None), check_vma=False
    )
```

profile of v0, /device:TPU:0, one launch (start us, length us, event | category | flops | bytes accessed | tf_op | source)
XLA Modules:
  0.0 61.6 jit_solution(6553873574818166186)
XLA Ops:
  0.0 0.0 copy-start
  0.0 1.2 %copy-done = f32[16,16,1024]{2,1,0:T(8,128)S(1)} copy-done((f32[16,16,1024]{2,1,0:T(8,128)S(1)}, f32[16,16,1024]{2,1,0:T(8,128)}, u32[]{:S(2)}) %copy-start) | copy-done | bytes 1048600
  1.2 0.0 copy-start.6
  1.2 0.8 %copy-done.6 = f32[16,1024]{1,0:T(8,128)S(1)} copy-done((f32[16,1024]{1,0:T(8,128)S(1)}, f32[16,1024]{1,0:T(8,128)}, u32[]{:S(2)}) %copy-start.6) | copy-done | bytes 65560
  2.1 6.5 %shard_map.82 = (f32[8,256,128]{2,1,0:T(8,128)S(1)}, f32[3,16,1024]{2,1,0:T(8,128)S(1)}, f32[3,16,1024]{2,1,0:T(8,128)S(1)}) custom-call(f32[16,1024]{1,0:T(8,128)S(1)} %copy-done.6, f32[256,1024]{1,0:T(8,128)S(1)} %bitcast.2), custom_call_target="tpu_custom_call" | custom-call | tf_op jit(solution)/shard_map/pallas_call | solution.py:361
  8.6 0.1 collective-permute-start
  8.7 0.7 %collective-permute-start.1 = (f32[3,16,1024]{2,1,0:T(8,128)S(1)}, f32[3,16,1024]{2,1,0:T(8,128)S(1)}, u32[]{:S(2)}, u32[]{:S(2)}) collective-permute-start(f32[3,16,1024]{2,1,0:T(8,128)S(1)} %get-tuple-element.16), channel_id=1, source_target_pairs={{1,2},{2,1},{3,4},{4,3},{5,6},{6,5},{9,10},{10,9},{11,12},{12,11},... | collective-permute-start | bytes 589832 | tf_op jit(solution)/shard_map/ppermute | solution.py:337
  9.3 0.7 %collective-permute-done.got_e = f32[3,16,1024]{2,1,0:T(8,128)S(1)} collective-permute-done((f32[3,16,1024]{2,1,0:T(8,128)S(1)}, f32[3,16,1024]{2,1,0:T(8,128)S(1)}, u32[]{:S(2)}, u32[]{:S(2)}) %collective-permute-start) | collective-permute-done | bytes 196640 | tf_op jit(solution)/shard_map/ppermute | solution.py:337
  10.1 0.0 collective-permute-done.1.got_o
  10.1 0.0 copy-start.4
  10.1 0.0 copy-start.5
  10.1 1.4 %shard_map.83 = (f32[8,256,128]{2,1,0:T(8,128)S(1)}, f32[8,128,128]{2,1,0:T(8,128)S(1)}, f32[6,8,1024]{2,1,0:T(8,128)S(1)}, f32[6,8,1024]{2,1,0:T(8,128)S(1)}) custom-call(f32[8,256,128]{2,1,0:T(8,128)S(1)} %get-tuple-element.14.x, f32[3,16,1024]{2,1,0:T(8,128)S(1)} %collective-permute-done.got_e, f32[3,16,1024]{2,1,0:T(8,128)S(1)} %collective-permute-done.1.got_o), custom_call_target="tpu_custom_call" | custom-call | tf_op jit(solution)/shard_map/pallas_call | solution.py:364
  11.4 1.7 %collective-permute-start.2 = (f32[6,8,1024]{2,1,0:T(8,128)S(1)}, f32[6,8,1024]{2,1,0:T(8,128)S(1)}, u32[]{:S(2)}, u32[]{:S(2)}) collective-permute-start(f32[6,8,1024]{2,1,0:T(8,128)S(1)} %get-tuple-element.19), channel_id=1, source_target_pairs={{0,8},{8,0},{16,24},{24,16},{32,40},{40,32},{48,56},{56,48},{64,72... | collective-permute-start | bytes 589832 | tf_op jit(solution)/shard_map/ppermute | solution.py:337
  13.1 0.7 %collective-permute-start.3 = (f32[6,8,1024]{2,1,0:T(8,128)S(1)}, f32[6,8,1024]{2,1,0:T(8,128)S(1)}, u32[]{:S(2)}, u32[]{:S(2)}) collective-permute-start(f32[6,8,1024]{2,1,0:T(8,128)S(1)} %get-tuple-element.20), channel_id=1, source_target_pairs={{8,16},{16,8},{24,32},{32,24},{40,48},{48,40},{56,64},{64,56},{72,... | collective-permute-start | bytes 589832 | tf_op jit(solution)/shard_map/ppermute | solution.py:337
  13.8 3.4 %collective-permute-done.2.got_e = f32[6,8,1024]{2,1,0:T(8,128)S(1)} collective-permute-done((f32[6,8,1024]{2,1,0:T(8,128)S(1)}, f32[6,8,1024]{2,1,0:T(8,128)S(1)}, u32[]{:S(2)}, u32[]{:S(2)}) %collective-permute-start.2) | collective-permute-done | bytes 196640 | tf_op jit(solution)/shard_map/ppermute | solution.py:337
  17.2 0.0 collective-permute-done.3.got_o
  17.2 0.0 copy-done.4
  17.2 0.0 copy-done.5
  17.2 0.0 copy-start.7
  17.2 0.0 copy-start.2
  17.2 2.7 %shard_map.84 = (f32[256,1024]{1,0:T(8,128)}, f32[8,8,512]{2,1,0:T(8,128)S(1)}) custom-call(f32[16,1024]{1,0:T(8,128)S(1)} %copy-done.5, f32[16,1024]{1,0:T(8,128)S(1)} %copy-done.4, f32[8,256,128]{2,1,0:T(8,128)S(1)} %get-tuple-element.17.one, f32[8,128,128]{2,1,0:T(8,128)S(1)} %get-tuple-element.18.two, f32[6,8,1024]{2,1,0:T(8,128)S(1)} %collective-permute-done.2.got_e, ...), custom_call_target="tpu_custom_call" | custom-call | tf_op jit(solution)/shard_map/pallas_call | solution.py:368
  19.9 0.0 copy-start.1
  19.9 18.5 %all_to_all.10.got = f32[8,8,512]{2,1,0:T(8,128)S(1)} all-to-all(f32[8,8,512]{2,1,0:T(8,128)S(1)} %get-tuple-element.21), channel_id=1, replica_groups=mesh['gz'=16,'gy'=8] {'gy'}, dimensions={0} | all-to-all | bytes 262144 | tf_op jit(solution)/shard_map/all_to_all | solution.py:373
  38.4 0.0 copy-done.7
  38.4 0.3 shard_map.85
  38.7 0.0 copy-start.3
  38.7 20.4 %all_to_all.11.got = f32[16,8,640]{2,1,0:T(8,128)S(1)} all-to-all(f32[16,8,640]{2,1,0:T(8,128)S(1)} %shard_map.85), channel_id=1, replica_groups=mesh['gz'=16,'gy'=8] {'gz'}, dimensions={0} | all-to-all | bytes 655360 | tf_op jit(solution)/shard_map/all_to_all | solution.py:377
  59.1 0.0 copy-done.2
  59.1 0.0 copy-done.1
  59.1 0.0 copy-done.3
  59.1 2.4 %shard_map.86 = f32[16,16,1024]{2,1,0:T(8,128)} custom-call(f32[16,1024]{1,0:T(8,128)S(1)} %copy-done.3, f32[16,128,128]{2,1,0:T(8,128)S(1)} %copy-done.1, f32[16,64,128]{2,1,0:T(8,128)S(1)} %copy-done.2, f32[16,8,640]{2,1,0:T(8,128)S(1)} %all_to_all.11.got, f32[16,16,1024]{2,1,0:T(8,128)} %bitcast.3), custom_call_target="tpu_custom_call", output_to_operand_aliasing={{}: (4, {})} | custom-call | tf_op jit(solution)/shard_map/pallas_call | solution.py:380
Async XLA Ops:
  0.0 1.2 %copy-start = (f32[16,16,1024]{2,1,0:T(8,128)S(1)}, f32[16,16,1024]{2,1,0:T(8,128)}, u32[]{:S(2)}) copy-start(f32[16,16,1024]{2,1,0:T(8,128)} %param.8) | copy-start | bytes 3145732
  1.2 0.8 %copy-start.6 = (f32[16,1024]{1,0:T(8,128)S(1)}, f32[16,1024]{1,0:T(8,128)}, u32[]{:S(2)}) copy-start(f32[16,1024]{1,0:T(8,128)} %constant.14.clone.table) | copy-start | bytes 196612
  8.6 1.5 %collective-permute-start = (f32[3,16,1024]{2,1,0:T(8,128)S(1)}, f32[3,16,1024]{2,1,0:T(8,128)S(1)}, u32[]{:S(2)}, u32[]{:S(2)}) collective-permute-start(f32[3,16,1024]{2,1,0:T(8,128)S(1)} %get-tuple-element.15), channel_id=1, source_target_pairs={{0,1},{1,0},{2,3},{3,2},{4,5},{5,4},{6,7},{7,6},{8,9},{9,8},{10,11... | collective-permute-start | bytes 589832 | tf_op jit(solution)/shard_map/ppermute | solution.py:337
  8.7 1.4 %collective-permute-start.1 = (f32[3,16,1024]{2,1,0:T(8,128)S(1)}, f32[3,16,1024]{2,1,0:T(8,128)S(1)}, u32[]{:S(2)}, u32[]{:S(2)}) collective-permute-start(f32[3,16,1024]{2,1,0:T(8,128)S(1)} %get-tuple-element.16), channel_id=1, source_target_pairs={{1,2},{2,1},{3,4},{4,3},{5,6},{6,5},{9,10},{10,9},{11,12},{12,11},... | collective-permute-start | bytes 589832 | tf_op jit(solution)/shard_map/ppermute | solution.py:337
  10.1 7.1 %copy-start.4 = (f32[16,1024]{1,0:T(8,128)S(1)}, f32[16,1024]{1,0:T(8,128)}, u32[]{:S(2)}) copy-start(f32[16,1024]{1,0:T(8,128)} %constant.16.clone.table3) | copy-start | bytes 196612
  10.1 7.1 %copy-start.5 = (f32[16,1024]{1,0:T(8,128)S(1)}, f32[16,1024]{1,0:T(8,128)}, u32[]{:S(2)}) copy-start(f32[16,1024]{1,0:T(8,128)} %constant.15.clone.table2) | copy-start | bytes 196612
  11.4 5.7 %collective-permute-start.2 = (f32[6,8,1024]{2,1,0:T(8,128)S(1)}, f32[6,8,1024]{2,1,0:T(8,128)S(1)}, u32[]{:S(2)}, u32[]{:S(2)}) collective-permute-start(f32[6,8,1024]{2,1,0:T(8,128)S(1)} %get-tuple-element.19), channel_id=1, source_target_pairs={{0,8},{8,0},{16,24},{24,16},{32,40},{40,32},{48,56},{56,48},{64,72... | collective-permute-start | bytes 589832 | tf_op jit(solution)/shard_map/ppermute | solution.py:337
  13.1 4.1 %collective-permute-start.3 = (f32[6,8,1024]{2,1,0:T(8,128)S(1)}, f32[6,8,1024]{2,1,0:T(8,128)S(1)}, u32[]{:S(2)}, u32[]{:S(2)}) collective-permute-start(f32[6,8,1024]{2,1,0:T(8,128)S(1)} %get-tuple-element.20), channel_id=1, source_target_pairs={{8,16},{16,8},{24,32},{32,24},{40,48},{48,40},{56,64},{64,56},{72,... | collective-permute-start | bytes 589832 | tf_op jit(solution)/shard_map/ppermute | solution.py:337
  17.2 21.2 %copy-start.7 = (f32[8,16,64]{2,1,0:T(8,128)S(1)}, f32[8,16,64]{2,1,0:T(8,128)}, u32[]{:S(2)}) copy-start(f32[8,16,64]{2,1,0:T(8,128)} %constant.18.clone.weights) | copy-start | bytes 98308
  17.2 41.9 %copy-start.2 = (f32[16,64,128]{2,1,0:T(8,128)S(1)}, f32[16,64,128]{2,1,0:T(8,128)}, u32[]{:S(2)}) copy-start(f32[16,64,128]{2,1,0:T(8,128)} %constant.20.clone.weights4) | copy-start | bytes 1572868
  19.9 39.2 %copy-start.1 = (f32[16,128,128]{2,1,0:T(8,128)S(1)}, f32[16,128,128]{2,1,0:T(8,128)}, u32[]{:S(2)}) copy-start(f32[16,128,128]{2,1,0:T(8,128)} %constant.19.clone.weights3) | copy-start | bytes 3145732
  38.7 20.4 %copy-start.3 = (f32[16,1024]{1,0:T(8,128)S(1)}, f32[16,1024]{1,0:T(8,128)}, u32[]{:S(2)}) copy-start(f32[16,1024]{1,0:T(8,128)} %constant.17.clone.table4) | copy-start | bytes 196612
where the time goes:
time: 62 us; the launch traced here: 61.6 us
  blocking collectives  38.9 us (63%)
  Pallas kernels  13.3 us (21%)
  waiting for transfers between devices  4.18 us (7%)
  starting transfers between devices  3.04 us (5%)
  local copies, waits for them, and re-layouts  2.09 us (3%)
    all_to_all x1, blocking collectives, per_device(): got = lax.all_to_all(pay, 'gz', 0, 0, tiled=True)  20.4 us
    all_to_all x1, blocking collectives, per_device(): got = lax.all_to_all(pay, 'gy', 0, 0, tiled=True)  18.5 us
    pallas_call x1, Pallas kernels, per_device(): x, pay_e, pay_o = call(along_x, [tiled, payload, payload])(tables[0], flat)  6.53 us
    ppermute x4, waiting for transfers between devices, swap(): return lax.ppermute(values, axis, pairs)  4.18 us
    ppermute x4, starting transfers between devices, swap(): return lax.ppermute(values, axis, pairs)  3.04 us
    pallas_call x1, Pallas kernels, per_device(): call(along_z, [f32(planes * rows, cells), f32(ny, 8, cells // 2)], [pltpu...  2.7 us
    pallas_call x1, Pallas kernels, per_device(): call(coarse_z, f32(planes, rows, cells), [pltpu.VMEM((4, rows, cells), jn...  2.44 us
    unnamed x16, local copies, waits for them, and re-layouts  2.09 us
  transfers between devices with their start and end apart: 4, of which 2 were waited for; matrix products, arithmetic and copies ran while one was open for 0% of the time, Pallas kernels for 0%

commit v1 on v0

v1 whole, which is shorter than its diff:
```python
import functools

import jax
import jax.numpy as jnp
import numpy as np
from jax import lax
from jax.experimental import pallas as pl
from jax.experimental.pallas import tpu as pltpu
from jax.sharding import PartitionSpec as P

A1 = -1.586134342059924
B1 = -0.052980118572961
A2 = 0.882911075530934
B2 = 0.443506852043971
GAIN = 1.230174104914001

WIDE = 1024
LANES = 128
TILES = WIDE // LANES
HIGH = lax.Precision.HIGHEST


def lift(rows, left, right, first, last, choose):
    p, q = left
    s_next, r = right
    smooth, detail = rows[0::2], rows[1::2]
    m = len(smooth)
    s_next = choose(last, smooth[-1], s_next)
    d1 = [detail[i] + A1 * (smooth[i] + (smooth[i + 1] if i + 1 < m else s_next)) for i in range(m)]
    d1_before = choose(first, d1[0], p + A1 * smooth[0])
    s1 = [smooth[i] + B1 * ((d1[i - 1] if i else d1_before) + d1[i]) for i in range(m)]
    s1_after = choose(last, s1[-1], r + B1 * d1[-1])
    d2 = [d1[i] + A2 * (s1[i] + (s1[i + 1] if i + 1 < m else s1_after)) for i in range(m)]
    d2_before = choose(first, d2[0], d1_before + A2 * (q + B1 * d1_before + s1[0]))
    s2 = [s1[i] + B2 * ((d2[i - 1] if i else d2_before) + d2[i]) for i in range(m)]
    return [v * (1.0 / GAIN) for v in s2], [v * (GAIN / 2.0) for v in d2]


def lift_alone(rows):
    zero = jnp.zeros_like(rows[0])
    return lift(rows, (zero, zero), (zero, zero), False, False, lambda c, a, b: a if c else b)[0]


def edges(rows):
    s, d = rows[0::2], rows[1::2]
    to_right = (d[-1] + A1 * s[-1], s[-1] + B1 * (d[-2] + A1 * (s[-2] + s[-1])))
    to_left = (s[0], s[0] + B1 * (d[0] + A1 * (s[0] + s[1])))
    return to_right, to_left


def own_left(to_left):
    s, r = to_left
    c2 = (B2 * A2 * B1 * A1 / GAIN) * s
    c1 = ((B1 * A1 + B2 * A1 + 3 * B2 * A2 * B1 * A1) / GAIN) * s + (B2 * A2 / GAIN) * r
    return c1 + A1 * c2, (1 + B1 * A1) * c2


def own_right(to_right):
    p, q = to_right
    c0 = ((B1 + B2 + 3 * B2 * A2 * B1) / GAIN) * p + (B2 * A2 / GAIN) * q
    c1 = (B2 * A2 * B1 / GAIN) * p
    return c0, c0 + B1 * (c1 + A1 * c0)


def add_pairs(a, b):
    return a[0] + b[0], a[1] + b[1]


def mix(flag, a, b):
    return jnp.where(flag, a, b)


def interleave(smooth, detail):
    return [v for pair in zip(smooth, detail) for v in pair]


def lane_factors(stride):
    run = np.arange(WIDE) // stride
    ends = run[-1]
    odd, even = run % 2 == 1, run % 2 == 0
    table = np.zeros((16, WIDE), np.float64)
    for k, a in enumerate((A1, B1, A2, B2)):
        at = even if k % 2 else odd
        closed = run == (0 if k % 2 else ends)
        before, after = (4 + k, k) if k % 2 else (k, 4 + k)
        table[before] = np.where(at, np.where(closed, 2 * a, a), 0.0)
        table[after] = np.where(at & ~closed, a, 0.0)
    table[8] = np.where(even, 1.0 / GAIN, GAIN / 2.0)
    return table.astype(np.float32)


def lift_lanes(v, table, stride):
    for k in range(4):
        before = pltpu.roll(v, stride, 1)
        after = pltpu.roll(v, WIDE - stride, 1)
        v = v + table[k : k + 1, :] * before + table[4 + k : 5 + k, :] * after
    return v * table[8:9, :]


def lane_id(shape):
    return lax.broadcasted_iota(jnp.int32, shape, len(shape) - 1)


def pack_two(a, b, even):
    return jnp.where(even, a, pltpu.roll(b, 1, 1))


def unpack_two(w):
    return w, pltpu.roll(w, LANES - 1, 1)


def gather_tiles(ref, at):
    return jnp.concatenate([ref[t, at, :] for t in range(TILES)], axis=1)


def tile(t):
    return slice(t * LANES, (t + 1) * LANES)


def times(count, body, unroll=1):
    def step(i, carry):
        body(i)
        return carry

    lax.fori_loop(0, count, step, 0, unroll=unroll)


def tile_lanes(t):
    return pl.ds(pl.multiple_of(t * LANES, LANES), LANES)


def lift_two(a, b, phase):
    lane = lane_id((a[0].shape[0], LANES))
    here = lane % (2 * phase) < phase
    count, reach = len(a), 2 * phase
    s = [jnp.where(here, x, pltpu.roll(y, phase, 1)) for x, y in zip(a, b)]
    d = [jnp.where(here, pltpu.roll(x, LANES - phase, 1), y) for x, y in zip(a, b)]

    def ahead(x):
        r = [pltpu.roll(w, LANES - reach, 1) for w in x]
        return [jnp.where(lane < LANES - reach, r[t], r[t + 1] if t + 1 < count else x[t]) for t in range(count)]

    def behind(x):
        r = [pltpu.roll(w, reach, 1) for w in x]
        return [jnp.where(lane >= reach, r[t], r[t - 1] if t else x[t]) for t in range(count)]

    d = [x + A1 * (y + z) for x, y, z in zip(d, s, ahead(s))]
    s = [x + B1 * (y + z) for x, y, z in zip(s, d, behind(d))]
    d = [x + A2 * (y + z) for x, y, z in zip(d, s, ahead(s))]
    s = [(x + B2 * (y + z)) * (1.0 / GAIN) for x, y, z in zip(s, d, behind(d))]
    return s, [x * (GAIN / 2.0) for x in d]


def separate(s, d, phase):
    here = lane_id(s[0].shape) % (2 * phase) < phase
    a = [jnp.where(here, x, pltpu.roll(y, phase, 1)) for x, y in zip(s, d)]
    b = [jnp.where(here, pltpu.roll(x, LANES - phase, 1), y) for x, y in zip(s, d)]
    return a, b


def tiles_of(ref, at):
    v = ref[at, :]
    return [v[:, tile(t)] for t in range(TILES)]


def put_tiles(ref, at, parts):
    for t, v in enumerate(parts):
        ref[at, tile(t)] = v


def along_x(weights3, weights4, density, out, pay_e, pay_o, own, pay, x, w3, w4, e1, e2, e3, sem):
    me = lax.axis_index("gy")
    part = x.shape[0] // 4
    loads = [
        pltpu.make_async_copy(density.at[pl.ds(k * part, part)], x.at[pl.ds(k * part, part)], sem.at[k])
        for k in (0, 2, 1, 3)
    ]
    loads.append(pltpu.make_async_copy(weights3.at[me], w3, sem.at[4]))
    loads.append(pltpu.make_async_copy(weights4.at[me], w4, sem.at[5]))
    for load in loads:
        load.start()

    def plane(i):
        z, y = i // 2, i % 2
        at = pl.multiple_of(z * 16 + y * 8, 8)
        far = pl.multiple_of(z * 16 + y * 8 + 128, 8)
        s, d = lift_two(tiles_of(x, pl.ds(at, 8)), tiles_of(x, pl.ds(far, 8)), 1)
        put_tiles(e1, pl.ds(at, 8), s)
        a, b = separate(s, d, 1)
        for t in range(TILES):
            out[t, pl.ds(at, 8), :] = a[t]
            out[t, pl.ds(far, 8), :] = b[t]

    loads[0].wait()
    loads[1].wait()
    times(8, plane, 4)
    loads[2].wait()
    loads[3].wait()
    times(8, lambda i: plane(i + 8), 4)

    def second(i):
        at = pl.multiple_of(i * 8, 8)
        s, _ = lift_two(tiles_of(e1, pl.ds(at, 8)), tiles_of(e1, pl.ds(at + 64, 8)), 2)
        put_tiles(e2, pl.ds(at, 8), s)

    times(8, second, 4)

    def third(i):
        at = pl.multiple_of(i * 8, 8)
        s, _ = lift_two(tiles_of(e2, pl.ds(at, 8)), tiles_of(e2, pl.ds(at + 32, 8)), 4)
        put_tiles(e3, pl.ds(at, 8), s)

    times(4, third, 4)
    loads[4].wait()
    loads[5].wait()
    flip = me % 2 == 1
    even = lane_id((8, LANES)) % 2 == 0
    three = jnp.dot(w3[...], e2[...], precision=HIGH, preferred_element_type=jnp.float32)
    own[...] = three[0:16]
    pay_e[3] = mix(flip, three[32:48], three[16:32])
    pay_o[3] = mix(flip, three[16:32], three[32:48])
    four = jnp.dot(w4[...], e3[...], precision=HIGH, preferred_element_type=jnp.float32)
    for to in range(pay.shape[0]):
        pay[to, :, 0:WIDE] = mix(to > me, three[48:56], three[56:64])
        pay[to, 0:4, WIDE:] = four[to * 4 : to * 4 + 4, : WIDE // 2]
        pay[to, 4:8, WIDE:] = four[to * 4 : to * 4 + 4, WIDE // 2 :]

    def column(t):
        lanes = tile_lanes(t)
        for half in range(2):
            rows = [out[t, pl.ds(half * 128 + y, 8, stride=16), :] for y in range(16)]
            to_right, to_left = edges(rows)
            next_right, next_left = edges(lift_alone(rows))
            going_right = to_right + (pack_two(*next_right, even),)
            going_left = to_left + (pack_two(*next_left, even),)
            for c in range(3):
                pay_e[c, pl.ds(half * 8, 8), lanes] = mix(flip, going_left[c], going_right[c])
                pay_o[c, pl.ds(half * 8, 8), lanes] = mix(flip, going_right[c], going_left[c])

    times(TILES, column, 2)


def along_y(near3, weights3, weights4, x, got_e, got_o, own, got, one, two, pay_e, pay_o, pay, n3, w3, w4, held3, held4, turned3, turned4, sem):
    mz = lax.axis_index("gz")
    loads = [
        pltpu.make_async_copy(near3, n3, sem.at[0]),
        pltpu.make_async_copy(weights3.at[mz], w3, sem.at[1]),
        pltpu.make_async_copy(weights4.at[mz], w4, sem.at[2]),
    ]
    for load in loads:
        load.start()
    me = lax.axis_index("gy")
    first, last, flip = me == 0, me == lax.axis_size("gy") - 1, me % 2 == 1
    even = lane_id((8, LANES)) % 2 == 0

    def column(t):
        lanes = tile_lanes(t)
        for half in range(2):
            rows = [x[t, pl.ds(half * 128 + y, 8, stride=16), :] for y in range(16)]
            e = [got_e[c, pl.ds(half * 8, 8), lanes] for c in range(3)]
            o = [got_o[c, pl.ds(half * 8, 8), lanes] for c in range(3)]
            left = [mix(flip, e[c], o[c]) for c in range(3)]
            right = [mix(flip, o[c], e[c]) for c in range(3)]
            to_right, to_left = edges(rows)
            smooth, detail = lift(rows, left[:2], right[:2], first, last, mix)
            for y, v in enumerate(interleave(smooth, detail)):
                one[t, pl.ds(half * 128 + y, 8, stride=16), :] = v
            left2 = add_pairs(unpack_two(left[2]), own_left(to_left))
            right2 = add_pairs(unpack_two(right[2]), own_right(to_right))
            smooth, detail = lift(smooth, left2, right2, first, last, mix)
            for y, v in enumerate(interleave(smooth, detail)):
                two[t, pl.ds(half * 64 + y, 8, stride=8), :] = v

    times(TILES, column, TILES)
    for load in loads:
        load.wait()
    far = jnp.concatenate(
        [
            mix(me >= 2, got[jnp.maximum(me - 2, 0), :, 0:WIDE], 0.0),
            mix(me + 2 < got.shape[0], got[jnp.minimum(me + 2, got.shape[0] - 1), :, 0:WIDE], 0.0),
        ],
        axis=0,
    )
    held3[...] = (own[...] + (got_e[3] + got_o[3])) + jnp.dot(
        n3[...], far, precision=HIGH, preferred_element_type=jnp.float32
    )
    four = got[0, :, WIDE:]
    for k in range(1, got.shape[0]):
        four = four + got[k, :, WIDE:]
    held4[:, 0 : WIDE // 2] = four[0:4]
    held4[:, WIDE // 2 :] = four[4:8]
    lane = lane_id((4, LANES))
    for t in range(TILES):
        rows = [held3[pl.ds(4 * r, 4), tile(t)] for r in range(4)]
        for f in range(4):
            v = None
            for r in range(4):
                moved = pltpu.roll(rows[r], (r - f) % LANES, 1) if r != f else rows[r]
                v = jnp.where(lane % 4 == r, moved, v) if r else moved
            turned3[pl.ds(4 * f, 4), tile(t)] = v
        v = held4[:, tile(t)]
        for f in range(8):
            turned4[pl.ds(4 * f, 4), tile(t)] = pltpu.roll(v, LANES - f, 1) if f else v
    three = jnp.dot(w3[...], turned3[...], precision=HIGH, preferred_element_type=jnp.float32)
    four = jnp.dot(w4[...], turned4[...], precision=HIGH, preferred_element_type=jnp.float32)
    count = pay.shape[0]
    lane = lane_id((count, LANES))
    for t in range(TILES):
        v = four[0:count, tile(t)]
        for k in range(1, 4):
            v = jnp.where(lane % 8 == k, pltpu.roll(four[k * count : (k + 1) * count, tile(t)], k, 1), v)
        pay[:, t, WIDE // 2 :] = v
    for to in range(count):
        pay[to, 0:4, 0 : WIDE // 2] = three[to * 4 : to * 4 + 4, : WIDE // 2]
        pay[to, 4:8, 0 : WIDE // 2] = three[to * 4 : to * 4 + 4, WIDE // 2 :]
    flip = lax.axis_index("gz") % 2 == 1

    def stack(t):
        lanes = tile_lanes(t)
        going_right, going_left = [None] * 6, [None] * 6
        for half in range(2):
            rows = [one[t, pl.ds(z * 16 + half * 8, 8), :] for z in range(16)]
            to_right, to_left = edges(rows)
            for c in range(2):
                going_right[2 * c + half] = to_right[c]
                going_left[2 * c + half] = to_left[c]
        rows = [two[t, pl.ds(z * 8, 8), :] for z in range(16)]
        to_right, to_left = edges(rows)
        next_right, next_left = edges(lift_alone(rows))
        going_right[4:] = pack_two(*to_right, even), pack_two(*next_right, even)
        going_left[4:] = pack_two(*to_left, even), pack_two(*next_left, even)
        for c in range(6):
            pay_e[c, :, lanes] = mix(flip, going_left[c], going_right[c])
            pay_o[c, :, lanes] = mix(flip, going_right[c], going_left[c])

    times(TILES, stack, TILES)


def along_z(tables, one, two, got_e, got_o, got, result, out, fine, spread, coarse, table, sem):
    load = pltpu.make_async_copy(tables, table, sem.at[16])
    load.start()
    me = lax.axis_index("gz")
    first, last, flip = me == 0, me == lax.axis_size("gz") - 1, me % 2 == 1

    def stack(t):
        lanes = tile_lanes(t)
        e = [got_e[c, :, lanes] for c in range(6)]
        o = [got_o[c, :, lanes] for c in range(6)]
        left = [mix(flip, e[c], o[c]) for c in range(6)]
        right = [mix(flip, o[c], e[c]) for c in range(6)]
        for half in range(2):
            rows = [one[t, pl.ds(z * 16 + half * 8, 8), :] for z in range(16)]
            smooth, detail = lift(rows, left[half:4:2], right[half:4:2], first, last, mix)
            for z, v in enumerate(interleave(smooth, detail)):
                out[z, pl.ds(half * 8, 8), lanes] = v
        rows = [two[t, pl.ds(z * 8, 8), :] for z in range(16)]
        to_right, to_left = edges(rows)
        smooth, _ = lift(rows, unpack_two(left[4]), unpack_two(right[4]), first, last, mix)
        left2 = add_pairs(unpack_two(left[5]), own_left(to_left))
        right2 = add_pairs(unpack_two(right[5]), own_right(to_right))
        smooth, detail = lift(smooth, left2, right2, first, last, mix)
        for z, v in enumerate(interleave(smooth, detail)):
            fine[pl.ds(z * 8, 8), lanes] = v

    times(TILES, stack, TILES)
    sends = [pltpu.make_async_copy(out.at[z], result.at[z], sem.at[z]) for z in range(16)]
    for z in range(1, 16, 2):
        sends[z].start()
    half = WIDE // 2
    load.wait()
    total = got[0]
    for k in range(1, got.shape[0]):
        total = total + got[k]
    three = jnp.concatenate([total[0:4, :half], total[4:8, :half]], axis=1)
    three = lift_lanes(three, table.at[1], 4)
    four = jnp.concatenate([total[t : t + 1, half:] for t in range(TILES)], axis=1)
    four = lift_lanes(four, table.at[2], 8)
    for t in range(TILES):
        v = three[:, tile(t)]
        for r in range(4):
            coarse[t, pl.ds(r, 4, stride=4), :] = pltpu.roll(v, LANES - r, 1) if r else v
        v = four[:, tile(t)]
        here = lane_id((1, LANES)) % 8 == 0
        for k in range(4):
            at = pl.ds((k // 2) * 8 + (k % 2) * 2, 1)
            moved = pltpu.roll(v, LANES - k, 1) if k else v
            coarse[t, at, :] = jnp.where(here, moved, coarse[t, at, :])
    row = lax.broadcasted_iota(jnp.int32, (16, LANES), 0)
    lane = lane_id((16, LANES))
    at_two = (row % 2 == 0) & (lane % 2 == 0)
    at_three = (row % 4 == 0) & (lane % 4 == 0)
    for z in range(8):
        v = lift_lanes(fine[pl.ds(z * 8, 8), :], table.at[0], 2)
        for t in range(TILES):
            spread[t, pl.ds(z * 16, 8, stride=2), :] = v[:, tile(t)]
            w = jnp.where(at_two, spread[t, pl.ds(z * 16, 16), :], out[2 * z, :, tile(t)])
            if z % 2 == 0:
                spread[t, pl.ds(z * 16, 4, stride=4), :] = coarse[t, pl.ds(z * 2, 4), :]
                w = jnp.where(at_three, spread[t, pl.ds(z * 16, 16), :], w)
            out[2 * z, :, tile(t)] = w
        sends[2 * z].start()
    for send in sends:
        send.wait()


def deep_levels(n):
    fixed = lambda c, a, b: a if c else b
    level = lambda rows: lift(rows, (0.0, 0.0), (0.0, 0.0), True, True, fixed)
    cells = level(level(list(np.eye(n)))[0])[0]
    smooth, detail = level(cells)
    return cells, np.stack(interleave(smooth, detail)), np.stack(interleave(*level(smooth)))


def weights_y(devices):
    cells, three, four = deep_levels(16 * devices)
    w3 = np.zeros((devices, 64, 4, 16), np.float64)
    w4 = np.zeros((devices, devices, 2, 2, 2, 16), np.float64)
    for a in range(devices):
        mine = slice(16 * a, 16 * a + 16)
        for k, b in enumerate((a, a + 1, a - 1)):
            for r in range(4):
                for z in range(4):
                    if 0 <= b < devices:
                        w3[a, 16 * k + 4 * r + z, z] = three[4 * b + r, mine]
        for z in range(4):
            for c in range(2):
                if a + 2 < devices:
                    w3[a, 48 + 4 * c + z, z] = edges(cells[4 * a + 4 : 4 * a + 8])[0][c][mine]
                if a - 2 >= 0:
                    w3[a, 56 + 4 * c + z, z] = edges(cells[4 * a - 4 : 4 * a])[1][c][mine]
        for z in range(2):
            w4[a, :, :, z, z] = four[:, mine].reshape(devices, 2, 16)
    near = np.zeros((4, 4, 4, 4), np.float64)
    fixed = lambda c, x, y: y
    for c in range(4):
        unit = [1.0 if c == k else 0.0 for k in range(4)]
        rows = interleave(*lift([0.0] * 4, unit[:2], unit[2:], False, False, fixed))
        for r in range(4):
            for z in range(4):
                near[r, z, c, z] = rows[r]
    return (
        near.reshape(16, 16).astype(np.float32),
        w3.reshape(devices, 64, 64).astype(np.float32),
        w4.reshape(devices, 4 * devices, 32).astype(np.float32),
    )


def weights_z(devices):
    _, three, four = deep_levels(16 * devices)
    w3 = np.zeros((devices, devices, 4, 4, 4), np.float64)
    w4 = np.zeros((devices, 2, 2, devices, 8, 2, 2), np.float64)
    for a in range(devices):
        for f in range(8):
            for zz in range(4):
                if f < 4:
                    z = 16 * a + zz + 4 * (f // 2) + 8 * (f % 2)
                    w3[a, :, :, f, zz] = three[:, z].reshape(devices, 4)
                if zz < 2:
                    z = 16 * a + zz + 2 * (f // 4) + 4 * (f // 2 % 2) + 8 * (f % 2)
                    for o in range(2):
                        w4[a, :, o, :, f, o, zz] = four[:, z].reshape(devices, 2).T
    return (
        w3.reshape(devices, 4 * devices, 16).astype(np.float32),
        w4.reshape(devices, 4 * devices, 32).astype(np.float32),
    )


def swap(values, axis, start):
    devices = lax.axis_size(axis)
    pairs = []
    for i in range(start, devices - 1, 2):
        pairs += [(i, i + 1), (i + 1, i)]
    return lax.ppermute(values, axis, pairs)


def f32(*shape):
    return jax.ShapeDtypeStruct(shape, jnp.float32)


def call(body, out, scratch=(), **more):
    return pl.pallas_call(
        body,
        out_shape=out,
        scratch_shapes=list(scratch),
        compiler_params=pltpu.CompilerParams(vmem_limit_bytes=24 * 1024 * 1024),
        **more,
    )


def per_device(density):
    planes, rows, cells = density.shape
    ny, nz = lax.axis_size("gy"), lax.axis_size("gz")
    near, y3, y4 = [jnp.asarray(w) for w in weights_y(ny)]
    z3, z4 = [jnp.asarray(w) for w in weights_z(nz)]
    tables = jnp.asarray(np.stack([lane_factors(s) for s in (2, 4, 8)]))
    vmem = lambda *shape: pltpu.VMEM(shape, jnp.float32)
    sems = lambda count: pltpu.SemaphoreType.DMA((count,))
    far, here = pl.BlockSpec(memory_space=pltpu.HBM), pl.BlockSpec(memory_space=pltpu.VMEM)
    stay = lambda v: pltpu.with_memory_space_constraint(v, pltpu.HBM)
    near, y3, y4, z3, z4, tables = [stay(v) for v in (near, y3, y4, z3, z4, tables)]
    flat = stay(density.reshape(planes * rows, cells))
    tiled = f32(TILES, planes * rows, LANES)
    payload = f32(4, 16, cells)
    x, pay_e, pay_o, own, pay = call(
        along_x,
        [tiled, payload, payload, f32(16, cells), f32(ny, 8, cells * 3 // 2)],
        [
            vmem(planes * rows, cells),
            vmem(64, 64),
            vmem(4 * ny, 32),
            vmem(128, cells),
            vmem(64, cells),
            vmem(32, cells),
            sems(6),
        ],
        in_specs=[far, far, far],
    )(y3, y4, flat)
    got_e, got_o = swap(pay_e, "gy", 0), swap(pay_o, "gy", 1)
    got = lax.all_to_all(pay, "gy", 0, 0, tiled=True)
    payload = f32(6, 8, cells)
    one, two, pay_e, pay_o, pay = call(
        along_y,
        [
            tiled,
            f32(TILES, planes * rows // 2, LANES),
            payload,
            payload,
            f32(nz, 8, cells // 2 + LANES),
        ],
        [
            vmem(16, 16),
            vmem(4 * nz, 16),
            vmem(4 * nz, 32),
            vmem(16, cells),
            vmem(4, cells),
            vmem(16, cells),
            vmem(32, cells),
            sems(3),
        ],
        in_specs=[far, far, far] + [here] * 5,
    )(near, z3, z4, x, got_e, got_o, own, got)
    got_e, got_o = swap(pay_e, "gz", 0), swap(pay_o, "gz", 1)
    got = lax.all_to_all(pay, "gz", 0, 0, tiled=True)
    return call(
        along_z,
        f32(planes, rows, cells),
        [
            vmem(planes, rows, cells),
            vmem(64, cells),
            vmem(TILES, 128, LANES),
            vmem(TILES, 16, LANES),
            vmem(3, 16, cells),
            sems(planes + 1),
        ],
        in_specs=[far] + [here] * 5,
        out_specs=far,
    )(tables, one, two, got_e, got_o, got)


def solution(mesh):
    return jax.shard_map(
        per_device, mesh=mesh, in_specs=(P("gz", "gy", None),), out_specs=P("gz", "gy", None), check_vma=False
    )
```

time: 62 us -> 50.4 us (0.81)
  the two profiles are of different devices: /device:TPU:0 before, /device:TPU:8 now
where the time goes in v1:
time: 50.4 us; the launch traced here: 50 us
  starting transfers between devices  19.5 us (39%)
  waiting for transfers between devices  15 us (30%)
  Pallas kernels  12.6 us (25%)
  local copies, waits for them, and re-layouts  2.8 us (6%)
    all_to_all x1, waiting for transfers between devices, per_device(): got = lax.all_to_all(pay, 'gy', 0, 0, tiled=True)  7.74 us
    all_to_all x1, starting transfers between devices, per_device(): got = lax.all_to_all(pay, 'gz', 0, 0, tiled=True)  7.54 us
    ppermute x4, waiting for transfers between devices, swap(): return lax.ppermute(values, axis, pairs)  7.23 us
    ppermute x4, starting transfers between devices, swap(): return lax.ppermute(values, axis, pairs)  6.68 us
    pallas_call x1, Pallas kernels, per_device(): call(along_x, [tiled, payload, payload, f32(16, cells), f32(ny, 8, cells...  6.11 us
    all_to_all x1, starting transfers between devices, per_device(): got = lax.all_to_all(pay, 'gy', 0, 0, tiled=True)  5.31 us
    pallas_call x1, Pallas kernels, per_device(): call(along_z, f32(planes, rows, cells), [vmem(planes, rows, cells), vmem(...  3.68 us
    unnamed x12, local copies, waits for them, and re-layouts  2.8 us
  transfers between devices with their start and end apart: 6, of which 4 were waited for; matrix products, arithmetic and copies ran while one was open for 0% of the time, Pallas kernels for 0%

profile of v1, /device:TPU:8, one launch (start us, length us, event | category | flops | bytes accessed | tf_op | source)
XLA Modules:
  0.0 50.0 jit_solution(4210382776167983648)
XLA Ops:
  0.0 6.1 %shard_map.73 = (f32[8,256,128]{2,1,0:T(8,128)S(1)}, f32[4,16,1024]{2,1,0:T(8,128)S(1)}, f32[4,16,1024]{2,1,0:T(8,128)S(1)}, f32[16,1024]{1,0:T(8,128)S(1)}, f32[8,8,1536]{2,1,0:T(8,128)}) custom-call(f32[8,64,64]{2,1,0:T(8,128)} %constant.13.clone.weights3, f32[8,32,32]{2,1,0:T(8,128)} %constant.14.clone.weights4, f32[256,1024]{1,0:T(8,128)} %bitcast.1), custom_call_target="tpu_custom_call" | custom-call | tf_op jit(solution)/shard_map/pallas_call | solution.py:504
  6.1 0.0 copy-start
  6.1 0.6 %copy-done = f32[16,1024]{1,0:T(8,128)} copy-done((f32[16,1024]{1,0:T(8,128)}, f32[16,1024]{1,0:T(8,128)S(1)}, u32[]{:S(2)}) %copy-start) | copy-done | bytes 65560
  6.7 5.3 %all-to-all-start = ((f32[8,8,1536]{2,1,0:T(8,128)}), f32[8,8,1536]{2,1,0:T(8,128)S(1)}, u32[]{:S(2)}, u32[]{:S(2)}) async-start(f32[8,8,1536]{2,1,0:T(8,128)} %get-tuple-element.19), calls=%async_computation | async-start | bytes 786432 | tf_op jit(solution)/shard_map/all_to_all | solution.py:519
  12.1 0.5 %collective-permute-start = (f32[4,16,1024]{2,1,0:T(8,128)S(1)}, f32[4,16,1024]{2,1,0:T(8,128)S(1)}, u32[]{:S(2)}, u32[]{:S(2)}) collective-permute-start(f32[4,16,1024]{2,1,0:T(8,128)S(1)} %get-tuple-element.16), channel_id=1, source_target_pairs={{0,1},{1,0},{2,3},{3,2},{4,5},{5,4},{6,7},{7,6},{8,9},{9,8},{10,11... | collective-permute-start | bytes 786440 | tf_op jit(solution)/shard_map/ppermute | solution.py:473
  12.6 0.7 %collective-permute-start.1 = (f32[4,16,1024]{2,1,0:T(8,128)S(1)}, f32[4,16,1024]{2,1,0:T(8,128)S(1)}, u32[]{:S(2)}, u32[]{:S(2)}) collective-permute-start(f32[4,16,1024]{2,1,0:T(8,128)S(1)} %get-tuple-element.17), channel_id=1, source_target_pairs={{1,2},{2,1},{3,4},{4,3},{5,6},{6,5},{9,10},{10,9},{11,12},{12,11},... | collective-permute-start | bytes 786440 | tf_op jit(solution)/shard_map/ppermute | solution.py:473
  13.2 0.5 collective-permute-done.got_e
  13.7 0.0 collective-permute-done.1.got_o
  13.7 7.7 %all-to-all-done.got = f32[8,8,1536]{2,1,0:T(8,128)S(1)} async-done(((f32[8,8,1536]{2,1,0:T(8,128)}), f32[8,8,1536]{2,1,0:T(8,128)S(1)}, u32[]{:S(2)}, u32[]{:S(2)}) %all-to-all-start) | async-done | bytes 393248 | tf_op jit(solution)/shard_map/all_to_all | solution.py:519
  21.5 0.0 copy-start.1
  21.5 0.8 %copy-done.1 = f32[16,1024]{1,0:T(8,128)S(1)} copy-done((f32[16,1024]{1,0:T(8,128)S(1)}, f32[16,1024]{1,0:T(8,128)}, u32[]{:S(2)}) %copy-start.1) | copy-done | bytes 65560
  22.3 2.8 %shard_map.74 = (f32[8,256,128]{2,1,0:T(8,128)S(1)}, f32[8,128,128]{2,1,0:T(8,128)S(1)}, f32[6,8,1024]{2,1,0:T(8,128)S(1)}, f32[6,8,1024]{2,1,0:T(8,128)S(1)}, f32[16,8,640]{2,1,0:T(8,128)}) custom-call(f32[16,16]{1,0:T(8,128)} %constant.12.clone.near3, f32[16,64,16]{2,1,0:T(8,128)} %constant.15.clone.weights3, f32[16,64,32]{2,1,0:T(8,128)} %constant.16.clone.weights4, ...), custom_call_target="tpu_custom_call" | custom-call | tf_op jit(solution)/shard_map/pallas_call | solution.py:521
  25.1 0.0 copy-start.2
  25.1 0.7 %copy-done.2 = f32[6,8,1024]{2,1,0:T(8,128)} copy-done((f32[6,8,1024]{2,1,0:T(8,128)}, f32[6,8,1024]{2,1,0:T(8,128)S(1)}, u32[]{:S(2)}) %copy-start.2) | copy-done | bytes 196632
  25.8 0.0 copy-start.4
  25.8 0.7 %copy-done.4 = f32[6,8,1024]{2,1,0:T(8,128)} copy-done((f32[6,8,1024]{2,1,0:T(8,128)}, f32[6,8,1024]{2,1,0:T(8,128)S(1)}, u32[]{:S(2)}) %copy-start.4) | copy-done | bytes 196632
  26.5 0.0 copy-start.5
  26.5 0.0 copy-start.3
  26.5 7.5 %all-to-all-start.1 = ((f32[16,8,640]{2,1,0:T(8,128)}), f32[16,8,640]{2,1,0:T(8,128)S(1)}, u32[]{:S(2)}, u32[]{:S(2)}) async-start(f32[16,8,640]{2,1,0:T(8,128)} %get-tuple-element.24), calls=%async_computation.1 | async-start | bytes 655360 | tf_op jit(solution)/shard_map/all_to_all | solution.py:543
  34.0 0.0 copy-done.5
  34.0 1.5 %collective-permute-start.2 = (f32[6,8,1024]{2,1,0:T(8,128)S(1)}, f32[6,8,1024]{2,1,0:T(8,128)S(1)}, u32[]{:S(2)}, u32[]{:S(2)}) collective-permute-start(f32[6,8,1024]{2,1,0:T(8,128)S(1)} %copy-done.5), channel_id=1, source_target_pairs={{0,8},{8,0},{16,24},{24,16},{32,40},{40,32},{48,56},{56,48},{64,72... | collective-permute-start | bytes 589832 | tf_op jit(solution)/shard_map/ppermute | solution.py:473
  35.6 0.0 copy-done.3
  35.6 4.0 %collective-permute-start.3 = (f32[6,8,1024]{2,1,0:T(8,128)S(1)}, f32[6,8,1024]{2,1,0:T(8,128)S(1)}, u32[]{:S(2)}, u32[]{:S(2)}) collective-permute-start(f32[6,8,1024]{2,1,0:T(8,128)S(1)} %copy-done.3), channel_id=1, source_target_pairs={{8,16},{16,8},{24,32},{32,24},{40,48},{48,40},{56,64},{64,56},{72,... | collective-permute-start | bytes 589832 | tf_op jit(solution)/shard_map/ppermute | solution.py:473
  39.5 4.8 %collective-permute-done.2.got_e = f32[6,8,1024]{2,1,0:T(8,128)S(1)} collective-permute-done((f32[6,8,1024]{2,1,0:T(8,128)S(1)}, f32[6,8,1024]{2,1,0:T(8,128)S(1)}, u32[]{:S(2)}, u32[]{:S(2)}) %collective-permute-start.2) | collective-permute-done | bytes 196640 | tf_op jit(solution)/shard_map/ppermute | solution.py:473
  44.3 1.9 %collective-permute-done.3.got_o = f32[6,8,1024]{2,1,0:T(8,128)S(1)} collective-permute-done((f32[6,8,1024]{2,1,0:T(8,128)S(1)}, f32[6,8,1024]{2,1,0:T(8,128)S(1)}, u32[]{:S(2)}, u32[]{:S(2)}) %collective-permute-start.3) | collective-permute-done | bytes 196640 | tf_op jit(solution)/shard_map/ppermute | solution.py:473
  46.3 0.0 all-to-all-done.1.got
  46.3 3.7 %shard_map.75 = f32[16,16,1024]{2,1,0:T(8,128)} custom-call(f32[3,16,1024]{2,1,0:T(8,128)} %constant.17.clone.tables, f32[8,256,128]{2,1,0:T(8,128)S(1)} %get-tuple-element.20.one, f32[8,128,128]{2,1,0:T(8,128)S(1)} %get-tuple-element.21.two, f32[6,8,1024]{2,1,0:T(8,128)S(1)} %collective-permute-done.2.got_e, ...), custom_call_target="tpu_custom_call" | custom-call | tf_op jit(solution)/shard_map/pallas_call | solution.py:544
Async XLA Ops:
  6.1 0.6 %copy-start = (f32[16,1024]{1,0:T(8,128)}, f32[16,1024]{1,0:T(8,128)S(1)}, u32[]{:S(2)}) copy-start(f32[16,1024]{1,0:T(8,128)S(1)} %get-tuple-element.18.own) | copy-start | bytes 196612
  6.7 14.7 %all-to-all-start = ((f32[8,8,1536]{2,1,0:T(8,128)}), f32[8,8,1536]{2,1,0:T(8,128)S(1)}, u32[]{:S(2)}, u32[]{:S(2)}) async-start(f32[8,8,1536]{2,1,0:T(8,128)} %get-tuple-element.19), calls=%async_computation | async-start | bytes 786432 | tf_op jit(solution)/shard_map/all_to_all | solution.py:519
  12.1 1.7 %collective-permute-start = (f32[4,16,1024]{2,1,0:T(8,128)S(1)}, f32[4,16,1024]{2,1,0:T(8,128)S(1)}, u32[]{:S(2)}, u32[]{:S(2)}) collective-permute-start(f32[4,16,1024]{2,1,0:T(8,128)S(1)} %get-tuple-element.16), channel_id=1, source_target_pairs={{0,1},{1,0},{2,3},{3,2},{4,5},{5,4},{6,7},{7,6},{8,9},{9,8},{10,11... | collective-permute-start | bytes 786440 | tf_op jit(solution)/shard_map/ppermute | solution.py:473
  12.6 1.2 %collective-permute-start.1 = (f32[4,16,1024]{2,1,0:T(8,128)S(1)}, f32[4,16,1024]{2,1,0:T(8,128)S(1)}, u32[]{:S(2)}, u32[]{:S(2)}) collective-permute-start(f32[4,16,1024]{2,1,0:T(8,128)S(1)} %get-tuple-element.17), channel_id=1, source_target_pairs={{1,2},{2,1},{3,4},{4,3},{5,6},{6,5},{9,10},{10,9},{11,12},{12,11},... | collective-permute-start | bytes 786440 | tf_op jit(solution)/shard_map/ppermute | solution.py:473
  21.5 0.8 %copy-start.1 = (f32[16,1024]{1,0:T(8,128)S(1)}, f32[16,1024]{1,0:T(8,128)}, u32[]{:S(2)}) copy-start(f32[16,1024]{1,0:T(8,128)} %copy-done) | copy-start | bytes 196612
  25.1 0.7 %copy-start.2 = (f32[6,8,1024]{2,1,0:T(8,128)}, f32[6,8,1024]{2,1,0:T(8,128)S(1)}, u32[]{:S(2)}) copy-start(f32[6,8,1024]{2,1,0:T(8,128)S(1)} %get-tuple-element.23) | copy-start | bytes 589828
  25.8 0.7 %copy-start.4 = (f32[6,8,1024]{2,1,0:T(8,128)}, f32[6,8,1024]{2,1,0:T(8,128)S(1)}, u32[]{:S(2)}) copy-start(f32[6,8,1024]{2,1,0:T(8,128)S(1)} %get-tuple-element.22) | copy-start | bytes 589828
  26.5 7.5 %copy-start.5 = (f32[6,8,1024]{2,1,0:T(8,128)S(1)}, f32[6,8,1024]{2,1,0:T(8,128)}, u32[]{:S(2)}) copy-start(f32[6,8,1024]{2,1,0:T(8,128)} %copy-done.4) | copy-start | bytes 589828
  26.5 9.1 %copy-start.3 = (f32[6,8,1024]{2,1,0:T(8,128)S(1)}, f32[6,8,1024]{2,1,0:T(8,128)}, u32[]{:S(2)}) copy-start(f32[6,8,1024]{2,1,0:T(8,128)} %copy-done.2) | copy-start | bytes 589828
  26.5 19.8 %all-to-all-start.1 = ((f32[16,8,640]{2,1,0:T(8,128)}), f32[16,8,640]{2,1,0:T(8,128)S(1)}, u32[]{:S(2)}, u32[]{:S(2)}) async-start(f32[16,8,640]{2,1,0:T(8,128)} %get-tuple-element.24), calls=%async_computation.1 | async-start | bytes 655360 | tf_op jit(solution)/shard_map/all_to_all | solution.py:543
  34.0 10.3 %collective-permute-start.2 = (f32[6,8,1024]{2,1,0:T(8,128)S(1)}, f32[6,8,1024]{2,1,0:T(8,128)S(1)}, u32[]{:S(2)}, u32[]{:S(2)}) collective-permute-start(f32[6,8,1024]{2,1,0:T(8,128)S(1)} %copy-done.5), channel_id=1, source_target_pairs={{0,8},{8,0},{16,24},{24,16},{32,40},{40,32},{48,56},{56,48},{64,72... | collective-permute-start | bytes 589832 | tf_op jit(solution)/shard_map/ppermute | solution.py:473
  35.6 10.7 %collective-permute-start.3 = (f32[6,8,1024]{2,1,0:T(8,128)S(1)}, f32[6,8,1024]{2,1,0:T(8,128)S(1)}, u32[]{:S(2)}, u32[]{:S(2)}) collective-permute-start(f32[6,8,1024]{2,1,0:T(8,128)S(1)} %copy-done.3), channel_id=1, source_target_pairs={{8,16},{16,8},{24,32},{32,24},{40,48},{48,40},{56,64},{64,56},{72,... | collective-permute-start | bytes 589832 | tf_op jit(solution)/shard_map/ppermute | solution.py:473

commit v2 on v1

--- a/solution.py
+++ b/solution.py
@@ -109,15 +109,16 @@
     return w, pltpu.roll(w, LANES - 1, 1)
 
 
-def gather_tiles(ref, at):
-    return jnp.concatenate([ref[t, at, :] for t in range(TILES)], axis=1)
-
-
 def tile(t):
     return slice(t * LANES, (t + 1) * LANES)
 
 
 def times(count, body, unroll=1):
+    if unroll == count:
+        for i in range(count):
+            body(i)
+        return
+
     def step(i, carry):
         body(i)
         return carry
@@ -126,7 +127,7 @@
 
 
 def tile_lanes(t):
-    return pl.ds(pl.multiple_of(t * LANES, LANES), LANES)
+    return pl.ds(t * LANES if isinstance(t, int) else pl.multiple_of(t * LANES, LANES), LANES)
 
 
 def lift_two(a, b, phase):
@@ -168,15 +169,12 @@
         ref[at, tile(t)] = v
 
 
-def along_x(weights3, weights4, density, out, pay_e, pay_o, own, pay, x, w3, w4, e1, e2, e3, sem):
-    me = lax.axis_index("gy")
+def along_x(density, out, pay_e, pay_o, e1, x, sem):
     part = x.shape[0] // 4
     loads = [
         pltpu.make_async_copy(density.at[pl.ds(k * part, part)], x.at[pl.ds(k * part, part)], sem.at[k])
         for k in (0, 2, 1, 3)
     ]
-    loads.append(pltpu.make_async_copy(weights3.at[me], w3, sem.at[4]))
-    loads.append(pltpu.make_async_copy(weights4.at[me], w4, sem.at[5]))
     for load in loads:
         load.start()
 
@@ -197,33 +195,8 @@
     loads[2].wait()
     loads[3].wait()
     times(8, lambda i: plane(i + 8), 4)
-
-    def second(i):
-        at = pl.multiple_of(i * 8, 8)
-        s, _ = lift_two(tiles_of(e1, pl.ds(at, 8)), tiles_of(e1, pl.ds(at + 64, 8)), 2)
-        put_tiles(e2, pl.ds(at, 8), s)
-
-    times(8, second, 4)
-
-    def third(i):
-        at = pl.multiple_of(i * 8, 8)
-        s, _ = lift_two(tiles_of(e2, pl.ds(at, 8)), tiles_of(e2, pl.ds(at + 32, 8)), 4)
-        put_tiles(e3, pl.ds(at, 8), s)
-
-    times(4, third, 4)
-    loads[4].wait()
-    loads[5].wait()
-    flip = me % 2 == 1
+    flip = lax.axis_index("gy") % 2 == 1
     even = lane_id((8, LANES)) % 2 == 0
-    three = jnp.dot(w3[...], e2[...], precision=HIGH, preferred_element_type=jnp.float32)
-    own[...] = three[0:16]
-    pay_e[3] = mix(flip, three[32:48], three[16:32])
-    pay_o[3] = mix(flip, three[16:32], three[32:48])
-    four = jnp.dot(w4[...], e3[...], precision=HIGH, preferred_element_type=jnp.float32)
-    for to in range(pay.shape[0]):
-        pay[to, :, 0:WIDE] = mix(to > me, three[48:56], three[56:64])
-        pay[to, 0:4, WIDE:] = four[to * 4 : to * 4 + 4, : WIDE // 2]
-        pay[to, 4:8, WIDE:] = four[to * 4 : to * 4 + 4, WIDE // 2 :]
 
     def column(t):
         lanes = tile_lanes(t)
@@ -240,15 +213,42 @@
     times(TILES, column, 2)
 
 
-def along_y(near3, weights3, weights4, x, got_e, got_o, own, got, one, two, pay_e, pay_o, pay, n3, w3, w4, held3, held4, turned3, turned4, sem):
-    mz = lax.axis_index("gz")
+def thin_y(weights3, weights4, e1, own, pay, w3, w4, e2, e3, sem):
+    me = lax.axis_index("gy")
     loads = [
-        pltpu.make_async_copy(near3, n3, sem.at[0]),
-        pltpu.make_async_copy(weights3.at[mz], w3, sem.at[1]),
-        pltpu.make_async_copy(weights4.at[mz], w4, sem.at[2]),
+        pltpu.make_async_copy(weights3.at[me], w3, sem.at[0]),
+        pltpu.make_async_copy(weights4.at[me], w4, sem.at[1]),
     ]
     for load in loads:
         load.start()
+
+    def second(i):
+        at = pl.multiple_of(i * 8, 8)
+        s, _ = lift_two(tiles_of(e1, pl.ds(at, 8)), tiles_of(e1, pl.ds(at + 64, 8)), 2)
+        put_tiles(e2, pl.ds(at, 8), s)
+
+    times(8, second, 4)
+
+    def third(i):
+        at = pl.multiple_of(i * 8, 8)
+        s, _ = lift_two(tiles_of(e2, pl.ds(at, 8)), tiles_of(e2, pl.ds(at + 32, 8)), 4)
+        put_tiles(e3, pl.ds(at, 8), s)
+
+    times(4, third, 4)
+    for load in loads:
+        load.wait()
+    three = jnp.dot(w3[...], e2[...], precision=HIGH, preferred_element_type=jnp.float32)
+    own[...] = three[0:16]
+    four = jnp.dot(w4[...], e3[...], precision=HIGH, preferred_element_type=jnp.float32)
+    for to in range(pay.shape[0]):
+        right = mix(to == me + 1, three[16:24], three[24:32])
+        left = mix(to == me - 1, three[32:40], three[40:48])
+        pay[to, :, 0:WIDE] = mix(to > me, right, left)
+        pay[to, 0:4, WIDE:] = four[to * 4 : to * 4 + 4, : WIDE // 2]
+        pay[to, 4:8, WIDE:] = four[to * 4 : to * 4 + 4, WIDE // 2 :]
+
+
+def along_y(x, got_e, got_o, one, two, pay_e, pay_o):
     me = lax.axis_index("gy")
     first, last, flip = me == 0, me == lax.axis_size("gy") - 1, me % 2 == 1
     even = lane_id((8, LANES)) % 2 == 0
@@ -272,47 +272,6 @@
                 two[t, pl.ds(half * 64 + y, 8, stride=8), :] = v
 
     times(TILES, column, TILES)
-    for load in loads:
-        load.wait()
-    far = jnp.concatenate(
-        [
-            mix(me >= 2, got[jnp.maximum(me - 2, 0), :, 0:WIDE], 0.0),
-            mix(me + 2 < got.shape[0], got[jnp.minimum(me + 2, got.shape[0] - 1), :, 0:WIDE], 0.0),
-        ],
-        axis=0,
-    )
-    held3[...] = (own[...] + (got_e[3] + got_o[3])) + jnp.dot(
-        n3[...], far, precision=HIGH, preferred_element_type=jnp.float32
-    )
-    four = got[0, :, WIDE:]
-    for k in range(1, got.shape[0]):
-        four = four + got[k, :, WIDE:]
-    held4[:, 0 : WIDE // 2] = four[0:4]
-    held4[:, WIDE // 2 :] = four[4:8]
-    lane = lane_id((4, LANES))
-    for t in range(TILES):
-        rows = [held3[pl.ds(4 * r, 4), tile(t)] for r in range(4)]
-        for f in range(4):
-            v = None
-            for r in range(4):
-                moved = pltpu.roll(rows[r], (r - f) % LANES, 1) if r != f else rows[r]
-                v = jnp.where(lane % 4 == r, moved, v) if r else moved
-            turned3[pl.ds(4 * f, 4), tile(t)] = v
-        v = held4[:, tile(t)]
-        for f in range(8):
-            turned4[pl.ds(4 * f, 4), tile(t)] = pltpu.roll(v, LANES - f, 1) if f else v
-    three = jnp.dot(w3[...], turned3[...], precision=HIGH, preferred_element_type=jnp.float32)
-    four = jnp.dot(w4[...], turned4[...], precision=HIGH, preferred_element_type=jnp.float32)
-    count = pay.shape[0]
-    lane = lane_id((count, LANES))
-    for t in range(TILES):
-        v = four[0:count, tile(t)]
-        for k in range(1, 4):
-            v = jnp.where(lane % 8 == k, pltpu.roll(four[k * count : (k + 1) * count, tile(t)], k, 1), v)
-        pay[:, t, WIDE // 2 :] = v
-    for to in range(count):
-        pay[to, 0:4, 0 : WIDE // 2] = three[to * 4 : to * 4 + 4, : WIDE // 2]
-        pay[to, 4:8, 0 : WIDE // 2] = three[to * 4 : to * 4 + 4, WIDE // 2 :]
     flip = lax.axis_index("gz") % 2 == 1
 
     def stack(t):
@@ -336,8 +295,67 @@
     times(TILES, stack, TILES)
 
 
-def along_z(tables, one, two, got_e, got_o, got, result, out, fine, spread, coarse, table, sem):
-    load = pltpu.make_async_copy(tables, table, sem.at[16])
+def thin_z(weights3, weights4, two, own, got, pay, w3, w4, thick, cells, beyond, held4, turned3, turned4, sem):
+    mz = lax.axis_index("gz")
+    loads = [
+        pltpu.make_async_copy(weights3.at[mz], w3, sem.at[0]),
+        pltpu.make_async_copy(weights4.at[mz], w4, sem.at[1]),
+    ]
+    for load in loads:
+        load.start()
+    me, count = lax.axis_index("gy"), got.shape[0]
+    first, last = me == 0, me == count - 1
+    even = lane_id((8, LANES)) % 2 == 0
+    for t in range(TILES):
+        for r in range(4):
+            low, high = [two[t, pl.ds(64 * half + 2 * r, 8, stride=8), :] for half in range(2)]
+            v = pack_two(low, high, even)
+            thick[pl.ds(4 * r, 4), tile(t)] = v[0:4]
+            thick[pl.ds(16 + 4 * r, 4), tile(t)] = v[4:8]
+    for i in range(2):
+        s, _ = lift_two(tiles_of(thick, pl.ds(8 * i, 8)), tiles_of(thick, pl.ds(16 + 8 * i, 8)), 2)
+        put_tiles(cells, pl.ds(8 * i, 8), s)
+    near = lambda k: got[jnp.clip(me + k, 0, count - 1), :, 0:WIDE]
+    beyond[0:8] = own[0:8] + (mix(me >= 1, near(-1), 0.0) + mix(me >= 2, near(-2), 0.0))
+    beyond[8:16] = own[8:16] + (mix(me < count - 1, near(1), 0.0) + mix(me < count - 2, near(2), 0.0))
+    four = got[0, :, WIDE:]
+    for k in range(1, count):
+        four = four + got[k, :, WIDE:]
+    held4[:, 0 : WIDE // 2] = four[0:4]
+    held4[:, WIDE // 2 :] = four[4:8]
+    lane = lane_id((4, LANES))
+    for t in range(TILES):
+        at = lambda r: pl.ds(4 * r, 4)
+        p, q, s, r = [beyond[at(c), tile(t)] for c in range(4)]
+        rows = [cells[at(c), tile(t)] for c in range(4)]
+        rows = interleave(*lift(rows, (p, q), (s, r), first, last, mix))
+        for f in range(4):
+            v = None
+            for r in range(4):
+                moved = pltpu.roll(rows[r], (r - f) % LANES, 1) if r != f else rows[r]
+                v = jnp.where(lane % 4 == r, moved, v) if r else moved
+            turned3[at(f), tile(t)] = v
+        v = held4[:, tile(t)]
+        for f in range(8):
+            turned4[at(f), tile(t)] = pltpu.roll(v, LANES - f, 1) if f else v
+    for load in loads:
+        load.wait()
+    three = jnp.dot(w3[...], turned3[...], precision=HIGH, preferred_element_type=jnp.float32)
+    four = jnp.dot(w4[...], turned4[...], precision=HIGH, preferred_element_type=jnp.float32)
+    count = pay.shape[0]
+    lane = lane_id((count, LANES))
+    for t in range(TILES):
+        v = four[0:count, tile(t)]
+        for k in range(1, 4):
+            v = jnp.where(lane % 8 == k, pltpu.roll(four[k * count : (k + 1) * count, tile(t)], k, 1), v)
+        pay[:, t, WIDE // 2 :] = v
+    for to in range(count):
+        pay[to, 0:4, 0 : WIDE // 2] = three[to * 4 : to * 4 + 4, : WIDE // 2]
+        pay[to, 4:8, 0 : WIDE // 2] = three[to * 4 : to * 4 + 4, WIDE // 2 :]
+
+
+def along_z(tables, one, two, got_e, got_o, result, fourth, out, fine, spread, table, sem):
+    load = pltpu.make_async_copy(tables.at[0], table, sem.at[16])
     load.start()
     me = lax.axis_index("gz")
     first, last, flip = me == 0, me == lax.axis_size("gz") - 1, me % 2 == 1
@@ -363,14 +381,35 @@
             fine[pl.ds(z * 8, 8), lanes] = v
 
     times(TILES, stack, TILES)
-    sends = [pltpu.make_async_copy(out.at[z], result.at[z], sem.at[z]) for z in range(16)]
+    sends = {z: pltpu.make_async_copy(out.at[z], result.at[z], sem.at[z]) for z in range(16) if z % 4}
     for z in range(1, 16, 2):
         sends[z].start()
+    load.wait()
+    row = lax.broadcasted_iota(jnp.int32, (16, LANES), 0)
+    here = (row % 2 == 0) & (lane_id((16, LANES)) % 2 == 0)
+    for z in (1, 3, 5, 7, 0, 2, 4, 6):
+        v = lift_lanes(fine[pl.ds(z * 8, 8), :], table, 2)
+        for t in range(TILES):
+            spread[t, pl.ds(z * 16, 8, stride=2), :] = v[:, tile(t)]
+            w = jnp.where(here, spread[t, pl.ds(z * 16, 16), :], out[2 * z, :, tile(t)])
+            if z % 2:
+                out[2 * z, :, tile(t)] = w
+            else:
+                fourth[z // 2, :, tile(t)] = w
+        if z % 2:
+            sends[2 * z].start()
+    for send in sends.values():
+        send.wait()
+
+
+def join(tables, got, fourth, base, result, planes, spread, coarse, table, sem):
+    load = pltpu.make_async_copy(tables, table, sem.at[4])
+    load.start()
     half = WIDE // 2
-    load.wait()
     total = got[0]
     for k in range(1, got.shape[0]):
         total = total + got[k]
+    load.wait()
     three = jnp.concatenate([total[0:4, :half], total[4:8, :half]], axis=1)
     three = lift_lanes(three, table.at[1], 4)
     four = jnp.concatenate([total[t : t + 1, half:] for t in range(TILES)], axis=1)
@@ -386,19 +425,13 @@
             moved = pltpu.roll(v, LANES - k, 1) if k else v
             coarse[t, at, :] = jnp.where(here, moved, coarse[t, at, :])
     row = lax.broadcasted_iota(jnp.int32, (16, LANES), 0)
-    lane = lane_id((16, LANES))
-    at_two = (row % 2 == 0) & (lane % 2 == 0)
-    at_three = (row % 4 == 0) & (lane % 4 == 0)
-    for z in range(8):
-        v = lift_lanes(fine[pl.ds(z * 8, 8), :], table.at[0], 2)
+    here = (row % 4 == 0) & (lane_id((16, LANES)) % 4 == 0)
+    sends = [pltpu.make_async_copy(planes.at[i], result.at[4 * i], sem.at[i]) for i in range(4)]
+    for i in range(4):
         for t in range(TILES):
-            spread[t, pl.ds(z * 16, 8, stride=2), :] = v[:, tile(t)]
-            w = jnp.where(at_two, spread[t, pl.ds(z * 16, 16), :], out[2 * z, :, tile(t)])
-            if z % 2 == 0:
-                spread[t, pl.ds(z * 16, 4, stride=4), :] = coarse[t, pl.ds(z * 2, 4), :]
-                w = jnp.where(at_three, spread[t, pl.ds(z * 16, 16), :], w)
-            out[2 * z, :, tile(t)] = w
-        sends[2 * z].start()
+            spread[t, pl.ds(i * 16, 4, stride=4), :] = coarse[t, pl.ds(i * 4, 4), :]
+            planes[i, :, tile(t)] = jnp.where(here, spread[t, pl.ds(i * 16, 16), :], fourth[i, :, tile(t)])
+        sends[i].start()
     for send in sends:
         send.wait()
 
@@ -412,35 +445,21 @@
 
 
 def weights_y(devices):
-    cells, three, four = deep_levels(16 * devices)
-    w3 = np.zeros((devices, 64, 4, 16), np.float64)
+    cells, _, four = deep_levels(16 * devices)
+    w3 = np.zeros((devices, 48, 4, 16), np.float64)
     w4 = np.zeros((devices, devices, 2, 2, 2, 16), np.float64)
     for a in range(devices):
         mine = slice(16 * a, 16 * a + 16)
-        for k, b in enumerate((a, a + 1, a - 1)):
-            for r in range(4):
-                for z in range(4):
-                    if 0 <= b < devices:
-                        w3[a, 16 * k + 4 * r + z, z] = three[4 * b + r, mine]
-        for z in range(4):
-            for c in range(2):
-                if a + 2 < devices:
-                    w3[a, 48 + 4 * c + z, z] = edges(cells[4 * a + 4 : 4 * a + 8])[0][c][mine]
-                if a - 2 >= 0:
-                    w3[a, 56 + 4 * c + z, z] = edges(cells[4 * a - 4 : 4 * a])[1][c][mine]
+        for row, side, b in ((0, 0, -1), (8, 1, 1), (16, 0, 0), (24, 0, 1), (32, 1, 0), (40, 1, -1)):
+            if 0 <= a + b < devices:
+                pair = edges(cells[4 * (a + b) : 4 * (a + b) + 4])[side]
+                for c in range(2):
+                    for z in range(4):
+                        w3[a, row + 4 * c + z, z] = pair[c][mine]
         for z in range(2):
             w4[a, :, :, z, z] = four[:, mine].reshape(devices, 2, 16)
-    near = np.zeros((4, 4, 4, 4), np.float64)
-    fixed = lambda c, x, y: y
-    for c in range(4):
-        unit = [1.0 if c == k else 0.0 for k in range(4)]
-        rows = interleave(*lift([0.0] * 4, unit[:2], unit[2:], False, False, fixed))
-        for r in range(4):
-            for z in range(4):
-                near[r, z, c, z] = rows[r]
     return (
-        near.reshape(16, 16).astype(np.float32),
-        w3.reshape(devices, 64, 64).astype(np.float32),
+        w3.reshape(devices, 48, 64).astype(np.float32),
         w4.reshape(devices, 4 * devices, 32).astype(np.float32),
     )
 
@@ -477,11 +496,12 @@
     return jax.ShapeDtypeStruct(shape, jnp.float32)
 
 
-def call(body, out, scratch=(), **more):
+def call(body, out, scratch=(), cost=4 << 20, **more):
     return pl.pallas_call(
         body,
         out_shape=out,
         scratch_shapes=list(scratch),
+        cost_estimate=pl.CostEstimate(flops=cost * 10, bytes_accessed=4 << 20, transcendentals=0),
         compiler_params=pltpu.CompilerParams(vmem_limit_bytes=24 * 1024 * 1024),
         **more,
     )
@@ -490,71 +510,70 @@
 def per_device(density):
     planes, rows, cells = density.shape
     ny, nz = lax.axis_size("gy"), lax.axis_size("gz")
-    near, y3, y4 = [jnp.asarray(w) for w in weights_y(ny)]
-    z3, z4 = [jnp.asarray(w) for w in weights_z(nz)]
-    tables = jnp.asarray(np.stack([lane_factors(s) for s in (2, 4, 8)]))
     vmem = lambda *shape: pltpu.VMEM(shape, jnp.float32)
     sems = lambda count: pltpu.SemaphoreType.DMA((count,))
     far, here = pl.BlockSpec(memory_space=pltpu.HBM), pl.BlockSpec(memory_space=pltpu.VMEM)
-    stay = lambda v: pltpu.with_memory_space_constraint(v, pltpu.HBM)
-    near, y3, y4, z3, z4, tables = [stay(v) for v in (near, y3, y4, z3, z4, tables)]
-    flat = stay(density.reshape(planes * rows, cells))
+    stay = lambda v: pltpu.with_memory_space_constraint(jnp.asarray(v), pltpu.HBM)
+    tables = stay(np.stack([lane_factors(s) for s in (2, 4, 8)]))
     tiled = f32(TILES, planes * rows, LANES)
-    payload = f32(4, 16, cells)
-    x, pay_e, pay_o, own, pay = call(
+
+    payload = f32(3, 16, cells)
+    x, pay_e, pay_o, e1 = call(
         along_x,
-        [tiled, payload, payload, f32(16, cells), f32(ny, 8, cells * 3 // 2)],
+        [tiled, payload, payload, f32(planes * rows // 2, cells)],
+        [vmem(planes * rows, cells), sems(4)],
+        in_specs=[far],
+    )(stay(density.reshape(planes * rows, cells)))
+    got_e, got_o = swap(pay_e, "gy", 0), swap(pay_o, "gy", 1)
+    own, pay = call(
+        thin_y,
+        [f32(16, cells), f32(ny, 8, cells * 3 // 2)],
+        [vmem(48, 64), vmem(4 * ny, 32), vmem(64, cells), vmem(32, cells), sems(2)],
+        cost=40 << 20,
+        in_specs=[far, far, here],
+    )(*[stay(w) for w in weights_y(ny)], e1)
+    got = lax.all_to_all(pay, "gy", 0, 0, tiled=True)
+
+    payload = f32(6, 8, cells)
+    one, two, pay_e, pay_o = call(along_y, [tiled, f32(TILES, planes * rows // 2, LANES), payload, payload], cost=400 << 20, input_output_aliases={0: 0})(
+        x, got_e, got_o
+    )
+    got_e, got_o = swap(pay_e, "gz", 0), swap(pay_o, "gz", 1)
+    pay = call(
+        thin_z,
+        f32(nz, 8, cells // 2 + LANES),
         [
-            vmem(planes * rows, cells),
-            vmem(64, 64),
-            vmem(4 * ny, 32),
-            vmem(128, cells),
-            vmem(64, cells),
-            vmem(32, cells),
-            sems(6),
-        ],
-        in_specs=[far, far, far],
-    )(y3, y4, flat)
-    got_e, got_o = swap(pay_e, "gy", 0), swap(pay_o, "gy", 1)
-    got = lax.all_to_all(pay, "gy", 0, 0, tiled=True)
-    payload = f32(6, 8, cells)
-    one, two, pay_e, pay_o, pay = call(
-        along_y,
-        [
-            tiled,
-            f32(TILES, planes * rows // 2, LANES),
-            payload,
-            payload,
-            f32(nz, 8, cells // 2 + LANES),
-        ],
-        [
-            vmem(16, 16),
             vmem(4 * nz, 16),
             vmem(4 * nz, 32),
+            vmem(32, cells),
+            vmem(16, cells),
             vmem(16, cells),
             vmem(4, cells),
             vmem(16, cells),
             vmem(32, cells),
-            sems(3),
+            sems(2),
         ],
-        in_specs=[far, far, far] + [here] * 5,
-    )(near, z3, z4, x, got_e, got_o, own, got)
-    got_e, got_o = swap(pay_e, "gz", 0), swap(pay_o, "gz", 1)
+        cost=40 << 20,
+        in_specs=[far, far, here, here, here],
+    )(*[stay(w) for w in weights_z(nz)], two, own, got)
     got = lax.all_to_all(pay, "gz", 0, 0, tiled=True)
+
+    base, fourth = call(
+        along_z,
+        [f32(planes, rows, cells), f32(planes // 4, rows, cells)],
+        [vmem(planes, rows, cells), vmem(64, cells), vmem(TILES, 128, LANES), vmem(16, cells), sems(planes + 1)],
+        cost=400 << 20,
+        in_specs=[far] + [here] * 4,
+        out_specs=[far, here],
+    )(tables, one, two, got_e, got_o)
     return call(
-        along_z,
+        join,
         f32(planes, rows, cells),
-        [
-            vmem(planes, rows, cells),
-            vmem(64, cells),
-            vmem(TILES, 128, LANES),
-            vmem(TILES, 16, LANES),
-            vmem(3, 16, cells),
-            sems(planes + 1),
-        ],
-        in_specs=[far] + [here] * 5,
+        [vmem(planes // 4, rows, cells), vmem(TILES, 64, LANES), vmem(TILES, 16, LANES), vmem(3, 16, cells), sems(5)],
+        in_specs=[far, here, here, far],
         out_specs=far,
-    )(tables, one, two, got_e, got_o, got)
+        input_output_aliases={3: 0},
+    )(tables, got, fourth, stay(base))
 
 
 def solution(mesh):

time: 50.4 us -> 45.4 us (0.901)
  the two profiles are of different devices: /device:TPU:8 before, /device:TPU:0 now
where the time goes in v2:
time: 45.4 us; the launch traced here: 45 us
  starting transfers between devices  17.9 us (39%)
  Pallas kernels  15.5 us (34%)
  waiting for transfers between devices  11.5 us (25%)
    all_to_all x1, starting transfers between devices, per_device(): got = lax.all_to_all(pay, 'gy', 0, 0, tiled=True)  7.83 us
    all_to_all x1, starting transfers between devices, per_device(): got = lax.all_to_all(pay, 'gz', 0, 0, tiled=True)  7.05 us
    all_to_all x1, waiting for transfers between devices, per_device(): got = lax.all_to_all(pay, 'gz', 0, 0, tiled=True)  6.19 us
    all_to_all x1, waiting for transfers between devices, per_device(): got = lax.all_to_all(pay, 'gy', 0, 0, tiled=True)  5.32 us
    pallas_call x1, Pallas kernels, per_device(): call(along_x, [tiled, payload, payload, f32(planes * rows // 2, cells)],...  3.79 us
    ppermute x4, starting transfers between devices, swap(): return lax.ppermute(values, axis, pairs)  3 us
    pallas_call x1, Pallas kernels, per_device(): call(along_z, [f32(planes, rows, cells), f32(planes // 4, rows, cells)],...  2.97 us
    pallas_call x1, Pallas kernels, per_device(): call(thin_z, f32(nz, 8, cells // 2 + LANES), [vmem(4 * nz, 16), vmem(4 *...  2.76 us
  transfers between devices with their start and end apart: 6, of which 2 were waited for; matrix products, arithmetic and copies ran while one was open for 0% of the time, Pallas kernels for 21%

profile of v2, /device:TPU:0, one launch (start us, length us, event | category | flops | bytes accessed | tf_op | source)
XLA Modules:
  0.0 45.0 jit_solution(18200470434842665739)
XLA Ops:
  0.0 3.8 %shard_map.64 = (f32[8,256,128]{2,1,0:T(8,128)S(1)}, f32[3,16,1024]{2,1,0:T(8,128)S(1)}, f32[3,16,1024]{2,1,0:T(8,128)S(1)}, f32[128,1024]{1,0:T(8,128)S(1)}) custom-call(f32[256,1024]{1,0:T(8,128)} %bitcast.1), custom_call_target="tpu_custom_call" | custom-call | flops 41943040 | bytes 4194304 | tf_op jit(solution)/shard_map/pallas_call | solution.py:521
  3.8 0.1 collective-permute-start
  3.9 0.7 %collective-permute-start.1 = (f32[3,16,1024]{2,1,0:T(8,128)S(1)}, f32[3,16,1024]{2,1,0:T(8,128)S(1)}, u32[]{:S(2)}, u32[]{:S(2)}) collective-permute-start(f32[3,16,1024]{2,1,0:T(8,128)S(1)} %get-tuple-element.19), channel_id=1, source_target_pairs={{1,2},{2,1},{3,4},{4,3},{5,6},{6,5},{9,10},{10,9},{11,12},{12,11},... | collective-permute-start | bytes 589832 | tf_op jit(solution)/shard_map/ppermute | solution.py:492
  4.6 2.4 %shard_map.66 = (f32[16,1024]{1,0:T(8,128)S(1)}, f32[8,8,1536]{2,1,0:T(8,128)}) custom-call(f32[8,48,64]{2,1,0:T(8,128)} %constant.11.clone.weights3, f32[8,32,32]{2,1,0:T(8,128)} %constant.12.clone.weights4, f32[128,1024]{1,0:T(8,128)S(1)} %get-tuple-element.21.e1), custom_call_target="tpu_custom_call" | custom-call | flops 419430400 | bytes 4194304 | tf_op jit(solution)/shard_map/pallas_call | solution.py:528
  7.0 7.8 %all-to-all-start = ((f32[8,8,1536]{2,1,0:T(8,128)}), f32[8,8,1536]{2,1,0:T(8,128)S(1)}, u32[]{:S(2)}, u32[]{:S(2)}) async-start(f32[8,8,1536]{2,1,0:T(8,128)} %get-tuple-element.23), calls=%async_computation | async-start | bytes 786432 | tf_op jit(solution)/shard_map/all_to_all | solution.py:535
  14.9 0.0 collective-permute-done.got_e
  14.9 0.0 collective-permute-done.1.got_o
  14.9 1.4 %shard_map.65 = (f32[8,256,128]{2,1,0:T(8,128)S(1)}, f32[8,128,128]{2,1,0:T(8,128)S(1)}, f32[6,8,1024]{2,1,0:T(8,128)S(1)}, f32[6,8,1024]{2,1,0:T(8,128)S(1)}) custom-call(f32[8,256,128]{2,1,0:T(8,128)S(1)} %get-tuple-element.17.x, f32[3,16,1024]{2,1,0:T(8,128)S(1)} %collective-permute-done.got_e, ...), custom_call_target="tpu_custom_call", output_to_operand_aliasing={{0}: (0, {})} | custom-call | flops 4194304000 | bytes 4194304 | tf_op jit(solution)/shard_map/pallas_call | solution.py:538
  16.2 1.6 %collective-permute-start.2 = (f32[6,8,1024]{2,1,0:T(8,128)S(1)}, f32[6,8,1024]{2,1,0:T(8,128)S(1)}, u32[]{:S(2)}, u32[]{:S(2)}) collective-permute-start(f32[6,8,1024]{2,1,0:T(8,128)S(1)} %get-tuple-element.25), channel_id=1, source_target_pairs={{0,8},{8,0},{16,24},{24,16},{32,40},{40,32},{48,56},{56,48},{64,72... | collective-permute-start | bytes 589832 | tf_op jit(solution)/shard_map/ppermute | solution.py:492
  17.8 0.7 %collective-permute-start.3 = (f32[6,8,1024]{2,1,0:T(8,128)S(1)}, f32[6,8,1024]{2,1,0:T(8,128)S(1)}, u32[]{:S(2)}, u32[]{:S(2)}) collective-permute-start(f32[6,8,1024]{2,1,0:T(8,128)S(1)} %get-tuple-element.26), channel_id=1, source_target_pairs={{8,16},{16,8},{24,32},{32,24},{40,48},{48,40},{56,64},{64,56},{72,... | collective-permute-start | bytes 589832 | tf_op jit(solution)/shard_map/ppermute | solution.py:492
  18.5 5.3 %all-to-all-done.got = f32[8,8,1536]{2,1,0:T(8,128)S(1)} async-done(((f32[8,8,1536]{2,1,0:T(8,128)}), f32[8,8,1536]{2,1,0:T(8,128)S(1)}, u32[]{:S(2)}, u32[]{:S(2)}) %all-to-all-start) | async-done | bytes 393248 | tf_op jit(solution)/shard_map/all_to_all | solution.py:535
  23.8 2.8 %shard_map.67 = f32[16,8,640]{2,1,0:T(8,128)} custom-call(f32[16,64,16]{2,1,0:T(8,128)} %constant.13.clone.weights3, f32[16,64,32]{2,1,0:T(8,128)} %constant.14.clone.weights4, f32[8,128,128]{2,1,0:T(8,128)S(1)} %get-tuple-element.20.two, f32[16,1024]{1,0:T(8,128)S(1)} %get-tuple-element.22.own, f32[8,8,1536]{2,1,0:T(8,128)S(1)} %all-to-all-done.got), custom_call_target="tpu_custom_call" | custom-call | flops 419430400 | bytes 4194304 | tf_op jit(solution)/shard_map/pallas_call | solution.py:542
  26.6 7.1 %all-to-all-start.1 = ((f32[16,8,640]{2,1,0:T(8,128)}), f32[16,8,640]{2,1,0:T(8,128)S(1)}, u32[]{:S(2)}, u32[]{:S(2)}) async-start(f32[16,8,640]{2,1,0:T(8,128)} %shard_map.67), calls=%async_computation.1 | async-start | bytes 655360 | tf_op jit(solution)/shard_map/all_to_all | solution.py:559
  33.6 0.0 collective-permute-done.2.got_e
  33.6 0.0 collective-permute-done.3.got_o
  33.7 3.0 %shard_map.68 = (f32[16,16,1024]{2,1,0:T(8,128)}, f32[4,16,1024]{2,1,0:T(8,128)S(1)}) custom-call(f32[3,16,1024]{2,1,0:T(8,128)} %constant.10.clone.tables, f32[8,256,128]{2,1,0:T(8,128)S(1)} %get-tuple-element.24.one, f32[8,128,128]{2,1,0:T(8,128)S(1)} %get-tuple-element.20.two, f32[6,8,1024]{2,1,0:T(8,128)S(1)} %collective-permute-done.2.got_e, ...), custom_call_target="tpu_custom_call" | custom-call | flops 4194304000 | bytes 4194304 | tf_op jit(solution)/shard_map/pallas_call | solution.py:561
  36.6 6.2 %all-to-all-done.1.got = f32[16,8,640]{2,1,0:T(8,128)S(1)} async-done(((f32[16,8,640]{2,1,0:T(8,128)}), f32[16,8,640]{2,1,0:T(8,128)S(1)}, u32[]{:S(2)}, u32[]{:S(2)}) %all-to-all-start.1) | async-done | bytes 327712 | tf_op jit(solution)/shard_map/all_to_all | solution.py:559
  42.8 2.2 %shard_map.69 = f32[16,16,1024]{2,1,0:T(8,128)} custom-call(f32[3,16,1024]{2,1,0:T(8,128)} %constant.10.clone.tables, f32[16,8,640]{2,1,0:T(8,128)S(1)} %all-to-all-done.1.got, f32[4,16,1024]{2,1,0:T(8,128)S(1)} %get-tuple-element.27.fourth, f32[16,16,1024]{2,1,0:T(8,128)} %get-tuple-element.28.base), custom_call_target="tpu_custom_call", output_to_operand_aliasing={{}: (3, {})} | custom-call | flops 41943040 | bytes 4194304 | tf_op jit(solution)/shard_map/pallas_call | solution.py:569
Async XLA Ops:
  3.8 11.1 %collective-permute-start = (f32[3,16,1024]{2,1,0:T(8,128)S(1)}, f32[3,16,1024]{2,1,0:T(8,128)S(1)}, u32[]{:S(2)}, u32[]{:S(2)}) collective-permute-start(f32[3,16,1024]{2,1,0:T(8,128)S(1)} %get-tuple-element.18), channel_id=1, source_target_pairs={{0,1},{1,0},{2,3},{3,2},{4,5},{5,4},{6,7},{7,6},{8,9},{9,8},{10,11... | collective-permute-start | bytes 589832 | tf_op jit(solution)/shard_map/ppermute | solution.py:492
  3.9 11.0 %collective-permute-start.1 = (f32[3,16,1024]{2,1,0:T(8,128)S(1)}, f32[3,16,1024]{2,1,0:T(8,128)S(1)}, u32[]{:S(2)}, u32[]{:S(2)}) collective-permute-start(f32[3,16,1024]{2,1,0:T(8,128)S(1)} %get-tuple-element.19), channel_id=1, source_target_pairs={{1,2},{2,1},{3,4},{4,3},{5,6},{6,5},{9,10},{10,9},{11,12},{12,11},... | collective-permute-start | bytes 589832 | tf_op jit(solution)/shard_map/ppermute | solution.py:492
  7.0 16.8 %all-to-all-start = ((f32[8,8,1536]{2,1,0:T(8,128)}), f32[8,8,1536]{2,1,0:T(8,128)S(1)}, u32[]{:S(2)}, u32[]{:S(2)}) async-start(f32[8,8,1536]{2,1,0:T(8,128)} %get-tuple-element.23), calls=%async_computation | async-start | bytes 786432 | tf_op jit(solution)/shard_map/all_to_all | solution.py:535
  16.2 17.4 %collective-permute-start.2 = (f32[6,8,1024]{2,1,0:T(8,128)S(1)}, f32[6,8,1024]{2,1,0:T(8,128)S(1)}, u32[]{:S(2)}, u32[]{:S(2)}) collective-permute-start(f32[6,8,1024]{2,1,0:T(8,128)S(1)} %get-tuple-element.25), channel_id=1, source_target_pairs={{0,8},{8,0},{16,24},{24,16},{32,40},{40,32},{48,56},{56,48},{64,72... | collective-permute-start | bytes 589832 | tf_op jit(solution)/shard_map/ppermute | solution.py:492
  17.8 15.8 %collective-permute-start.3 = (f32[6,8,1024]{2,1,0:T(8,128)S(1)}, f32[6,8,1024]{2,1,0:T(8,128)S(1)}, u32[]{:S(2)}, u32[]{:S(2)}) collective-permute-start(f32[6,8,1024]{2,1,0:T(8,128)S(1)} %get-tuple-element.26), channel_id=1, source_target_pairs={{8,16},{16,8},{24,32},{32,24},{40,48},{48,40},{56,64},{64,56},{72,... | collective-permute-start | bytes 589832 | tf_op jit(solution)/shard_map/ppermute | solution.py:492
  26.6 16.2 %all-to-all-start.1 = ((f32[16,8,640]{2,1,0:T(8,128)}), f32[16,8,640]{2,1,0:T(8,128)S(1)}, u32[]{:S(2)}, u32[]{:S(2)}) async-start(f32[16,8,640]{2,1,0:T(8,128)} %shard_map.67), calls=%async_computation.1 | async-start | bytes 655360 | tf_op jit(solution)/shard_map/all_to_all | solution.py:559

commit v3 on v2

--- a/solution.py
+++ b/solution.py
@@ -74,27 +74,18 @@
     return [v for pair in zip(smooth, detail) for v in pair]
 
 
-def lane_factors(stride):
-    run = np.arange(WIDE) // stride
-    ends = run[-1]
-    odd, even = run % 2 == 1, run % 2 == 0
-    table = np.zeros((16, WIDE), np.float64)
+def lift_runs(v, stride):
+    lane, count = lane_id(v[0].shape), len(v)
+    odd = lane // stride % 2 == 1
     for k, a in enumerate((A1, B1, A2, B2)):
-        at = even if k % 2 else odd
-        closed = run == (0 if k % 2 else ends)
-        before, after = (4 + k, k) if k % 2 else (k, 4 + k)
-        table[before] = np.where(at, np.where(closed, 2 * a, a), 0.0)
-        table[after] = np.where(at & ~closed, a, 0.0)
-    table[8] = np.where(even, 1.0 / GAIN, GAIN / 2.0)
-    return table.astype(np.float32)
-
-
-def lift_lanes(v, table, stride):
-    for k in range(4):
-        before = pltpu.roll(v, stride, 1)
-        after = pltpu.roll(v, WIDE - stride, 1)
-        v = v + table[k : k + 1, :] * before + table[4 + k : 5 + k, :] * after
-    return v * table[8:9, :]
+        up = [pltpu.roll(x, stride, 1) for x in v]
+        down = [pltpu.roll(x, LANES - stride, 1) for x in v]
+        before = [jnp.where(lane >= stride, up[t], up[t - 1] if t else down[t]) for t in range(count)]
+        after = [jnp.where(lane < LANES - stride, down[t], down[t + 1] if t + 1 < count else up[t]) for t in range(count)]
+        factor = jnp.where(odd, 0.0, a) if k % 2 else jnp.where(odd, a, 0.0)
+        v = [x + factor * (y + z) for x, y, z in zip(v, before, after)]
+    scale = jnp.where(odd, GAIN / 2.0, 1.0 / GAIN)
+    return [x * scale for x in v]
 
 
 def lane_id(shape):
@@ -169,14 +160,22 @@
         ref[at, tile(t)] = v
 
 
-def along_x(density, out, pay_e, pay_o, e1, x, sem):
-    part = x.shape[0] // 4
-    loads = [
-        pltpu.make_async_copy(density.at[pl.ds(k * part, part)], x.at[pl.ds(k * part, part)], sem.at[k])
-        for k in (0, 2, 1, 3)
+def along_x(weights3, weights4, density, out, pay_e, pay_o, e1, w3, w4, x, sem):
+    me = lax.axis_index("gy")
+
+    def load(k):
+        at = pl.ds(pl.multiple_of(k * 32, 32), 32)
+        return pltpu.make_async_copy(density.at[at], x.at[at], sem.at[k])
+
+    for k in range(4):
+        load(k).start()
+        load(k + 4).start()
+    hints = [
+        pltpu.make_async_copy(weights3.at[me], w3, sem.at[8]),
+        pltpu.make_async_copy(weights4.at[me], w4, sem.at[9]),
     ]
-    for load in loads:
-        load.start()
+    for hint in hints:
+        hint.start()
 
     def plane(i):
         z, y = i // 2, i % 2
@@ -189,13 +188,14 @@
             out[t, pl.ds(at, 8), :] = a[t]
             out[t, pl.ds(far, 8), :] = b[t]
 
-    loads[0].wait()
-    loads[1].wait()
-    times(8, plane, 4)
-    loads[2].wait()
-    loads[3].wait()
-    times(8, lambda i: plane(i + 8), 4)
-    flip = lax.axis_index("gy") % 2 == 1
+    def group(k):
+        load(k).wait()
+        load(k + 4).wait()
+        for i in range(4):
+            plane(4 * k + i)
+
+    times(4, group)
+    flip = me % 2 == 1
     even = lane_id((8, LANES)) % 2 == 0
 
     def column(t):
@@ -210,17 +210,13 @@
                 pay_e[c, pl.ds(half * 8, 8), lanes] = mix(flip, going_left[c], going_right[c])
                 pay_o[c, pl.ds(half * 8, 8), lanes] = mix(flip, going_right[c], going_left[c])
 
-    times(TILES, column, 2)
-
-
-def thin_y(weights3, weights4, e1, own, pay, w3, w4, e2, e3, sem):
+    times(TILES, column, 4)
+    for hint in hints:
+        hint.wait()
+
+
+def thin_y(w3, w4, e1, own, result, pay, e2, e3, sem):
     me = lax.axis_index("gy")
-    loads = [
-        pltpu.make_async_copy(weights3.at[me], w3, sem.at[0]),
-        pltpu.make_async_copy(weights4.at[me], w4, sem.at[1]),
-    ]
-    for load in loads:
-        load.start()
 
     def second(i):
         at = pl.multiple_of(i * 8, 8)
@@ -228,6 +224,15 @@
         put_tiles(e2, pl.ds(at, 8), s)
 
     times(8, second, 4)
+    three = jnp.dot(w3[...], e2[...], precision=HIGH, preferred_element_type=jnp.float32)
+    own[...] = three[0:16]
+    for to in range(pay.shape[0]):
+        right = mix(to == me + 1, three[16:24], three[24:32])
+        left = mix(to == me - 1, three[32:40], three[40:48])
+        pay[to, :, 0:WIDE] = mix(to > me, right, left)
+    parts = [pl.ds(0, WIDE), pl.ds(WIDE, WIDE // 2)]
+    sends = [pltpu.make_async_copy(pay.at[:, :, p], result.at[:, :, p], sem.at[k]) for k, p in enumerate(parts)]
+    sends[0].start()
 
     def third(i):
         at = pl.multiple_of(i * 8, 8)
@@ -235,20 +240,16 @@
         put_tiles(e3, pl.ds(at, 8), s)
 
     times(4, third, 4)
-    for load in loads:
-        load.wait()
-    three = jnp.dot(w3[...], e2[...], precision=HIGH, preferred_element_type=jnp.float32)
-    own[...] = three[0:16]
     four = jnp.dot(w4[...], e3[...], precision=HIGH, preferred_element_type=jnp.float32)
     for to in range(pay.shape[0]):
-        right = mix(to == me + 1, three[16:24], three[24:32])
-        left = mix(to == me - 1, three[32:40], three[40:48])
-        pay[to, :, 0:WIDE] = mix(to > me, right, left)
         pay[to, 0:4, WIDE:] = four[to * 4 : to * 4 + 4, : WIDE // 2]
         pay[to, 4:8, WIDE:] = four[to * 4 : to * 4 + 4, WIDE // 2 :]
-
-
-def along_y(x, got_e, got_o, one, two, pay_e, pay_o):
+    sends[1].start()
+    for send in sends:
+        send.wait()
+
+
+def along_y(x, got_e, got_o, one, two, pay_e, pay_o, cells, thick):
     me = lax.axis_index("gy")
     first, last, flip = me == 0, me == lax.axis_size("gy") - 1, me % 2 == 1
     even = lane_id((8, LANES)) % 2 == 0
@@ -293,9 +294,18 @@
             pay_o[c, :, lanes] = mix(flip, going_right[c], going_left[c])
 
     times(TILES, stack, TILES)
-
-
-def thin_z(weights3, weights4, two, own, got, pay, w3, w4, thick, cells, beyond, held4, turned3, turned4, sem):
+    for t in range(TILES):
+        for r in range(4):
+            low, high = [two[t, pl.ds(64 * half + 2 * r, 8, stride=8), :] for half in range(2)]
+            v = pack_two(low, high, even)
+            thick[pl.ds(4 * r, 4), tile(t)] = v[0:4]
+            thick[pl.ds(16 + 4 * r, 4), tile(t)] = v[4:8]
+    for i in range(2):
+        s, _ = lift_two(tiles_of(thick, pl.ds(8 * i, 8)), tiles_of(thick, pl.ds(16 + 8 * i, 8)), 2)
+        put_tiles(cells, pl.ds(8 * i, 8), s)
+
+
+def thin_z(weights3, weights4, cells, own, got, result, pay, w3, w4, beyond, held4, turned3, turned4, sem):
     mz = lax.axis_index("gz")
     loads = [
         pltpu.make_async_copy(weights3.at[mz], w3, sem.at[0]),
@@ -305,16 +315,6 @@
         load.start()
     me, count = lax.axis_index("gy"), got.shape[0]
     first, last = me == 0, me == count - 1
-    even = lane_id((8, LANES)) % 2 == 0
-    for t in range(TILES):
-        for r in range(4):
-            low, high = [two[t, pl.ds(64 * half + 2 * r, 8, stride=8), :] for half in range(2)]
-            v = pack_two(low, high, even)
-            thick[pl.ds(4 * r, 4), tile(t)] = v[0:4]
-            thick[pl.ds(16 + 4 * r, 4), tile(t)] = v[4:8]
-    for i in range(2):
-        s, _ = lift_two(tiles_of(thick, pl.ds(8 * i, 8)), tiles_of(thick, pl.ds(16 + 8 * i, 8)), 2)
-        put_tiles(cells, pl.ds(8 * i, 8), s)
     near = lambda k: got[jnp.clip(me + k, 0, count - 1), :, 0:WIDE]
     beyond[0:8] = own[0:8] + (mix(me >= 1, near(-1), 0.0) + mix(me >= 2, near(-2), 0.0))
     beyond[8:16] = own[8:16] + (mix(me < count - 1, near(1), 0.0) + mix(me < count - 2, near(2), 0.0))
@@ -340,23 +340,27 @@
             turned4[at(f), tile(t)] = pltpu.roll(v, LANES - f, 1) if f else v
     for load in loads:
         load.wait()
+    count, half = pay.shape[0], WIDE // 2
+    parts = [pl.ds(0, half), pl.ds(half, LANES)]
+    sends = [pltpu.make_async_copy(pay.at[:, :, p], result.at[:, :, p], sem.at[2 + k]) for k, p in enumerate(parts)]
     three = jnp.dot(w3[...], turned3[...], precision=HIGH, preferred_element_type=jnp.float32)
+    for to in range(count):
+        pay[to, 0:4, 0:half] = three[to * 4 : to * 4 + 4, :half]
+        pay[to, 4:8, 0:half] = three[to * 4 : to * 4 + 4, half:]
+    sends[0].start()
     four = jnp.dot(w4[...], turned4[...], precision=HIGH, preferred_element_type=jnp.float32)
-    count = pay.shape[0]
     lane = lane_id((count, LANES))
     for t in range(TILES):
         v = four[0:count, tile(t)]
         for k in range(1, 4):
             v = jnp.where(lane % 8 == k, pltpu.roll(four[k * count : (k + 1) * count, tile(t)], k, 1), v)
-        pay[:, t, WIDE // 2 :] = v
-    for to in range(count):
-        pay[to, 0:4, 0 : WIDE // 2] = three[to * 4 : to * 4 + 4, : WIDE // 2]
-        pay[to, 4:8, 0 : WIDE // 2] = three[to * 4 : to * 4 + 4, WIDE // 2 :]
-
-
-def along_z(tables, one, two, got_e, got_o, result, fourth, out, fine, spread, table, sem):
-    load = pltpu.make_async_copy(tables.at[0], table, sem.at[16])
-    load.start()
+        pay[:, t, half:] = v
+    sends[1].start()
+    for send in sends:
+        send.wait()
+
+
+def along_z(one, two, got_e, got_o, result, fourth, out, fine, spread, sem):
     me = lax.axis_index("gz")
     first, last, flip = me == 0, me == lax.axis_size("gz") - 1, me % 2 == 1
 
@@ -384,13 +388,12 @@
     sends = {z: pltpu.make_async_copy(out.at[z], result.at[z], sem.at[z]) for z in range(16) if z % 4}
     for z in range(1, 16, 2):
         sends[z].start()
-    load.wait()
     row = lax.broadcasted_iota(jnp.int32, (16, LANES), 0)
     here = (row % 2 == 0) & (lane_id((16, LANES)) % 2 == 0)
     for z in (1, 3, 5, 7, 0, 2, 4, 6):
-        v = lift_lanes(fine[pl.ds(z * 8, 8), :], table, 2)
+        v = lift_runs(tiles_of(fine, pl.ds(z * 8, 8)), 2)
         for t in range(TILES):
-            spread[t, pl.ds(z * 16, 8, stride=2), :] = v[:, tile(t)]
+            spread[t, pl.ds(z * 16, 8, stride=2), :] = v[t]
             w = jnp.where(here, spread[t, pl.ds(z * 16, 16), :], out[2 * z, :, tile(t)])
             if z % 2:
                 out[2 * z, :, tile(t)] = w
@@ -402,34 +405,28 @@
         send.wait()
 
 
-def join(tables, got, fourth, base, result, planes, spread, coarse, table, sem):
-    load = pltpu.make_async_copy(tables, table, sem.at[4])
-    load.start()
+def join(got, fourth, base, result, planes, spread, sem):
     half = WIDE // 2
     total = got[0]
     for k in range(1, got.shape[0]):
         total = total + got[k]
-    load.wait()
-    three = jnp.concatenate([total[0:4, :half], total[4:8, :half]], axis=1)
-    three = lift_lanes(three, table.at[1], 4)
-    four = jnp.concatenate([total[t : t + 1, half:] for t in range(TILES)], axis=1)
-    four = lift_lanes(four, table.at[2], 8)
+    three = [total[0:4, tile(t)] for t in range(TILES // 2)] + [total[4:8, tile(t)] for t in range(TILES // 2)]
+    three = lift_runs(three, 4)
+    four = lift_runs([total[t : t + 1, half:] for t in range(TILES)], 8)
+    lane = lane_id((4, LANES))
+    row = lax.broadcasted_iota(jnp.int32, (4, LANES), 0)
     for t in range(TILES):
-        v = three[:, tile(t)]
         for r in range(4):
-            coarse[t, pl.ds(r, 4, stride=4), :] = pltpu.roll(v, LANES - r, 1) if r else v
-        v = four[:, tile(t)]
-        here = lane_id((1, LANES)) % 8 == 0
-        for k in range(4):
-            at = pl.ds((k // 2) * 8 + (k % 2) * 2, 1)
-            moved = pltpu.roll(v, LANES - k, 1) if k else v
-            coarse[t, at, :] = jnp.where(here, moved, coarse[t, at, :])
+            v = pltpu.roll(three[t], LANES - r, 1) if r else three[t]
+            for k in range(r // 2, 4, 2) if r % 2 == 0 else ():
+                w = pltpu.roll(four[t], LANES - k, 1) if k else four[t]
+                v = jnp.where((lane % 8 == 0) & (row == 2 * (k // 2)), jnp.broadcast_to(w, v.shape), v)
+            spread[t, pl.ds(4 * r, 4, stride=16), :] = v
     row = lax.broadcasted_iota(jnp.int32, (16, LANES), 0)
     here = (row % 4 == 0) & (lane_id((16, LANES)) % 4 == 0)
     sends = [pltpu.make_async_copy(planes.at[i], result.at[4 * i], sem.at[i]) for i in range(4)]
     for i in range(4):
         for t in range(TILES):
-            spread[t, pl.ds(i * 16, 4, stride=4), :] = coarse[t, pl.ds(i * 4, 4), :]
             planes[i, :, tile(t)] = jnp.where(here, spread[t, pl.ds(i * 16, 16), :], fourth[i, :, tile(t)])
         sends[i].start()
     for send in sends:
@@ -514,66 +511,71 @@
     sems = lambda count: pltpu.SemaphoreType.DMA((count,))
     far, here = pl.BlockSpec(memory_space=pltpu.HBM), pl.BlockSpec(memory_space=pltpu.VMEM)
     stay = lambda v: pltpu.with_memory_space_constraint(jnp.asarray(v), pltpu.HBM)
-    tables = stay(np.stack([lane_factors(s) for s in (2, 4, 8)]))
     tiled = f32(TILES, planes * rows, LANES)
 
     payload = f32(3, 16, cells)
-    x, pay_e, pay_o, e1 = call(
+    x, pay_e, pay_o, e1, y3, y4 = call(
         along_x,
-        [tiled, payload, payload, f32(planes * rows // 2, cells)],
-        [vmem(planes * rows, cells), sems(4)],
-        in_specs=[far],
-    )(stay(density.reshape(planes * rows, cells)))
+        [tiled, payload, payload, f32(planes * rows // 2, cells), f32(48, 64), f32(4 * ny, 32)],
+        [vmem(planes * rows, cells), sems(10)],
+        in_specs=[far, far, far],
+    )(*[stay(w) for w in weights_y(ny)], stay(density.reshape(planes * rows, cells)))
     got_e, got_o = swap(pay_e, "gy", 0), swap(pay_o, "gy", 1)
+    pay = (ny, 8, cells * 3 // 2)
     own, pay = call(
         thin_y,
-        [f32(16, cells), f32(ny, 8, cells * 3 // 2)],
-        [vmem(48, 64), vmem(4 * ny, 32), vmem(64, cells), vmem(32, cells), sems(2)],
+        [f32(16, cells), f32(*pay)],
+        [vmem(*pay), vmem(64, cells), vmem(32, cells), sems(2)],
         cost=40 << 20,
-        in_specs=[far, far, here],
-    )(*[stay(w) for w in weights_y(ny)], e1)
+        in_specs=[here, here, here],
+        out_specs=[here, far],
+    )(y3, y4, e1)
     got = lax.all_to_all(pay, "gy", 0, 0, tiled=True)
 
     payload = f32(6, 8, cells)
-    one, two, pay_e, pay_o = call(along_y, [tiled, f32(TILES, planes * rows // 2, LANES), payload, payload], cost=400 << 20, input_output_aliases={0: 0})(
-        x, got_e, got_o
-    )
+    one, two, pay_e, pay_o, third = call(
+        along_y,
+        [tiled, f32(TILES, planes * rows // 2, LANES), payload, payload, f32(16, cells)],
+        [vmem(32, cells)],
+        cost=400 << 20,
+        input_output_aliases={0: 0},
+    )(x, got_e, got_o)
     got_e, got_o = swap(pay_e, "gz", 0), swap(pay_o, "gz", 1)
+    pay = (nz, 8, cells // 2 + LANES)
     pay = call(
         thin_z,
-        f32(nz, 8, cells // 2 + LANES),
+        f32(*pay),
         [
+            vmem(*pay),
             vmem(4 * nz, 16),
             vmem(4 * nz, 32),
-            vmem(32, cells),
-            vmem(16, cells),
             vmem(16, cells),
             vmem(4, cells),
             vmem(16, cells),
             vmem(32, cells),
-            sems(2),
+            sems(4),
         ],
         cost=40 << 20,
         in_specs=[far, far, here, here, here],
-    )(*[stay(w) for w in weights_z(nz)], two, own, got)
+        out_specs=far,
+    )(*[stay(w) for w in weights_z(nz)], third, own, got)
     got = lax.all_to_all(pay, "gz", 0, 0, tiled=True)
 
     base, fourth = call(
         along_z,
         [f32(planes, rows, cells), f32(planes // 4, rows, cells)],
-        [vmem(planes, rows, cells), vmem(64, cells), vmem(TILES, 128, LANES), vmem(16, cells), sems(planes + 1)],
+        [vmem(planes, rows, cells), vmem(64, cells), vmem(TILES, 128, LANES), sems(planes)],
         cost=400 << 20,
-        in_specs=[far] + [here] * 4,
         out_specs=[far, here],
-    )(tables, one, two, got_e, got_o)
+    )(one, two, got_e, got_o)
     return call(
         join,
         f32(planes, rows, cells),
-        [vmem(planes // 4, rows, cells), vmem(TILES, 64, LANES), vmem(TILES, 16, LANES), vmem(3, 16, cells), sems(5)],
-        in_specs=[far, here, here, far],
+        [vmem(planes // 4, rows, cells), vmem(TILES, 64, LANES), sems(4)],
+        in_specs=[here, here, far],
         out_specs=far,
-        input_output_aliases={3: 0},
-    )(tables, got, fourth, stay(base))
+        input_output_aliases={2: 0},
+    )(got, fourth, stay(base))
 
 
 def solution(mesh):

time: 45.4 us -> 43.7 us (0.963)
  Pallas kernels: 15.5 us -> 13 us
  waiting for transfers between devices: 11.5 us -> 12.3 us
    all_to_all x1, waiting for transfers between devices: 6.19 us -> 7.34 us  [per_device(): got = lax.all_to_all(pay, 'gz', 0, 0, tiled=True)]
    pallas_call x1, Pallas kernels: 2.97 us -> 1.82 us  [per_device(): call(along_z, [f32(planes, rows, cells), f32(planes // 4, rows, cells)],...]
    pallas_call x1, Pallas kernels: 2.17 us -> 1.25 us  [per_device(): call(join, f32(planes, rows, cells), [vmem(planes // 4, rows, cells), vme...]
    pallas_call x3, Pallas kernels: 9 us -> 8.2 us  [the longest x1 3.65 us: per_device(): call(along_x, [tiled, payload, payload, f32(planes * rows // 2, cells), f...]
  transfers between devices with their start and end apart: 6 -> 6, of which waited for: 2 -> 2; matrix products, arithmetic and copies ran while one was open for 0% -> 0% of each run, Pallas kernels for 21% -> 19%
where the time goes in v3:
time: 43.7 us; the launch traced here: 43.3 us
  starting transfers between devices  17.9 us (41%)
  Pallas kernels  13 us (30%)
  waiting for transfers between devices  12.3 us (28%)
    all_to_all x1, starting transfers between devices, per_device(): got = lax.all_to_all(pay, 'gy', 0, 0, tiled=True)  7.83 us
    all_to_all x1, waiting for transfers between devices, per_device(): got = lax.all_to_all(pay, 'gz', 0, 0, tiled=True)  7.34 us
    all_to_all x1, starting transfers between devices, per_device(): got = lax.all_to_all(pay, 'gz', 0, 0, tiled=True)  7.04 us
    all_to_all x1, waiting for transfers between devices, per_device(): got = lax.all_to_all(pay, 'gy', 0, 0, tiled=True)  4.94 us
    pallas_call x1, Pallas kernels, per_device(): call(along_x, [tiled, payload, payload, f32(planes * rows // 2, cells), f...  3.65 us
    ppermute x4, starting transfers between devices, swap(): return lax.ppermute(values, axis, pairs)  2.99 us
    pallas_call x1, Pallas kernels, per_device(): call(thin_z, f32(*pay), [vmem(*pay), vmem(4 * nz, 16), vmem(4 * nz, 32),...  2.31 us
    pallas_call x1, Pallas kernels, per_device(): call(thin_y, [f32(16, cells), f32(*pay)], [vmem(*pay), vmem(64, cells), v...  2.25 us
  transfers between devices with their start and end apart: 6, of which 2 were waited for; matrix products, arithmetic and copies ran while one was open for 0% of the time, Pallas kernels for 19%

profile of v3, /device:TPU:0, one launch (start us, length us, event | category | flops | bytes accessed | tf_op | source)
XLA Modules:
  0.0 43.3 jit_solution(17100386032161716242)
XLA Ops:
  0.0 3.6 %shard_map.55 = (f32[8,256,128]{2,1,0:T(8,128)S(1)}, f32[3,16,1024]{2,1,0:T(8,128)S(1)}, f32[3,16,1024]{2,1,0:T(8,128)S(1)}, f32[128,1024]{1,0:T(8,128)S(1)}, f3...) custom-call(f32[8,48,64]{2,1,0:T(8,128)} %constant.8.clone.weights3, f32[8,32,32]{2,1,0:T(8,128)} %constant.9.clone.weights4, ...), custom_call_target="tpu_custom_call" | custom-call | flops 41943040 | bytes 4194304 | tf_op jit(solution)/shard_map/pallas_call | solution.py:517
  3.7 0.1 collective-permute-start
  3.7 0.7 %collective-permute-start.1 = (f32[3,16,1024]{2,1,0:T(8,128)S(1)}, f32[3,16,1024]{2,1,0:T(8,128)S(1)}, u32[]{:S(2)}, u32[]{:S(2)}) collective-permute-start(f32[3,16,1024]{2,1,0:T(8,128)S(1)} %get-tuple-element.22), channel_id=1, source_target_pairs={{1,2},{2,1},{3,4},{4,3},{5,6},{6,5},{9,10},{10,9},{11,12},{12,11},... | collective-permute-start | bytes 589832 | tf_op jit(solution)/shard_map/ppermute | solution.py:489
  4.4 2.2 %shard_map.57 = (f32[16,1024]{1,0:T(8,128)S(1)}, f32[8,8,1536]{2,1,0:T(8,128)}) custom-call(f32[48,64]{1,0:T(8,128)S(1)} %get-tuple-element.24.w3, f32[32,32]{1,0:T(8,128)S(1)} %get-tuple-element.25.w4, f32[128,1024]{1,0:T(8,128)S(1)} %get-tuple-element.26.e1), custom_call_target="tpu_custom_call" | custom-call | flops 419430400 | bytes 4194304 | tf_op jit(solution)/shard_map/pallas_call | solution.py:525
  6.7 7.8 %all-to-all-start = ((f32[8,8,1536]{2,1,0:T(8,128)}), f32[8,8,1536]{2,1,0:T(8,128)S(1)}, u32[]{:S(2)}, u32[]{:S(2)}) async-start(f32[8,8,1536]{2,1,0:T(8,128)} %get-tuple-element.28), calls=%async_computation | async-start | bytes 786432 | tf_op jit(solution)/shard_map/all_to_all | solution.py:533
  14.5 0.0 collective-permute-done.got_e
  14.5 0.0 collective-permute-done.1.got_o
  14.5 1.7 %shard_map.56 = (f32[8,256,128]{2,1,0:T(8,128)S(1)}, f32[8,128,128]{2,1,0:T(8,128)S(1)}, f32[6,8,1024]{2,1,0:T(8,128)S(1)}, f32[6,8,1024]{2,1,0:T(8,128)S(1)}, f32[16,1024]{1,0:T(8,128)S(1)}) custom-call(f32[8,256,128]{2,1,0:T(8,128)S(1)} %get-tuple-element.20.x, f32[3,16,1024]{2,1,0:T(8,128)S(1)} %collective-permute-done.got_e, ...), custom_call_target="tpu_custom_call", output_to_operand_aliasing={{0}: (0, {})} | custom-call | flops 4194304000 | bytes 4194304 | tf_op jit(solution)/shard_map/pallas_call | solution.py:536
  16.3 1.6 %collective-permute-start.2 = (f32[6,8,1024]{2,1,0:T(8,128)S(1)}, f32[6,8,1024]{2,1,0:T(8,128)S(1)}, u32[]{:S(2)}, u32[]{:S(2)}) collective-permute-start(f32[6,8,1024]{2,1,0:T(8,128)S(1)} %get-tuple-element.31), channel_id=1, source_target_pairs={{0,8},{8,0},{16,24},{24,16},{32,40},{40,32},{48,56},{56,48},{64,72... | collective-permute-start | bytes 589832 | tf_op jit(solution)/shard_map/ppermute | solution.py:489
  17.8 0.7 %collective-permute-start.3 = (f32[6,8,1024]{2,1,0:T(8,128)S(1)}, f32[6,8,1024]{2,1,0:T(8,128)S(1)}, u32[]{:S(2)}, u32[]{:S(2)}) collective-permute-start(f32[6,8,1024]{2,1,0:T(8,128)S(1)} %get-tuple-element.32), channel_id=1, source_target_pairs={{8,16},{16,8},{24,32},{32,24},{40,48},{48,40},{56,64},{64,56},{72,... | collective-permute-start | bytes 589832 | tf_op jit(solution)/shard_map/ppermute | solution.py:489
  18.5 4.9 %all-to-all-done.got = f32[8,8,1536]{2,1,0:T(8,128)S(1)} async-done(((f32[8,8,1536]{2,1,0:T(8,128)}), f32[8,8,1536]{2,1,0:T(8,128)S(1)}, u32[]{:S(2)}, u32[]{:S(2)}) %all-to-all-start) | async-done | bytes 393248 | tf_op jit(solution)/shard_map/all_to_all | solution.py:533
  23.5 2.3 %shard_map.58 = f32[16,8,640]{2,1,0:T(8,128)} custom-call(f32[16,64,16]{2,1,0:T(8,128)} %constant.10.clone.weights3, f32[16,64,32]{2,1,0:T(8,128)} %constant.11.clone.weights4, f32[16,1024]{1,0:T(8,128)S(1)} %get-tuple-element.23.cells, f32[16,1024]{1,0:T(8,128)S(1)} %get-tuple-element.27.own, f32[8,8,1536]{2,1,0:T(8,128)S(1)} %all-to-all-done.got), custom_call_target="tpu_custom_call" | custom-call | flops 419430400 | bytes 4194304 | tf_op jit(solution)/shard_map/pallas_call | solution.py:545
  25.8 7.0 %all-to-all-start.1 = ((f32[16,8,640]{2,1,0:T(8,128)}), f32[16,8,640]{2,1,0:T(8,128)S(1)}, u32[]{:S(2)}, u32[]{:S(2)}) async-start(f32[16,8,640]{2,1,0:T(8,128)} %shard_map.58), calls=%async_computation.1 | async-start | bytes 655360 | tf_op jit(solution)/shard_map/all_to_all | solution.py:562
  32.8 0.0 collective-permute-done.2.got_e
  32.8 0.0 collective-permute-done.3.got_o
  32.8 1.8 %shard_map.59 = (f32[16,16,1024]{2,1,0:T(8,128)}, f32[4,16,1024]{2,1,0:T(8,128)S(1)}) custom-call(f32[8,256,128]{2,1,0:T(8,128)S(1)} %get-tuple-element.29.one, f32[8,128,128]{2,1,0:T(8,128)S(1)} %get-tuple-element.30.two, f32[6,8,1024]{2,1,0:T(8,128)S(1)} %collective-permute-done.2.got_e, f32[6,8,1024]{2,1,0:T(8,128)S(1)} %collective-permute-done.3.got_o), custom_call_target="tpu_custom_call" | custom-call | flops 4194304000 | bytes 4194304 | tf_op jit(solution)/shard_map/pallas_call | solution.py:564
  34.7 7.3 %all-to-all-done.1.got = f32[16,8,640]{2,1,0:T(8,128)S(1)} async-done(((f32[16,8,640]{2,1,0:T(8,128)}), f32[16,8,640]{2,1,0:T(8,128)S(1)}, u32[]{:S(2)}, u32[]{:S(2)}) %all-to-all-start.1) | async-done | bytes 327712 | tf_op jit(solution)/shard_map/all_to_all | solution.py:562
  42.0 1.3 %shard_map.60 = f32[16,16,1024]{2,1,0:T(8,128)} custom-call(f32[16,8,640]{2,1,0:T(8,128)S(1)} %all-to-all-done.1.got, f32[4,16,1024]{2,1,0:T(8,128)S(1)} %get-tuple-element.33.fourth, f32[16,16,1024]{2,1,0:T(8,128)} %get-tuple-element.34.base), custom_call_target="tpu_custom_call", output_to_operand_aliasing={{}: (2, {})} | custom-call | flops 41943040 | bytes 4194304 | tf_op jit(solution)/shard_map/pallas_call | solution.py:571
Async XLA Ops:
  3.7 10.9 %collective-permute-start = (f32[3,16,1024]{2,1,0:T(8,128)S(1)}, f32[3,16,1024]{2,1,0:T(8,128)S(1)}, u32[]{:S(2)}, u32[]{:S(2)}) collective-permute-start(f32[3,16,1024]{2,1,0:T(8,128)S(1)} %get-tuple-element.21), channel_id=1, source_target_pairs={{0,1},{1,0},{2,3},{3,2},{4,5},{5,4},{6,7},{7,6},{8,9},{9,8},{10,11... | collective-permute-start | bytes 589832 | tf_op jit(solution)/shard_map/ppermute | solution.py:489
  3.7 10.8 %collective-permute-start.1 = (f32[3,16,1024]{2,1,0:T(8,128)S(1)}, f32[3,16,1024]{2,1,0:T(8,128)S(1)}, u32[]{:S(2)}, u32[]{:S(2)}) collective-permute-start(f32[3,16,1024]{2,1,0:T(8,128)S(1)} %get-tuple-element.22), channel_id=1, source_target_pairs={{1,2},{2,1},{3,4},{4,3},{5,6},{6,5},{9,10},{10,9},{11,12},{12,11},... | collective-permute-start | bytes 589832 | tf_op jit(solution)/shard_map/ppermute | solution.py:489
  6.7 16.8 %all-to-all-start = ((f32[8,8,1536]{2,1,0:T(8,128)}), f32[8,8,1536]{2,1,0:T(8,128)S(1)}, u32[]{:S(2)}, u32[]{:S(2)}) async-start(f32[8,8,1536]{2,1,0:T(8,128)} %get-tuple-element.28), calls=%async_computation | async-start | bytes 786432 | tf_op jit(solution)/shard_map/all_to_all | solution.py:533
  16.3 16.6 %collective-permute-start.2 = (f32[6,8,1024]{2,1,0:T(8,128)S(1)}, f32[6,8,1024]{2,1,0:T(8,128)S(1)}, u32[]{:S(2)}, u32[]{:S(2)}) collective-permute-start(f32[6,8,1024]{2,1,0:T(8,128)S(1)} %get-tuple-element.31), channel_id=1, source_target_pairs={{0,8},{8,0},{16,24},{24,16},{32,40},{40,32},{48,56},{56,48},{64,72... | collective-permute-start | bytes 589832 | tf_op jit(solution)/shard_map/ppermute | solution.py:489
  17.8 15.0 %collective-permute-start.3 = (f32[6,8,1024]{2,1,0:T(8,128)S(1)}, f32[6,8,1024]{2,1,0:T(8,128)S(1)}, u32[]{:S(2)}, u32[]{:S(2)}) collective-permute-start(f32[6,8,1024]{2,1,0:T(8,128)S(1)} %get-tuple-element.32), channel_id=1, source_target_pairs={{8,16},{16,8},{24,32},{32,24},{40,48},{48,40},{56,64},{64,56},{72,... | collective-permute-start | bytes 589832 | tf_op jit(solution)/shard_map/ppermute | solution.py:489
  25.8 16.2 %all-to-all-start.1 = ((f32[16,8,640]{2,1,0:T(8,128)}), f32[16,8,640]{2,1,0:T(8,128)S(1)}, u32[]{:S(2)}, u32[]{:S(2)}) async-start(f32[16,8,640]{2,1,0:T(8,128)} %shard_map.58), calls=%async_computation.1 | async-start | bytes 655360 | tf_op jit(solution)/shard_map/all_to_all | solution.py:562

commit v4 on v3

--- a/solution.py
+++ b/solution.py
@@ -2,6 +2,7 @@
 
 import jax
 import jax.numpy as jnp
+import ml_dtypes
 import numpy as np
 from jax import lax
 from jax.experimental import pallas as pl
@@ -17,7 +18,6 @@
 WIDE = 1024
 LANES = 128
 TILES = WIDE // LANES
-HIGH = lax.Precision.HIGHEST
 
 
 def lift(rows, left, right, first, last, choose):
@@ -74,18 +74,55 @@
     return [v for pair in zip(smooth, detail) for v in pair]
 
 
+def filters():
+    fixed = lambda c, a, b: a if c else b
+    smooth, detail = lift(list(np.eye(32)), (0.0, 0.0), (0.0, 0.0), True, True, fixed)
+    return [float(v) for v in smooth[8][16:21]], [float(v) for v in detail[8][17:21]]
+
+
+def moved(tiles, step):
+    if step == 0:
+        return list(tiles)
+    lane, count = lane_id(tiles[0].shape), len(tiles)
+    r = [pltpu.roll(x, -step % LANES, 1) for x in tiles]
+    if step > 0:
+        return [jnp.where(lane < LANES - step, r[t], r[t + 1]) if t + 1 < count else r[t] for t in range(count)]
+    return [jnp.where(lane >= -step, r[t], r[t - 1]) if t else r[t] for t in range(count)]
+
+
 def lift_runs(v, stride):
-    lane, count = lane_id(v[0].shape), len(v)
-    odd = lane // stride % 2 == 1
-    for k, a in enumerate((A1, B1, A2, B2)):
-        up = [pltpu.roll(x, stride, 1) for x in v]
-        down = [pltpu.roll(x, LANES - stride, 1) for x in v]
-        before = [jnp.where(lane >= stride, up[t], up[t - 1] if t else down[t]) for t in range(count)]
-        after = [jnp.where(lane < LANES - stride, down[t], down[t + 1] if t + 1 < count else up[t]) for t in range(count)]
-        factor = jnp.where(odd, 0.0, a) if k % 2 else jnp.where(odd, a, 0.0)
-        v = [x + factor * (y + z) for x, y, z in zip(v, before, after)]
-    scale = jnp.where(odd, GAIN / 2.0, 1.0 / GAIN)
-    return [x * scale for x in v]
+    run = lane_id(v[0].shape) // stride
+    ends = LANES // stride - 1
+    at = {k: moved(v, k * stride) for k in range(-4, 5)}
+    for k in range(1, 5):
+        for j in range(k):
+            at[-k][0] = jnp.where(run == j, at[k - 2 * j][0], at[-k][0])
+    for k in range(1, 5):
+        for j in range(k):
+            at[k][-1] = jnp.where(run == ends - j, at[2 * j - k][-1], at[k][-1])
+    smooth, detail = filters()
+    weight = [jnp.where(run % 2 == 0, a, b) for a, b in zip(smooth, detail + [0.0])]
+    out = [weight[0] * x for x in v]
+    for k in range(1, 5):
+        out = [x + weight[k] * (y + z) for x, y, z in zip(out, at[-k], at[k])]
+    return out
+
+
+def split_left(w):
+    parts = []
+    for _ in range(3):
+        parts.append((w - sum(p.astype(np.float32) for p in parts)).astype(ml_dtypes.bfloat16))
+    one, two, three = parts
+    return np.concatenate([one, one, two, one, two, three], axis=-1)
+
+
+def product(left, x):
+    one = x.astype(jnp.bfloat16)
+    rest = x - one.astype(jnp.float32)
+    two = rest.astype(jnp.bfloat16)
+    three = (rest - two.astype(jnp.float32)).astype(jnp.bfloat16)
+    right = jnp.concatenate([one, two, one, three, two, one], axis=0)
+    return jnp.dot(left, right, preferred_element_type=jnp.float32)
 
 
 def lane_id(shape):
@@ -223,8 +260,8 @@
         s, _ = lift_two(tiles_of(e1, pl.ds(at, 8)), tiles_of(e1, pl.ds(at + 64, 8)), 2)
         put_tiles(e2, pl.ds(at, 8), s)
 
-    times(8, second, 4)
-    three = jnp.dot(w3[...], e2[...], precision=HIGH, preferred_element_type=jnp.float32)
+    times(8, second, 8)
+    three = product(w3[...], e2[...])
     own[...] = three[0:16]
     for to in range(pay.shape[0]):
         right = mix(to == me + 1, three[16:24], three[24:32])
@@ -240,7 +277,7 @@
         put_tiles(e3, pl.ds(at, 8), s)
 
     times(4, third, 4)
-    four = jnp.dot(w4[...], e3[...], precision=HIGH, preferred_element_type=jnp.float32)
+    four = product(w4[...], e3[...])
     for to in range(pay.shape[0]):
         pay[to, 0:4, WIDE:] = four[to * 4 : to * 4 + 4, : WIDE // 2]
         pay[to, 4:8, WIDE:] = four[to * 4 : to * 4 + 4, WIDE // 2 :]
@@ -343,12 +380,12 @@
     count, half = pay.shape[0], WIDE // 2
     parts = [pl.ds(0, half), pl.ds(half, LANES)]
     sends = [pltpu.make_async_copy(pay.at[:, :, p], result.at[:, :, p], sem.at[2 + k]) for k, p in enumerate(parts)]
-    three = jnp.dot(w3[...], turned3[...], precision=HIGH, preferred_element_type=jnp.float32)
+    three = product(w3[...], turned3[...])
     for to in range(count):
         pay[to, 0:4, 0:half] = three[to * 4 : to * 4 + 4, :half]
         pay[to, 4:8, 0:half] = three[to * 4 : to * 4 + 4, half:]
     sends[0].start()
-    four = jnp.dot(w4[...], turned4[...], precision=HIGH, preferred_element_type=jnp.float32)
+    four = product(w4[...], turned4[...])
     lane = lane_id((count, LANES))
     for t in range(TILES):
         v = four[0:count, tile(t)]
@@ -456,8 +493,8 @@
         for z in range(2):
             w4[a, :, :, z, z] = four[:, mine].reshape(devices, 2, 16)
     return (
-        w3.reshape(devices, 48, 64).astype(np.float32),
-        w4.reshape(devices, 4 * devices, 32).astype(np.float32),
+        split_left(w3.reshape(devices, 48, 64).astype(np.float32)),
+        split_left(w4.reshape(devices, 4 * devices, 32).astype(np.float32)),
     )
 
 
@@ -476,8 +513,8 @@
                     for o in range(2):
                         w4[a, :, o, :, f, o, zz] = four[:, z].reshape(devices, 2).T
     return (
-        w3.reshape(devices, 4 * devices, 16).astype(np.float32),
-        w4.reshape(devices, 4 * devices, 32).astype(np.float32),
+        split_left(w3.reshape(devices, 4 * devices, 16).astype(np.float32)),
+        split_left(w4.reshape(devices, 4 * devices, 32).astype(np.float32)),
     )
 
 
@@ -491,6 +528,10 @@
 
 def f32(*shape):
     return jax.ShapeDtypeStruct(shape, jnp.float32)
+
+
+def bf16(*shape):
+    return jax.ShapeDtypeStruct(shape, jnp.bfloat16)
 
 
 def call(body, out, scratch=(), cost=4 << 20, **more):
@@ -516,7 +557,7 @@
     payload = f32(3, 16, cells)
     x, pay_e, pay_o, e1, y3, y4 = call(
         along_x,
-        [tiled, payload, payload, f32(planes * rows // 2, cells), f32(48, 64), f32(4 * ny, 32)],
+        [tiled, payload, payload, f32(planes * rows // 2, cells), bf16(48, 6 * 64), bf16(4 * ny, 6 * 32)],
         [vmem(planes * rows, cells), sems(10)],
         in_specs=[far, far, far],
     )(*[stay(w) for w in weights_y(ny)], stay(density.reshape(planes * rows, cells)))
@@ -547,8 +588,8 @@
         f32(*pay),
         [
             vmem(*pay),
-            vmem(4 * nz, 16),
-            vmem(4 * nz, 32),
+            pltpu.VMEM((4 * nz, 6 * 16), jnp.bfloat16),
+            pltpu.VMEM((4 * nz, 6 * 32), jnp.bfloat16),
             vmem(16, cells),
             vmem(4, cells),
             vmem(16, cells),

time: 43.7 us -> 42.7 us (0.977)
  Pallas kernels: 13 us -> 12.1 us
    pallas_call x1, Pallas kernels: 2.25 us -> 1.79 us  [per_device(): call(thin_y, [f32(16, cells), f32(*pay)], [vmem(*pay), vmem(64, cells), v...]
  transfers between devices with their start and end apart: 6 -> 6, of which waited for: 2 -> 2; matrix products, arithmetic and copies ran while one was open for 0% -> 0% of each run, Pallas kernels for 19% -> 17%
where the time goes in v4:
time: 42.7 us; the launch traced here: 42.3 us
  starting transfers between devices  17.9 us (42%)
  waiting for transfers between devices  12.3 us (29%)
  Pallas kernels  12.1 us (28%)
    all_to_all x1, starting transfers between devices, per_device(): got = lax.all_to_all(pay, 'gy', 0, 0, tiled=True)  7.83 us
    all_to_all x1, waiting for transfers between devices, per_device(): got = lax.all_to_all(pay, 'gz', 0, 0, tiled=True)  7.36 us
    all_to_all x1, starting transfers between devices, per_device(): got = lax.all_to_all(pay, 'gz', 0, 0, tiled=True)  7.05 us
    all_to_all x1, waiting for transfers between devices, per_device(): got = lax.all_to_all(pay, 'gy', 0, 0, tiled=True)  4.94 us
    pallas_call x1, Pallas kernels, per_device(): call(along_x, [tiled, payload, payload, f32(planes * rows // 2, cells), b...  3.65 us
    ppermute x4, starting transfers between devices, swap(): return lax.ppermute(values, axis, pairs)  2.99 us
    pallas_call x1, Pallas kernels, per_device(): call(thin_z, f32(*pay), [vmem(*pay), pltpu.VMEM((4 * nz, 6 * 16), jnp.bfl...  2 us
    pallas_call x1, Pallas kernels, per_device(): call(along_z, [f32(planes, rows, cells), f32(planes // 4, rows, cells)],...  1.8 us
  transfers between devices with their start and end apart: 6, of which 2 were waited for; matrix products, arithmetic and copies ran while one was open for 0% of the time, Pallas kernels for 17%

profile of v4, /device:TPU:0, one launch (start us, length us, event | category | flops | bytes accessed | tf_op | source)
XLA Modules:
  0.0 42.3 jit_solution(6352191519706440602)
XLA Ops:
  0.0 3.6 %shard_map.55 = (f32[8,256,128]{2,1,0:T(8,128)S(1)}, f32[3,16,1024]{2,1,0:T(8,128)S(1)}, f32[3,16,1024]{2,1,0:T(8,128)S(1)}, f32[128,1024]{1,0:T(8,128)S(1)}, bf...) custom-call(bf16[8,48,384]{2,1,0:T(8,128)(2,1)} %constant.8.clone.weights3, ...), custom_call_target="tpu_custom_call" | custom-call | flops 41943040 | bytes 4194304 | tf_op jit(solution)/shard_map/pallas_call | solution.py:558
  3.7 0.1 collective-permute-start
  3.7 0.7 %collective-permute-start.1 = (f32[3,16,1024]{2,1,0:T(8,128)S(1)}, f32[3,16,1024]{2,1,0:T(8,128)S(1)}, u32[]{:S(2)}, u32[]{:S(2)}) collective-permute-start(f32[3,16,1024]{2,1,0:T(8,128)S(1)} %get-tuple-element.22), channel_id=1, source_target_pairs={{1,2},{2,1},{3,4},{4,3},{5,6},{6,5},{9,10},{10,9},{11,12},{12,11},... | collective-permute-start | bytes 589832 | tf_op jit(solution)/shard_map/ppermute | solution.py:526
  4.4 1.8 %shard_map.57 = (f32[16,1024]{1,0:T(8,128)S(1)}, f32[8,8,1536]{2,1,0:T(8,128)}) custom-call(bf16[48,384]{1,0:T(8,128)(2,1)S(1)} %get-tuple-element.24.w3, bf16[32,192]{1,0:T(8,128)(2,1)S(1)} %get-tuple-element.25.w4, f32[128,1024]{1,0:T(8,128)S(1)} %get-tuple-element.26.e1), custom_call_target="tpu_custom_call" | custom-call | flops 419430400 | bytes 4194304 | tf_op jit(solution)/shard_map/pallas_call | solution.py:566
  6.2 7.8 %all-to-all-start = ((f32[8,8,1536]{2,1,0:T(8,128)}), f32[8,8,1536]{2,1,0:T(8,128)S(1)}, u32[]{:S(2)}, u32[]{:S(2)}) async-start(f32[8,8,1536]{2,1,0:T(8,128)} %get-tuple-element.28), calls=%async_computation | async-start | bytes 786432 | tf_op jit(solution)/shard_map/all_to_all | solution.py:574
  14.1 0.0 collective-permute-done.got_e
  14.1 0.0 collective-permute-done.1.got_o
  14.1 1.7 %shard_map.56 = (f32[8,256,128]{2,1,0:T(8,128)S(1)}, f32[8,128,128]{2,1,0:T(8,128)S(1)}, f32[6,8,1024]{2,1,0:T(8,128)S(1)}, f32[6,8,1024]{2,1,0:T(8,128)S(1)}, f32[16,1024]{1,0:T(8,128)S(1)}) custom-call(f32[8,256,128]{2,1,0:T(8,128)S(1)} %get-tuple-element.20.x, f32[3,16,1024]{2,1,0:T(8,128)S(1)} %collective-permute-done.got_e, ...), custom_call_target="tpu_custom_call", output_to_operand_aliasing={{0}: (0, {})} | custom-call | flops 4194304000 | bytes 4194304 | tf_op jit(solution)/shard_map/pallas_call | solution.py:577
  15.8 1.6 %collective-permute-start.2 = (f32[6,8,1024]{2,1,0:T(8,128)S(1)}, f32[6,8,1024]{2,1,0:T(8,128)S(1)}, u32[]{:S(2)}, u32[]{:S(2)}) collective-permute-start(f32[6,8,1024]{2,1,0:T(8,128)S(1)} %get-tuple-element.31), channel_id=1, source_target_pairs={{0,8},{8,0},{16,24},{24,16},{32,40},{40,32},{48,56},{56,48},{64,72... | collective-permute-start | bytes 589832 | tf_op jit(solution)/shard_map/ppermute | solution.py:526
  17.4 0.7 %collective-permute-start.3 = (f32[6,8,1024]{2,1,0:T(8,128)S(1)}, f32[6,8,1024]{2,1,0:T(8,128)S(1)}, u32[]{:S(2)}, u32[]{:S(2)}) collective-permute-start(f32[6,8,1024]{2,1,0:T(8,128)S(1)} %get-tuple-element.32), channel_id=1, source_target_pairs={{8,16},{16,8},{24,32},{32,24},{40,48},{48,40},{56,64},{64,56},{72,... | collective-permute-start | bytes 589832 | tf_op jit(solution)/shard_map/ppermute | solution.py:526
  18.1 4.9 %all-to-all-done.got = f32[8,8,1536]{2,1,0:T(8,128)S(1)} async-done(((f32[8,8,1536]{2,1,0:T(8,128)}), f32[8,8,1536]{2,1,0:T(8,128)S(1)}, u32[]{:S(2)}, u32[]{:S(2)}) %all-to-all-start) | async-done | bytes 393248 | tf_op jit(solution)/shard_map/all_to_all | solution.py:574
  23.0 2.0 %shard_map.58 = f32[16,8,640]{2,1,0:T(8,128)} custom-call(bf16[16,64,96]{2,1,0:T(8,128)(2,1)} %constant.10.clone.weights3, bf16[16,64,192]{2,1,0:T(8,128)(2,1)} %constant.11.clone.weights4, f32[16,1024]{1,0:T(8,128)S(1)} %get-tuple-element.23.cells, f32[16,1024]{1,0:T(8,128)S(1)} %get-tuple-element.27.own, f32[8,8,1536]{2,1,0:T(8,128)S(1)} %all-to-all-done.got), custom_call_target="tpu_custom_call" | custom-call | flops 419430400 | bytes 4194304 | tf_op jit(solution)/shard_map/pallas_call | solution.py:586
  25.0 7.0 %all-to-all-start.1 = ((f32[16,8,640]{2,1,0:T(8,128)}), f32[16,8,640]{2,1,0:T(8,128)S(1)}, u32[]{:S(2)}, u32[]{:S(2)}) async-start(f32[16,8,640]{2,1,0:T(8,128)} %shard_map.58), calls=%async_computation.1 | async-start | bytes 655360 | tf_op jit(solution)/shard_map/all_to_all | solution.py:603
  32.1 0.0 collective-permute-done.2.got_e
  32.1 0.0 collective-permute-done.3.got_o
  32.1 1.8 %shard_map.59 = (f32[16,16,1024]{2,1,0:T(8,128)}, f32[4,16,1024]{2,1,0:T(8,128)S(1)}) custom-call(f32[8,256,128]{2,1,0:T(8,128)S(1)} %get-tuple-element.29.one, f32[8,128,128]{2,1,0:T(8,128)S(1)} %get-tuple-element.30.two, f32[6,8,1024]{2,1,0:T(8,128)S(1)} %collective-permute-done.2.got_e, f32[6,8,1024]{2,1,0:T(8,128)S(1)} %collective-permute-done.3.got_o), custom_call_target="tpu_custom_call" | custom-call | flops 4194304000 | bytes 4194304 | tf_op jit(solution)/shard_map/pallas_call | solution.py:605
  33.9 7.4 %all-to-all-done.1.got = f32[16,8,640]{2,1,0:T(8,128)S(1)} async-done(((f32[16,8,640]{2,1,0:T(8,128)}), f32[16,8,640]{2,1,0:T(8,128)S(1)}, u32[]{:S(2)}, u32[]{:S(2)}) %all-to-all-start.1) | async-done | bytes 327712 | tf_op jit(solution)/shard_map/all_to_all | solution.py:603
  41.2 1.1 %shard_map.60 = f32[16,16,1024]{2,1,0:T(8,128)} custom-call(f32[16,8,640]{2,1,0:T(8,128)S(1)} %all-to-all-done.1.got, f32[4,16,1024]{2,1,0:T(8,128)S(1)} %get-tuple-element.33.fourth, f32[16,16,1024]{2,1,0:T(8,128)} %get-tuple-element.34.base), custom_call_target="tpu_custom_call", output_to_operand_aliasing={{}: (2, {})} | custom-call | flops 41943040 | bytes 4194304 | tf_op jit(solution)/shard_map/pallas_call | solution.py:612
Async XLA Ops:
  3.7 10.4 %collective-permute-start = (f32[3,16,1024]{2,1,0:T(8,128)S(1)}, f32[3,16,1024]{2,1,0:T(8,128)S(1)}, u32[]{:S(2)}, u32[]{:S(2)}) collective-permute-start(f32[3,16,1024]{2,1,0:T(8,128)S(1)} %get-tuple-element.21), channel_id=1, source_target_pairs={{0,1},{1,0},{2,3},{3,2},{4,5},{5,4},{6,7},{7,6},{8,9},{9,8},{10,11... | collective-permute-start | bytes 589832 | tf_op jit(solution)/shard_map/ppermute | solution.py:526
  3.7 10.3 %collective-permute-start.1 = (f32[3,16,1024]{2,1,0:T(8,128)S(1)}, f32[3,16,1024]{2,1,0:T(8,128)S(1)}, u32[]{:S(2)}, u32[]{:S(2)}) collective-permute-start(f32[3,16,1024]{2,1,0:T(8,128)S(1)} %get-tuple-element.22), channel_id=1, source_target_pairs={{1,2},{2,1},{3,4},{4,3},{5,6},{6,5},{9,10},{10,9},{11,12},{12,11},... | collective-permute-start | bytes 589832 | tf_op jit(solution)/shard_map/ppermute | solution.py:526
  6.2 16.8 %all-to-all-start = ((f32[8,8,1536]{2,1,0:T(8,128)}), f32[8,8,1536]{2,1,0:T(8,128)S(1)}, u32[]{:S(2)}, u32[]{:S(2)}) async-start(f32[8,8,1536]{2,1,0:T(8,128)} %get-tuple-element.28), calls=%async_computation | async-start | bytes 786432 | tf_op jit(solution)/shard_map/all_to_all | solution.py:574
  15.8 16.2 %collective-permute-start.2 = (f32[6,8,1024]{2,1,0:T(8,128)S(1)}, f32[6,8,1024]{2,1,0:T(8,128)S(1)}, u32[]{:S(2)}, u32[]{:S(2)}) collective-permute-start(f32[6,8,1024]{2,1,0:T(8,128)S(1)} %get-tuple-element.31), channel_id=1, source_target_pairs={{0,8},{8,0},{16,24},{24,16},{32,40},{40,32},{48,56},{56,48},{64,72... | collective-permute-start | bytes 589832 | tf_op jit(solution)/shard_map/ppermute | solution.py:526
  17.4 14.7 %collective-permute-start.3 = (f32[6,8,1024]{2,1,0:T(8,128)S(1)}, f32[6,8,1024]{2,1,0:T(8,128)S(1)}, u32[]{:S(2)}, u32[]{:S(2)}) collective-permute-start(f32[6,8,1024]{2,1,0:T(8,128)S(1)} %get-tuple-element.32), channel_id=1, source_target_pairs={{8,16},{16,8},{24,32},{32,24},{40,48},{48,40},{56,64},{64,56},{72,... | collective-permute-start | bytes 589832 | tf_op jit(solution)/shard_map/ppermute | solution.py:526
  25.0 16.2 %all-to-all-start.1 = ((f32[16,8,640]{2,1,0:T(8,128)}), f32[16,8,640]{2,1,0:T(8,128)S(1)}, u32[]{:S(2)}, u32[]{:S(2)}) async-start(f32[16,8,640]{2,1,0:T(8,128)} %shard_map.58), calls=%async_computation.1 | async-start | bytes 655360 | tf_op jit(solution)/shard_map/all_to_all | solution.py:603

commit v5 on v4

--- a/solution.py
+++ b/solution.py
@@ -261,7 +261,14 @@
         put_tiles(e2, pl.ds(at, 8), s)
 
     times(8, second, 8)
+    def third(i):
+        at = pl.multiple_of(i * 8, 8)
+        s, _ = lift_two(tiles_of(e2, pl.ds(at, 8)), tiles_of(e2, pl.ds(at + 32, 8)), 4)
+        put_tiles(e3, pl.ds(at, 8), s)
+
+    times(4, third, 4)
     three = product(w3[...], e2[...])
+    four = product(w4[...], e3[...])
     own[...] = three[0:16]
     for to in range(pay.shape[0]):
         right = mix(to == me + 1, three[16:24], three[24:32])
@@ -271,13 +278,6 @@
     sends = [pltpu.make_async_copy(pay.at[:, :, p], result.at[:, :, p], sem.at[k]) for k, p in enumerate(parts)]
     sends[0].start()
 
-    def third(i):
-        at = pl.multiple_of(i * 8, 8)
-        s, _ = lift_two(tiles_of(e2, pl.ds(at, 8)), tiles_of(e2, pl.ds(at + 32, 8)), 4)
-        put_tiles(e3, pl.ds(at, 8), s)
-
-    times(4, third, 4)
-    four = product(w4[...], e3[...])
     for to in range(pay.shape[0]):
         pay[to, 0:4, WIDE:] = four[to * 4 : to * 4 + 4, : WIDE // 2]
         pay[to, 4:8, WIDE:] = four[to * 4 : to * 4 + 4, WIDE // 2 :]
@@ -286,7 +286,14 @@
         send.wait()
 
 
-def along_y(x, got_e, got_o, one, two, pay_e, pay_o, cells, thick):
+def along_y(weights3, weights4, x, got_e, got_o, one, two, pay_e, pay_o, cells, w3, w4, thick, sem):
+    mz = lax.axis_index("gz")
+    hints = [
+        pltpu.make_async_copy(weights3.at[mz], w3, sem.at[0]),
+        pltpu.make_async_copy(weights4.at[mz], w4, sem.at[1]),
+    ]
+    for hint in hints:
+        hint.start()
     me = lax.axis_index("gy")
     first, last, flip = me == 0, me == lax.axis_size("gy") - 1, me % 2 == 1
     even = lane_id((8, LANES)) % 2 == 0
@@ -310,7 +317,7 @@
                 two[t, pl.ds(half * 64 + y, 8, stride=8), :] = v
 
     times(TILES, column, TILES)
-    flip = lax.axis_index("gz") % 2 == 1
+    flip = mz % 2 == 1
 
     def stack(t):
         lanes = tile_lanes(t)
@@ -340,16 +347,11 @@
     for i in range(2):
         s, _ = lift_two(tiles_of(thick, pl.ds(8 * i, 8)), tiles_of(thick, pl.ds(16 + 8 * i, 8)), 2)
         put_tiles(cells, pl.ds(8 * i, 8), s)
-
-
-def thin_z(weights3, weights4, cells, own, got, result, pay, w3, w4, beyond, held4, turned3, turned4, sem):
-    mz = lax.axis_index("gz")
-    loads = [
-        pltpu.make_async_copy(weights3.at[mz], w3, sem.at[0]),
-        pltpu.make_async_copy(weights4.at[mz], w4, sem.at[1]),
-    ]
-    for load in loads:
-        load.start()
+    for hint in hints:
+        hint.wait()
+
+
+def thin_z(w3, w4, cells, own, got, result, pay, beyond, held4, turned3, turned4, sem):
     me, count = lax.axis_index("gy"), got.shape[0]
     first, last = me == 0, me == count - 1
     near = lambda k: got[jnp.clip(me + k, 0, count - 1), :, 0:WIDE]
@@ -375,23 +377,21 @@
         v = held4[:, tile(t)]
         for f in range(8):
             turned4[at(f), tile(t)] = pltpu.roll(v, LANES - f, 1) if f else v
-    for load in loads:
-        load.wait()
-    count, half = pay.shape[0], WIDE // 2
-    parts = [pl.ds(0, half), pl.ds(half, LANES)]
-    sends = [pltpu.make_async_copy(pay.at[:, :, p], result.at[:, :, p], sem.at[2 + k]) for k, p in enumerate(parts)]
+    count = pay.shape[0]
+    parts = [pl.ds(0, WIDE), pl.ds(WIDE, LANES)]
+    sends = [pltpu.make_async_copy(pay.at[:, :, p], result.at[:, :, p], sem.at[k]) for k, p in enumerate(parts)]
     three = product(w3[...], turned3[...])
+    four = product(w4[...], turned4[...])
     for to in range(count):
-        pay[to, 0:4, 0:half] = three[to * 4 : to * 4 + 4, :half]
-        pay[to, 4:8, 0:half] = three[to * 4 : to * 4 + 4, half:]
+        pay[to, :, 0:WIDE] = three[to * 4 : to * 4 + 4]
     sends[0].start()
-    four = product(w4[...], turned4[...])
     lane = lane_id((count, LANES))
-    for t in range(TILES):
+    for t in range(TILES // 2):
         v = four[0:count, tile(t)]
-        for k in range(1, 4):
-            v = jnp.where(lane % 8 == k, pltpu.roll(four[k * count : (k + 1) * count, tile(t)], k, 1), v)
-        pay[:, t, half:] = v
+        for k in range(1, 8):
+            w = four[k % 4 * count : (k % 4 + 1) * count, tile(t + k // 4 * (TILES // 2))]
+            v = jnp.where(lane % 8 == k, pltpu.roll(w, k, 1), v)
+        pay[:, t, WIDE:] = v
     sends[1].start()
     for send in sends:
         send.wait()
@@ -443,13 +443,12 @@
 
 
 def join(got, fourth, base, result, planes, spread, sem):
-    half = WIDE // 2
     total = got[0]
     for k in range(1, got.shape[0]):
         total = total + got[k]
-    three = [total[0:4, tile(t)] for t in range(TILES // 2)] + [total[4:8, tile(t)] for t in range(TILES // 2)]
-    three = lift_runs(three, 4)
-    four = lift_runs([total[t : t + 1, half:] for t in range(TILES)], 8)
+    three = lift_runs([total[:, tile(t)] for t in range(TILES)], 4)
+    four = [total[t : t + 1, WIDE:] for t in range(TILES // 2)]
+    four = lift_runs(four + [pltpu.roll(x, LANES - 4, 1) for x in four], 8)
     lane = lane_id((4, LANES))
     row = lax.broadcasted_iota(jnp.int32, (4, LANES), 0)
     for t in range(TILES):
@@ -574,32 +573,31 @@
     got = lax.all_to_all(pay, "gy", 0, 0, tiled=True)
 
     payload = f32(6, 8, cells)
-    one, two, pay_e, pay_o, third = call(
+    one, two, pay_e, pay_o, third, z3, z4 = call(
         along_y,
-        [tiled, f32(TILES, planes * rows // 2, LANES), payload, payload, f32(16, cells)],
-        [vmem(32, cells)],
+        [
+            tiled,
+            f32(TILES, planes * rows // 2, LANES),
+            payload,
+            payload,
+            f32(16, cells),
+            bf16(4 * nz, 6 * 16),
+            bf16(4 * nz, 6 * 32),
+        ],
+        [vmem(32, cells), sems(2)],
         cost=400 << 20,
-        input_output_aliases={0: 0},
-    )(x, got_e, got_o)
+        in_specs=[far, far, here, here, here],
+        input_output_aliases={2: 0},
+    )(*[stay(w) for w in weights_z(nz)], x, got_e, got_o)
     got_e, got_o = swap(pay_e, "gz", 0), swap(pay_o, "gz", 1)
-    pay = (nz, 8, cells // 2 + LANES)
+    pay = (nz, 4, cells + LANES)
     pay = call(
         thin_z,
         f32(*pay),
-        [
-            vmem(*pay),
-            pltpu.VMEM((4 * nz, 6 * 16), jnp.bfloat16),
-            pltpu.VMEM((4 * nz, 6 * 32), jnp.bfloat16),
-            vmem(16, cells),
-            vmem(4, cells),
-            vmem(16, cells),
-            vmem(32, cells),
-            sems(4),
-        ],
+        [vmem(*pay), vmem(16, cells), vmem(4, cells), vmem(16, cells), vmem(32, cells), sems(2)],
         cost=40 << 20,
-        in_specs=[far, far, here, here, here],
         out_specs=far,
-    )(*[stay(w) for w in weights_z(nz)], third, own, got)
+    )(z3, z4, third, own, got)
     got = lax.all_to_all(pay, "gz", 0, 0, tiled=True)
 
     base, fourth = call(

time: 42.7 us -> 41.7 us (0.977)
  waiting for transfers between devices: 12.3 us -> 11.6 us
    pallas_call x1, Pallas kernels: 2 us -> 1.22 us  [per_device(): call(thin_z, f32(*pay), [vmem(*pay), vmem(16, cells), vmem(4, cells), vme...]
where the time goes in v5:
time: 41.7 us; the launch traced here: 41.3 us
  starting transfers between devices  17.9 us (43%)
  Pallas kernels  11.7 us (28%)
  waiting for transfers between devices  11.6 us (28%)
    all_to_all x1, starting transfers between devices, per_device(): got = lax.all_to_all(pay, 'gy', 0, 0, tiled=True)  7.83 us
    all_to_all x1, starting transfers between devices, per_device(): got = lax.all_to_all(pay, 'gz', 0, 0, tiled=True)  7.05 us
    all_to_all x1, waiting for transfers between devices, per_device(): got = lax.all_to_all(pay, 'gz', 0, 0, tiled=True)  7.04 us
    all_to_all x1, waiting for transfers between devices, per_device(): got = lax.all_to_all(pay, 'gy', 0, 0, tiled=True)  4.57 us
    pallas_call x1, Pallas kernels, per_device(): call(along_x, [tiled, payload, payload, f32(planes * rows // 2, cells), b...  3.65 us
    ppermute x4, starting transfers between devices, swap(): return lax.ppermute(values, axis, pairs)  2.99 us
    pallas_call x1, Pallas kernels, per_device(): call(along_y, [tiled, f32(TILES, planes * rows // 2, LANES), payload, pay...  2.11 us
    pallas_call x1, Pallas kernels, per_device(): call(along_z, [f32(planes, rows, cells), f32(planes // 4, rows, cells)],...  1.8 us
  transfers between devices with their start and end apart: 6, of which 2 were waited for; matrix products, arithmetic and copies ran while one was open for 0% of the time, Pallas kernels for 17%

profile of v5, /device:TPU:0, one launch (start us, length us, event | category | flops | bytes accessed | tf_op | source)
XLA Modules:
  0.0 41.3 jit_solution(5289539999257534427)
XLA Ops:
  0.0 3.6 %shard_map.55 = (f32[8,256,128]{2,1,0:T(8,128)S(1)}, f32[3,16,1024]{2,1,0:T(8,128)S(1)}, f32[3,16,1024]{2,1,0:T(8,128)S(1)}, f32[128,1024]{1,0:T(8,128)S(1)}, bf...) custom-call(bf16[8,48,384]{2,1,0:T(8,128)(2,1)} %constant.8.clone.weights3, ...), custom_call_target="tpu_custom_call" | custom-call | flops 41943040 | bytes 4194304 | tf_op jit(solution)/shard_map/pallas_call | solution.py:557
  3.7 0.1 collective-permute-start
  3.7 0.7 %collective-permute-start.1 = (f32[3,16,1024]{2,1,0:T(8,128)S(1)}, f32[3,16,1024]{2,1,0:T(8,128)S(1)}, u32[]{:S(2)}, u32[]{:S(2)}) collective-permute-start(f32[3,16,1024]{2,1,0:T(8,128)S(1)} %get-tuple-element.24), channel_id=1, source_target_pairs={{1,2},{2,1},{3,4},{4,3},{5,6},{6,5},{9,10},{10,9},{11,12},{12,11},... | collective-permute-start | bytes 589832 | tf_op jit(solution)/shard_map/ppermute | solution.py:525
  4.4 1.8 %shard_map.57 = (f32[16,1024]{1,0:T(8,128)S(1)}, f32[8,8,1536]{2,1,0:T(8,128)}) custom-call(bf16[48,384]{1,0:T(8,128)(2,1)S(1)} %get-tuple-element.28.w3, bf16[32,192]{1,0:T(8,128)(2,1)S(1)} %get-tuple-element.29.w4, f32[128,1024]{1,0:T(8,128)S(1)} %get-tuple-element.30.e1), custom_call_target="tpu_custom_call" | custom-call | flops 419430400 | bytes 4194304 | tf_op jit(solution)/shard_map/pallas_call | solution.py:565
  6.2 7.8 %all-to-all-start = ((f32[8,8,1536]{2,1,0:T(8,128)}), f32[8,8,1536]{2,1,0:T(8,128)S(1)}, u32[]{:S(2)}, u32[]{:S(2)}) async-start(f32[8,8,1536]{2,1,0:T(8,128)} %get-tuple-element.32), calls=%async_computation | async-start | bytes 786432 | tf_op jit(solution)/shard_map/all_to_all | solution.py:573
  14.1 0.0 collective-permute-done.got_e
  14.1 0.0 collective-permute-done.1.got_o
  14.1 2.1 %shard_map.56 = (f32[8,256,128]{2,1,0:T(8,128)S(1)}, f32[8,128,128]{2,1,0:T(8,128)S(1)}, f32[6,8,1024]{2,1,0:T(8,128)S(1)}, f32[6,8,1024]{2,1,0:T(8,128)S(1)}, f...) custom-call(bf16[16,64,96]{2,1,0:T(8,128)(2,1)} %constant.10.clone.w, ...), custom_call_target="tpu_custom_call", output_to_operand_aliasing={{0}: (2, {})} | custom-call | flops 4194304000 | bytes 4194304 | tf_op jit(solution)/shard_map/pallas_call | solution.py:576
  16.2 1.6 %collective-permute-start.2 = (f32[6,8,1024]{2,1,0:T(8,128)S(1)}, f32[6,8,1024]{2,1,0:T(8,128)S(1)}, u32[]{:S(2)}, u32[]{:S(2)}) collective-permute-start(f32[6,8,1024]{2,1,0:T(8,128)S(1)} %get-tuple-element.35), channel_id=1, source_target_pairs={{0,8},{8,0},{16,24},{24,16},{32,40},{40,32},{48,56},{56,48},{64,72... | collective-permute-start | bytes 589832 | tf_op jit(solution)/shard_map/ppermute | solution.py:525
  17.8 0.7 %collective-permute-start.3 = (f32[6,8,1024]{2,1,0:T(8,128)S(1)}, f32[6,8,1024]{2,1,0:T(8,128)S(1)}, u32[]{:S(2)}, u32[]{:S(2)}) collective-permute-start(f32[6,8,1024]{2,1,0:T(8,128)S(1)} %get-tuple-element.36), channel_id=1, source_target_pairs={{8,16},{16,8},{24,32},{32,24},{40,48},{48,40},{56,64},{64,56},{72,... | collective-permute-start | bytes 589832 | tf_op jit(solution)/shard_map/ppermute | solution.py:525
  18.4 4.6 %all-to-all-done.got = f32[8,8,1536]{2,1,0:T(8,128)S(1)} async-done(((f32[8,8,1536]{2,1,0:T(8,128)}), f32[8,8,1536]{2,1,0:T(8,128)S(1)}, u32[]{:S(2)}, u32[]{:S(2)}) %all-to-all-start) | async-done | bytes 393248 | tf_op jit(solution)/shard_map/all_to_all | solution.py:573
  23.0 1.2 %shard_map.58 = f32[16,4,1152]{2,1,0:T(4,128)} custom-call(bf16[64,96]{1,0:T(8,128)(2,1)S(1)} %get-tuple-element.25.w3, bf16[64,192]{1,0:T(8,128)(2,1)S(1)} %get-tuple-element.26.w4, f32[16,1024]{1,0:T(8,128)S(1)} %get-tuple-element.27.cells, f32[16,1024]{1,0:T(8,128)S(1)} %get-tuple-element.31.own, f32[8,8,1536]{2,1,0:T(8,128)S(1)} %all-to-all-done.got), custom_call_target="tpu_custom_call" | custom-call | flops 419430400 | bytes 4194304 | tf_op jit(solution)/shard_map/pallas_call | solution.py:594
  24.2 7.0 %all-to-all-start.1 = ((f32[16,4,1152]{2,1,0:T(4,128)}), f32[16,4,1152]{2,1,0:T(4,128)S(1)}, u32[]{:S(2)}, u32[]{:S(2)}) async-start(f32[16,4,1152]{2,1,0:T(4,128)} %shard_map.58), calls=%async_computation.1 | async-start | bytes 589824 | tf_op jit(solution)/shard_map/all_to_all | solution.py:601
  31.3 0.0 collective-permute-done.2.got_e
  31.3 0.0 collective-permute-done.3.got_o
  31.3 1.8 %shard_map.59 = (f32[16,16,1024]{2,1,0:T(8,128)}, f32[4,16,1024]{2,1,0:T(8,128)S(1)}) custom-call(f32[8,256,128]{2,1,0:T(8,128)S(1)} %get-tuple-element.33.one, f32[8,128,128]{2,1,0:T(8,128)S(1)} %get-tuple-element.34.two, f32[6,8,1024]{2,1,0:T(8,128)S(1)} %collective-permute-done.2.got_e, f32[6,8,1024]{2,1,0:T(8,128)S(1)} %collective-permute-done.3.got_o), custom_call_target="tpu_custom_call" | custom-call | flops 4194304000 | bytes 4194304 | tf_op jit(solution)/shard_map/pallas_call | solution.py:603
  33.1 7.0 %all-to-all-done.1.got = f32[16,4,1152]{2,1,0:T(4,128)S(1)} async-done(((f32[16,4,1152]{2,1,0:T(4,128)}), f32[16,4,1152]{2,1,0:T(4,128)S(1)}, u32[]{:S(2)}, u32[]{:S(2)}) %all-to-all-start.1) | async-done | bytes 294944 | tf_op jit(solution)/shard_map/all_to_all | solution.py:601
  40.2 1.1 %shard_map.60 = f32[16,16,1024]{2,1,0:T(8,128)} custom-call(f32[16,4,1152]{2,1,0:T(4,128)S(1)} %all-to-all-done.1.got, f32[4,16,1024]{2,1,0:T(8,128)S(1)} %get-tuple-element.37.fourth, f32[16,16,1024]{2,1,0:T(8,128)} %get-tuple-element.38.base), custom_call_target="tpu_custom_call", output_to_operand_aliasing={{}: (2, {})} | custom-call | flops 41943040 | bytes 4194304 | tf_op jit(solution)/shard_map/pallas_call | solution.py:610
Async XLA Ops:
  3.7 10.4 %collective-permute-start = (f32[3,16,1024]{2,1,0:T(8,128)S(1)}, f32[3,16,1024]{2,1,0:T(8,128)S(1)}, u32[]{:S(2)}, u32[]{:S(2)}) collective-permute-start(f32[3,16,1024]{2,1,0:T(8,128)S(1)} %get-tuple-element.23), channel_id=1, source_target_pairs={{0,1},{1,0},{2,3},{3,2},{4,5},{5,4},{6,7},{7,6},{8,9},{9,8},{10,11... | collective-permute-start | bytes 589832 | tf_op jit(solution)/shard_map/ppermute | solution.py:525
  3.7 10.3 %collective-permute-start.1 = (f32[3,16,1024]{2,1,0:T(8,128)S(1)}, f32[3,16,1024]{2,1,0:T(8,128)S(1)}, u32[]{:S(2)}, u32[]{:S(2)}) collective-permute-start(f32[3,16,1024]{2,1,0:T(8,128)S(1)} %get-tuple-element.24), channel_id=1, source_target_pairs={{1,2},{2,1},{3,4},{4,3},{5,6},{6,5},{9,10},{10,9},{11,12},{12,11},... | collective-permute-start | bytes 589832 | tf_op jit(solution)/shard_map/ppermute | solution.py:525
  6.2 16.8 %all-to-all-start = ((f32[8,8,1536]{2,1,0:T(8,128)}), f32[8,8,1536]{2,1,0:T(8,128)S(1)}, u32[]{:S(2)}, u32[]{:S(2)}) async-start(f32[8,8,1536]{2,1,0:T(8,128)} %get-tuple-element.32), calls=%async_computation | async-start | bytes 786432 | tf_op jit(solution)/shard_map/all_to_all | solution.py:573
  16.2 15.1 %collective-permute-start.2 = (f32[6,8,1024]{2,1,0:T(8,128)S(1)}, f32[6,8,1024]{2,1,0:T(8,128)S(1)}, u32[]{:S(2)}, u32[]{:S(2)}) collective-permute-start(f32[6,8,1024]{2,1,0:T(8,128)S(1)} %get-tuple-element.35), channel_id=1, source_target_pairs={{0,8},{8,0},{16,24},{24,16},{32,40},{40,32},{48,56},{56,48},{64,72... | collective-permute-start | bytes 589832 | tf_op jit(solution)/shard_map/ppermute | solution.py:525
  17.8 13.5 %collective-permute-start.3 = (f32[6,8,1024]{2,1,0:T(8,128)S(1)}, f32[6,8,1024]{2,1,0:T(8,128)S(1)}, u32[]{:S(2)}, u32[]{:S(2)}) collective-permute-start(f32[6,8,1024]{2,1,0:T(8,128)S(1)} %get-tuple-element.36), channel_id=1, source_target_pairs={{8,16},{16,8},{24,32},{32,24},{40,48},{48,40},{56,64},{64,56},{72,... | collective-permute-start | bytes 589832 | tf_op jit(solution)/shard_map/ppermute | solution.py:525
  24.2 15.9 %all-to-all-start.1 = ((f32[16,4,1152]{2,1,0:T(4,128)}), f32[16,4,1152]{2,1,0:T(4,128)S(1)}, u32[]{:S(2)}, u32[]{:S(2)}) async-start(f32[16,4,1152]{2,1,0:T(4,128)} %shard_map.58), calls=%async_computation.1 | async-start | bytes 589824 | tf_op jit(solution)/shard_map/all_to_all | solution.py:601

commit v6 on v5

--- a/solution.py
+++ b/solution.py
@@ -197,19 +197,23 @@
         ref[at, tile(t)] = v
 
 
-def along_x(weights3, weights4, density, out, pay_e, pay_o, e1, w3, w4, x, sem):
-    me = lax.axis_index("gy")
+def along_x(
+    y3, y4, z3, z4, density, out, pay_e, pay_o, own, result, next3, next4, x, e1, e2, e3, w3, w4, pay, load_sem, sem
+):
+    me, mz = lax.axis_index("gy"), lax.axis_index("gz")
 
     def load(k):
         at = pl.ds(pl.multiple_of(k * 32, 32), 32)
-        return pltpu.make_async_copy(density.at[at], x.at[at], sem.at[k])
+        return pltpu.make_async_copy(density.at[at], x.at[at], load_sem.at[k])
 
     for k in range(4):
         load(k).start()
         load(k + 4).start()
     hints = [
-        pltpu.make_async_copy(weights3.at[me], w3, sem.at[8]),
-        pltpu.make_async_copy(weights4.at[me], w4, sem.at[9]),
+        pltpu.make_async_copy(y3.at[me], w3, sem.at[0]),
+        pltpu.make_async_copy(y4.at[me], w4, sem.at[1]),
+        pltpu.make_async_copy(z3.at[mz], next3, sem.at[2]),
+        pltpu.make_async_copy(z4.at[mz], next4, sem.at[3]),
     ]
     for hint in hints:
         hint.start()
@@ -232,6 +236,9 @@
             plane(4 * k + i)
 
     times(4, group)
+    for hint in hints:
+        hint.wait()
+
     flip = me % 2 == 1
     even = lane_id((8, LANES)) % 2 == 0
 
@@ -247,20 +254,17 @@
                 pay_e[c, pl.ds(half * 8, 8), lanes] = mix(flip, going_left[c], going_right[c])
                 pay_o[c, pl.ds(half * 8, 8), lanes] = mix(flip, going_right[c], going_left[c])
 
-    times(TILES, column, 4)
-    for hint in hints:
-        hint.wait()
-
-
-def thin_y(w3, w4, e1, own, result, pay, e2, e3, sem):
-    me = lax.axis_index("gy")
-
     def second(i):
         at = pl.multiple_of(i * 8, 8)
         s, _ = lift_two(tiles_of(e1, pl.ds(at, 8)), tiles_of(e1, pl.ds(at + 64, 8)), 2)
         put_tiles(e2, pl.ds(at, 8), s)
 
-    times(8, second, 8)
+    def both(i):
+        second(i)
+        column(i)
+
+    times(8, both, 4)
+
     def third(i):
         at = pl.multiple_of(i * 8, 8)
         s, _ = lift_two(tiles_of(e2, pl.ds(at, 8)), tiles_of(e2, pl.ds(at + 32, 8)), 4)
@@ -274,26 +278,14 @@
         right = mix(to == me + 1, three[16:24], three[24:32])
         left = mix(to == me - 1, three[32:40], three[40:48])
         pay[to, :, 0:WIDE] = mix(to > me, right, left)
-    parts = [pl.ds(0, WIDE), pl.ds(WIDE, WIDE // 2)]
-    sends = [pltpu.make_async_copy(pay.at[:, :, p], result.at[:, :, p], sem.at[k]) for k, p in enumerate(parts)]
-    sends[0].start()
-
-    for to in range(pay.shape[0]):
         pay[to, 0:4, WIDE:] = four[to * 4 : to * 4 + 4, : WIDE // 2]
         pay[to, 4:8, WIDE:] = four[to * 4 : to * 4 + 4, WIDE // 2 :]
-    sends[1].start()
-    for send in sends:
-        send.wait()
-
-
-def along_y(weights3, weights4, x, got_e, got_o, one, two, pay_e, pay_o, cells, w3, w4, thick, sem):
-    mz = lax.axis_index("gz")
-    hints = [
-        pltpu.make_async_copy(weights3.at[mz], w3, sem.at[0]),
-        pltpu.make_async_copy(weights4.at[mz], w4, sem.at[1]),
-    ]
-    for hint in hints:
-        hint.start()
+    send = pltpu.make_async_copy(pay, result, sem.at[4])
+    send.start()
+    send.wait()
+
+
+def along_y(x, got_e, got_o, one, two, pay_e, pay_o, cells, thick):
     me = lax.axis_index("gy")
     first, last, flip = me == 0, me == lax.axis_size("gy") - 1, me % 2 == 1
     even = lane_id((8, LANES)) % 2 == 0
@@ -317,7 +309,7 @@
                 two[t, pl.ds(half * 64 + y, 8, stride=8), :] = v
 
     times(TILES, column, TILES)
-    flip = mz % 2 == 1
+    flip = lax.axis_index("gz") % 2 == 1
 
     def stack(t):
         lanes = tile_lanes(t)
@@ -347,8 +339,6 @@
     for i in range(2):
         s, _ = lift_two(tiles_of(thick, pl.ds(8 * i, 8)), tiles_of(thick, pl.ds(16 + 8 * i, 8)), 2)
         put_tiles(cells, pl.ds(8 * i, 8), s)
-    for hint in hints:
-        hint.wait()
 
 
 def thin_z(w3, w4, cells, own, got, result, pay, beyond, held4, turned3, turned4, sem):
@@ -554,41 +544,35 @@
     tiled = f32(TILES, planes * rows, LANES)
 
     payload = f32(3, 16, cells)
-    x, pay_e, pay_o, e1, y3, y4 = call(
+    pay = (ny, 8, cells * 3 // 2)
+    x, pay_e, pay_o, own, pay, z3, z4 = call(
         along_x,
-        [tiled, payload, payload, f32(planes * rows // 2, cells), bf16(48, 6 * 64), bf16(4 * ny, 6 * 32)],
-        [vmem(planes * rows, cells), sems(10)],
-        in_specs=[far, far, far],
-    )(*[stay(w) for w in weights_y(ny)], stay(density.reshape(planes * rows, cells)))
+        [tiled, payload, payload, f32(16, cells), f32(*pay), bf16(4 * nz, 6 * 16), bf16(4 * nz, 6 * 32)],
+        [
+            vmem(planes * rows, cells),
+            vmem(128, cells),
+            vmem(64, cells),
+            vmem(32, cells),
+            pltpu.VMEM((48, 6 * 64), jnp.bfloat16),
+            pltpu.VMEM((4 * ny, 6 * 32), jnp.bfloat16),
+            vmem(*pay),
+            sems(8),
+            sems(5),
+        ],
+        in_specs=[far] * 5,
+        out_specs=[here, here, here, here, far, here, here],
+    )(*[stay(w) for w in weights_y(ny) + weights_z(nz)], stay(density.reshape(planes * rows, cells)))
     got_e, got_o = swap(pay_e, "gy", 0), swap(pay_o, "gy", 1)
-    pay = (ny, 8, cells * 3 // 2)
-    own, pay = call(
-        thin_y,
-        [f32(16, cells), f32(*pay)],
-        [vmem(*pay), vmem(64, cells), vmem(32, cells), sems(2)],
-        cost=40 << 20,
-        in_specs=[here, here, here],
-        out_specs=[here, far],
-    )(y3, y4, e1)
     got = lax.all_to_all(pay, "gy", 0, 0, tiled=True)
 
     payload = f32(6, 8, cells)
-    one, two, pay_e, pay_o, third, z3, z4 = call(
+    one, two, pay_e, pay_o, third = call(
         along_y,
-        [
-            tiled,
-            f32(TILES, planes * rows // 2, LANES),
-            payload,
-            payload,
-            f32(16, cells),
-            bf16(4 * nz, 6 * 16),
-            bf16(4 * nz, 6 * 32),
-        ],
-        [vmem(32, cells), sems(2)],
+        [tiled, f32(TILES, planes * rows // 2, LANES), payload, payload, f32(16, cells)],
+        [vmem(32, cells)],
         cost=400 << 20,
-        in_specs=[far, far, here, here, here],
-        input_output_aliases={2: 0},
-    )(*[stay(w) for w in weights_z(nz)], x, got_e, got_o)
+        input_output_aliases={0: 0},
+    )(x, got_e, got_o)
     got_e, got_o = swap(pay_e, "gz", 0), swap(pay_o, "gz", 1)
     pay = (nz, 4, cells + LANES)
     pay = call(

time: 41.7 us -> 41.4 us (level)
  Pallas kernels: 11.7 us -> 11.2 us
    pallas_call x2 -> x1, Pallas kernels: 5.44 us -> 5.28 us  [per_device(): call(along_x, [tiled, payload, payload, f32(16, cells), f32(*pay), bf16(4...]
  transfers between devices with their start and end apart: 6 -> 6, of which waited for: 2 -> 2; matrix products, arithmetic and copies ran while one was open for 0% -> 0% of each run, Pallas kernels for 17% -> 12%
where the time goes in v6:
time: 41.4 us; the launch traced here: 41.1 us
  starting transfers between devices  17.9 us (43%)
  waiting for transfers between devices  12 us (29%)
  Pallas kernels  11.2 us (27%)
    all_to_all x1, starting transfers between devices, per_device(): got = lax.all_to_all(pay, 'gy', 0, 0, tiled=True)  7.83 us
    all_to_all x1, starting transfers between devices, per_device(): got = lax.all_to_all(pay, 'gz', 0, 0, tiled=True)  7.05 us
    all_to_all x1, waiting for transfers between devices, per_device(): got = lax.all_to_all(pay, 'gz', 0, 0, tiled=True)  7.04 us
    pallas_call x1, Pallas kernels, per_device(): call(along_x, [tiled, payload, payload, f32(16, cells), f32(*pay), bf16(4...  5.28 us
    all_to_all x1, waiting for transfers between devices, per_device(): got = lax.all_to_all(pay, 'gy', 0, 0, tiled=True)  4.94 us
    ppermute x4, starting transfers between devices, swap(): return lax.ppermute(values, axis, pairs)  2.99 us
    pallas_call x1, Pallas kernels, per_device(): call(along_z, [f32(planes, rows, cells), f32(planes // 4, rows, cells)],...  1.8 us
    pallas_call x1, Pallas kernels, per_device(): call(along_y, [tiled, f32(TILES, planes * rows // 2, LANES), payload, pay...  1.74 us
  transfers between devices with their start and end apart: 6, of which 2 were waited for; matrix products, arithmetic and copies ran while one was open for 0% of the time, Pallas kernels for 12%

profile of v6, /device:TPU:0, one launch (start us, length us, event | category | flops | bytes accessed | tf_op | source)
XLA Modules:
  0.0 41.1 jit_solution(7636943557725956076)
XLA Ops:
  0.0 5.3 %shard_map.55 = (f32[8,256,128]{2,1,0:T(8,128)S(1)}, f32[3,16,1024]{2,1,0:T(8,128)S(1)}, f32[3,16,1024]{2,1,0:T(8,128)S(1)}, f32[16,1024]{1,0:T(8,128)S(1)}, f32...) custom-call(bf16[8,48,384]{2,1,0:T(8,128)(2,1)} %constant.8.clone.y3, ...), custom_call_target="tpu_custom_call" | custom-call | flops 41943040 | bytes 4194304 | tf_op jit(solution)/shard_map/pallas_call | solution.py:548
  5.3 0.1 collective-permute-start
  5.4 0.7 %collective-permute-start.1 = (f32[3,16,1024]{2,1,0:T(8,128)S(1)}, f32[3,16,1024]{2,1,0:T(8,128)S(1)}, u32[]{:S(2)}, u32[]{:S(2)}) collective-permute-start(f32[3,16,1024]{2,1,0:T(8,128)S(1)} %get-tuple-element.23), channel_id=1, source_target_pairs={{1,2},{2,1},{3,4},{4,3},{5,6},{6,5},{9,10},{10,9},{11,12},{12,11},... | collective-permute-start | bytes 589832 | tf_op jit(solution)/shard_map/ppermute | solution.py:515
  6.1 7.8 %all-to-all-start = ((f32[8,8,1536]{2,1,0:T(8,128)}), f32[8,8,1536]{2,1,0:T(8,128)S(1)}, u32[]{:S(2)}, u32[]{:S(2)}) async-start(f32[8,8,1536]{2,1,0:T(8,128)} %get-tuple-element.26), calls=%async_computation | async-start | bytes 786432 | tf_op jit(solution)/shard_map/all_to_all | solution.py:566
  13.9 0.0 collective-permute-done.got_e
  13.9 0.0 collective-permute-done.1.got_o
  13.9 1.7 %shard_map.56 = (f32[8,256,128]{2,1,0:T(8,128)S(1)}, f32[8,128,128]{2,1,0:T(8,128)S(1)}, f32[6,8,1024]{2,1,0:T(8,128)S(1)}, f32[6,8,1024]{2,1,0:T(8,128)S(1)}, f32[16,1024]{1,0:T(8,128)S(1)}) custom-call(f32[8,256,128]{2,1,0:T(8,128)S(1)} %get-tuple-element.21.x, f32[3,16,1024]{2,1,0:T(8,128)S(1)} %collective-permute-done.got_e, ...), custom_call_target="tpu_custom_call", output_to_operand_aliasing={{0}: (0, {})} | custom-call | flops 4194304000 | bytes 4194304 | tf_op jit(solution)/shard_map/pallas_call | solution.py:569
  15.7 1.6 %collective-permute-start.2 = (f32[6,8,1024]{2,1,0:T(8,128)S(1)}, f32[6,8,1024]{2,1,0:T(8,128)S(1)}, u32[]{:S(2)}, u32[]{:S(2)}) collective-permute-start(f32[6,8,1024]{2,1,0:T(8,128)S(1)} %get-tuple-element.29), channel_id=1, source_target_pairs={{0,8},{8,0},{16,24},{24,16},{32,40},{40,32},{48,56},{56,48},{64,72... | collective-permute-start | bytes 589832 | tf_op jit(solution)/shard_map/ppermute | solution.py:515
  17.2 0.7 %collective-permute-start.3 = (f32[6,8,1024]{2,1,0:T(8,128)S(1)}, f32[6,8,1024]{2,1,0:T(8,128)S(1)}, u32[]{:S(2)}, u32[]{:S(2)}) collective-permute-start(f32[6,8,1024]{2,1,0:T(8,128)S(1)} %get-tuple-element.30), channel_id=1, source_target_pairs={{8,16},{16,8},{24,32},{32,24},{40,48},{48,40},{56,64},{64,56},{72,... | collective-permute-start | bytes 589832 | tf_op jit(solution)/shard_map/ppermute | solution.py:515
  17.9 4.9 %all-to-all-done.got = f32[8,8,1536]{2,1,0:T(8,128)S(1)} async-done(((f32[8,8,1536]{2,1,0:T(8,128)}), f32[8,8,1536]{2,1,0:T(8,128)S(1)}, u32[]{:S(2)}, u32[]{:S(2)}) %all-to-all-start) | async-done | bytes 393248 | tf_op jit(solution)/shard_map/all_to_all | solution.py:566
  22.8 1.2 %shard_map.57 = f32[16,4,1152]{2,1,0:T(4,128)} custom-call(bf16[64,96]{1,0:T(8,128)(2,1)S(1)} %get-tuple-element.19.w3, bf16[64,192]{1,0:T(8,128)(2,1)S(1)} %get-tuple-element.20.w4, f32[16,1024]{1,0:T(8,128)S(1)} %get-tuple-element.24.cells, f32[16,1024]{1,0:T(8,128)S(1)} %get-tuple-element.25.own, f32[8,8,1536]{2,1,0:T(8,128)S(1)} %all-to-all-done.got), custom_call_target="tpu_custom_call" | custom-call | flops 419430400 | bytes 4194304 | tf_op jit(solution)/shard_map/pallas_call | solution.py:578
  24.1 7.0 %all-to-all-start.1 = ((f32[16,4,1152]{2,1,0:T(4,128)}), f32[16,4,1152]{2,1,0:T(4,128)S(1)}, u32[]{:S(2)}, u32[]{:S(2)}) async-start(f32[16,4,1152]{2,1,0:T(4,128)} %shard_map.57), calls=%async_computation.1 | async-start | bytes 589824 | tf_op jit(solution)/shard_map/all_to_all | solution.py:585
  31.1 0.0 collective-permute-done.2.got_e
  31.1 0.0 collective-permute-done.3.got_o
  31.1 1.8 %shard_map.58 = (f32[16,16,1024]{2,1,0:T(8,128)}, f32[4,16,1024]{2,1,0:T(8,128)S(1)}) custom-call(f32[8,256,128]{2,1,0:T(8,128)S(1)} %get-tuple-element.27.one, f32[8,128,128]{2,1,0:T(8,128)S(1)} %get-tuple-element.28.two, f32[6,8,1024]{2,1,0:T(8,128)S(1)} %collective-permute-done.2.got_e, f32[6,8,1024]{2,1,0:T(8,128)S(1)} %collective-permute-done.3.got_o), custom_call_target="tpu_custom_call" | custom-call | flops 4194304000 | bytes 4194304 | tf_op jit(solution)/shard_map/pallas_call | solution.py:587
  32.9 7.0 %all-to-all-done.1.got = f32[16,4,1152]{2,1,0:T(4,128)S(1)} async-done(((f32[16,4,1152]{2,1,0:T(4,128)}), f32[16,4,1152]{2,1,0:T(4,128)S(1)}, u32[]{:S(2)}, u32[]{:S(2)}) %all-to-all-start.1) | async-done | bytes 294944 | tf_op jit(solution)/shard_map/all_to_all | solution.py:585
  40.0 1.1 %shard_map.59 = f32[16,16,1024]{2,1,0:T(8,128)} custom-call(f32[16,4,1152]{2,1,0:T(4,128)S(1)} %all-to-all-done.1.got, f32[4,16,1024]{2,1,0:T(8,128)S(1)} %get-tuple-element.31.fourth, f32[16,16,1024]{2,1,0:T(8,128)} %get-tuple-element.32.base), custom_call_target="tpu_custom_call", output_to_operand_aliasing={{}: (2, {})} | custom-call | flops 41943040 | bytes 4194304 | tf_op jit(solution)/shard_map/pallas_call | solution.py:594
Async XLA Ops:
  5.3 8.6 %collective-permute-start = (f32[3,16,1024]{2,1,0:T(8,128)S(1)}, f32[3,16,1024]{2,1,0:T(8,128)S(1)}, u32[]{:S(2)}, u32[]{:S(2)}) collective-permute-start(f32[3,16,1024]{2,1,0:T(8,128)S(1)} %get-tuple-element.22), channel_id=1, source_target_pairs={{0,1},{1,0},{2,3},{3,2},{4,5},{5,4},{6,7},{7,6},{8,9},{9,8},{10,11... | collective-permute-start | bytes 589832 | tf_op jit(solution)/shard_map/ppermute | solution.py:515
  5.4 8.5 %collective-permute-start.1 = (f32[3,16,1024]{2,1,0:T(8,128)S(1)}, f32[3,16,1024]{2,1,0:T(8,128)S(1)}, u32[]{:S(2)}, u32[]{:S(2)}) collective-permute-start(f32[3,16,1024]{2,1,0:T(8,128)S(1)} %get-tuple-element.23), channel_id=1, source_target_pairs={{1,2},{2,1},{3,4},{4,3},{5,6},{6,5},{9,10},{10,9},{11,12},{12,11},... | collective-permute-start | bytes 589832 | tf_op jit(solution)/shard_map/ppermute | solution.py:515
  6.1 16.8 %all-to-all-start = ((f32[8,8,1536]{2,1,0:T(8,128)}), f32[8,8,1536]{2,1,0:T(8,128)S(1)}, u32[]{:S(2)}, u32[]{:S(2)}) async-start(f32[8,8,1536]{2,1,0:T(8,128)} %get-tuple-element.26), calls=%async_computation | async-start | bytes 786432 | tf_op jit(solution)/shard_map/all_to_all | solution.py:566
  15.7 15.5 %collective-permute-start.2 = (f32[6,8,1024]{2,1,0:T(8,128)S(1)}, f32[6,8,1024]{2,1,0:T(8,128)S(1)}, u32[]{:S(2)}, u32[]{:S(2)}) collective-permute-start(f32[6,8,1024]{2,1,0:T(8,128)S(1)} %get-tuple-element.29), channel_id=1, source_target_pairs={{0,8},{8,0},{16,24},{24,16},{32,40},{40,32},{48,56},{56,48},{64,72... | collective-permute-start | bytes 589832 | tf_op jit(solution)/shard_map/ppermute | solution.py:515
  17.2 13.9 %collective-permute-start.3 = (f32[6,8,1024]{2,1,0:T(8,128)S(1)}, f32[6,8,1024]{2,1,0:T(8,128)S(1)}, u32[]{:S(2)}, u32[]{:S(2)}) collective-permute-start(f32[6,8,1024]{2,1,0:T(8,128)S(1)} %get-tuple-element.30), channel_id=1, source_target_pairs={{8,16},{16,8},{24,32},{32,24},{40,48},{48,40},{56,64},{64,56},{72,... | collective-permute-start | bytes 589832 | tf_op jit(solution)/shard_map/ppermute | solution.py:515
  24.1 15.9 %all-to-all-start.1 = ((f32[16,4,1152]{2,1,0:T(4,128)}), f32[16,4,1152]{2,1,0:T(4,128)S(1)}, u32[]{:S(2)}, u32[]{:S(2)}) async-start(f32[16,4,1152]{2,1,0:T(4,128)} %shard_map.57), calls=%async_computation.1 | async-start | bytes 589824 | tf_op jit(solution)/shard_map/all_to_all | solution.py:585

commit v7 on v6

--- a/solution.py
+++ b/solution.py
@@ -129,12 +129,40 @@
     return lax.broadcasted_iota(jnp.int32, shape, len(shape) - 1)
 
 
-def pack_two(a, b, even):
-    return jnp.where(even, a, pltpu.roll(b, 1, 1))
-
-
-def unpack_two(w):
-    return w, pltpu.roll(w, LANES - 1, 1)
+def in_even(shape):
+    return lane_id(shape) % 2 == 0
+
+
+def back(v):
+    return pltpu.roll(v, LANES - 1, 1)
+
+
+def on(v):
+    return pltpu.roll(v, 1, 1)
+
+
+def pack_right(p, q):
+    return jnp.where(in_even(p.shape), back(q), p)
+
+
+def unpack_right(v):
+    return back(v), v
+
+
+def pack_left(s, r):
+    return jnp.where(in_even(s.shape), s, on(r))
+
+
+def unpack_left(v):
+    return on(v), v
+
+
+def beyond_halves(left, right, to_right, to_left):
+    even = in_even(to_right[0].shape)
+    return (
+        tuple(jnp.where(even, x, on(y)) for x, y in zip(left, to_right)),
+        tuple(jnp.where(even, back(y), x) for x, y in zip(right, to_left)),
+    )
 
 
 def tile(t):
@@ -198,7 +226,7 @@
 
 
 def along_x(
-    y3, y4, z3, z4, density, out, pay_e, pay_o, own, result, next3, next4, x, e1, e2, e3, w3, w4, pay, load_sem, sem
+    y3, y4, z3, z4, density, smooth, detail, pay_e, pay_o, own, result, next3, next4, x, e2, e3, w3, w4, pay, load_sem, sem
 ):
     me, mz = lax.axis_index("gy"), lax.axis_index("gz")
 
@@ -223,11 +251,9 @@
         at = pl.multiple_of(z * 16 + y * 8, 8)
         far = pl.multiple_of(z * 16 + y * 8 + 128, 8)
         s, d = lift_two(tiles_of(x, pl.ds(at, 8)), tiles_of(x, pl.ds(far, 8)), 1)
-        put_tiles(e1, pl.ds(at, 8), s)
-        a, b = separate(s, d, 1)
         for t in range(TILES):
-            out[t, pl.ds(at, 8), :] = a[t]
-            out[t, pl.ds(far, 8), :] = b[t]
+            smooth[t, pl.ds(at, 8), :] = s[t]
+            detail[t, pl.ds(at, 8), :] = d[t]
 
     def group(k):
         load(k).wait()
@@ -239,31 +265,13 @@
     for hint in hints:
         hint.wait()
 
-    flip = me % 2 == 1
-    even = lane_id((8, LANES)) % 2 == 0
-
-    def column(t):
-        lanes = tile_lanes(t)
-        for half in range(2):
-            rows = [out[t, pl.ds(half * 128 + y, 8, stride=16), :] for y in range(16)]
-            to_right, to_left = edges(rows)
-            next_right, next_left = edges(lift_alone(rows))
-            going_right = to_right + (pack_two(*next_right, even),)
-            going_left = to_left + (pack_two(*next_left, even),)
-            for c in range(3):
-                pay_e[c, pl.ds(half * 8, 8), lanes] = mix(flip, going_left[c], going_right[c])
-                pay_o[c, pl.ds(half * 8, 8), lanes] = mix(flip, going_right[c], going_left[c])
-
     def second(i):
         at = pl.multiple_of(i * 8, 8)
-        s, _ = lift_two(tiles_of(e1, pl.ds(at, 8)), tiles_of(e1, pl.ds(at + 64, 8)), 2)
+        near, far = [[smooth[t, pl.ds(at + k, 8), :] for t in range(TILES)] for k in (0, 64)]
+        s, _ = lift_two(near, far, 2)
         put_tiles(e2, pl.ds(at, 8), s)
 
-    def both(i):
-        second(i)
-        column(i)
-
-    times(8, both, 4)
+    times(8, second, 8)
 
     def third(i):
         at = pl.multiple_of(i * 8, 8)
@@ -282,60 +290,72 @@
         pay[to, 4:8, WIDE:] = four[to * 4 : to * 4 + 4, WIDE // 2 :]
     send = pltpu.make_async_copy(pay, result, sem.at[4])
     send.start()
+    flip = me % 2 == 1
+
+    def column(t):
+        lanes = tile_lanes(t)
+        rows = [smooth[t, pl.ds(y, 8, stride=16), :] for y in range(16)]
+        parts = [edges(rows), edges(lift_alone(rows))]
+        parts.append(edges([detail[t, pl.ds(y, 8, stride=16), :] for y in range(16)]))
+        for c in range(6):
+            right, left = [parts[c // 2][side][c % 2] for side in range(2)]
+            pay_e[c, :, lanes] = mix(flip, left, right)
+            pay_o[c, :, lanes] = mix(flip, right, left)
+
+    times(TILES, column, 4)
     send.wait()
 
 
-def along_y(x, got_e, got_o, one, two, pay_e, pay_o, cells, thick):
+def along_y(smooth, detail, got_e, got_o, one_s, one_d, two, pay_e, pay_o, cells, thick):
     me = lax.axis_index("gy")
     first, last, flip = me == 0, me == lax.axis_size("gy") - 1, me % 2 == 1
-    even = lane_id((8, LANES)) % 2 == 0
 
     def column(t):
         lanes = tile_lanes(t)
-        for half in range(2):
-            rows = [x[t, pl.ds(half * 128 + y, 8, stride=16), :] for y in range(16)]
-            e = [got_e[c, pl.ds(half * 8, 8), lanes] for c in range(3)]
-            o = [got_o[c, pl.ds(half * 8, 8), lanes] for c in range(3)]
-            left = [mix(flip, e[c], o[c]) for c in range(3)]
-            right = [mix(flip, o[c], e[c]) for c in range(3)]
-            to_right, to_left = edges(rows)
-            smooth, detail = lift(rows, left[:2], right[:2], first, last, mix)
-            for y, v in enumerate(interleave(smooth, detail)):
-                one[t, pl.ds(half * 128 + y, 8, stride=16), :] = v
-            left2 = add_pairs(unpack_two(left[2]), own_left(to_left))
-            right2 = add_pairs(unpack_two(right[2]), own_right(to_right))
-            smooth, detail = lift(smooth, left2, right2, first, last, mix)
-            for y, v in enumerate(interleave(smooth, detail)):
-                two[t, pl.ds(half * 64 + y, 8, stride=8), :] = v
+        e = [got_e[c, :, lanes] for c in range(6)]
+        o = [got_o[c, :, lanes] for c in range(6)]
+        left = [mix(flip, e[c], o[c]) for c in range(6)]
+        right = [mix(flip, o[c], e[c]) for c in range(6)]
+        for k, (source, to) in enumerate(((detail, one_d), (smooth, one_s))):
+            rows = [source[t, pl.ds(y, 8, stride=16), :] for y in range(16)]
+            at = slice(0, 2) if k else slice(4, 6)
+            low, high = lift(rows, left[at], right[at], first, last, mix)
+            for y, v in enumerate(interleave(low, high)):
+                to[t, pl.ds(y, 8, stride=16), :] = v
+        to_right, to_left = edges(rows)
+        left2, right2 = add_pairs(left[2:4], own_left(to_left)), add_pairs(right[2:4], own_right(to_right))
+        low, high = lift(low, left2, right2, first, last, mix)
+        for y, v in enumerate(interleave(low, high)):
+            two[t, pl.ds(y, 8, stride=8), :] = v
+        for r, v in enumerate(low):
+            thick[pl.ds(4 * r, 4), lanes] = v[0:4]
+            thick[pl.ds(16 + 4 * r, 4), lanes] = v[4:8]
 
     times(TILES, column, TILES)
     flip = lax.axis_index("gz") % 2 == 1
 
     def stack(t):
         lanes = tile_lanes(t)
-        going_right, going_left = [None] * 6, [None] * 6
-        for half in range(2):
-            rows = [one[t, pl.ds(z * 16 + half * 8, 8), :] for z in range(16)]
+        going_right, going_left = [], []
+
+        def add(rows):
             to_right, to_left = edges(rows)
-            for c in range(2):
-                going_right[2 * c + half] = to_right[c]
-                going_left[2 * c + half] = to_left[c]
-        rows = [two[t, pl.ds(z * 8, 8), :] for z in range(16)]
-        to_right, to_left = edges(rows)
-        next_right, next_left = edges(lift_alone(rows))
-        going_right[4:] = pack_two(*to_right, even), pack_two(*next_right, even)
-        going_left[4:] = pack_two(*to_left, even), pack_two(*next_left, even)
+            going_right.append(pack_right(*to_right))
+            going_left.append(pack_left(*to_left))
+            return to_right, to_left
+
+        for source in (one_s, one_d):
+            for half in range(2):
+                add([source[t, pl.ds(z * 16 + half * 8, 8), :] for z in range(8)])
+        rows = [two[t, pl.ds(z * 8, 8), :] for z in range(8)]
+        nothing = jnp.zeros_like(rows[0])
+        left, right = beyond_halves((nothing, nothing), (nothing, nothing), *add(rows))
+        add(lift(rows, left, right, False, False, lambda c, a, b: b)[0])
         for c in range(6):
             pay_e[c, :, lanes] = mix(flip, going_left[c], going_right[c])
             pay_o[c, :, lanes] = mix(flip, going_right[c], going_left[c])
 
     times(TILES, stack, TILES)
-    for t in range(TILES):
-        for r in range(4):
-            low, high = [two[t, pl.ds(64 * half + 2 * r, 8, stride=8), :] for half in range(2)]
-            v = pack_two(low, high, even)
-            thick[pl.ds(4 * r, 4), tile(t)] = v[0:4]
-            thick[pl.ds(16 + 4 * r, 4), tile(t)] = v[4:8]
     for i in range(2):
         s, _ = lift_two(tiles_of(thick, pl.ds(8 * i, 8)), tiles_of(thick, pl.ds(16 + 8 * i, 8)), 2)
         put_tiles(cells, pl.ds(8 * i, 8), s)
@@ -387,28 +407,34 @@
         send.wait()
 
 
-def along_z(one, two, got_e, got_o, result, fourth, out, fine, spread, sem):
+def along_z(one_s, one_d, two, got_e, got_o, result, fourth, out, fine, spread, sem):
     me = lax.axis_index("gz")
-    first, last, flip = me == 0, me == lax.axis_size("gz") - 1, me % 2 == 1
+    flip, side = me % 2 == 1, lane_id((8, LANES)) % 2
+    first = side == jnp.where(me == 0, 0, 2)
+    last = side == jnp.where(me == lax.axis_size("gz") - 1, 1, 2)
 
     def stack(t):
         lanes = tile_lanes(t)
         e = [got_e[c, :, lanes] for c in range(6)]
         o = [got_o[c, :, lanes] for c in range(6)]
-        left = [mix(flip, e[c], o[c]) for c in range(6)]
-        right = [mix(flip, o[c], e[c]) for c in range(6)]
+        left = [unpack_right(mix(flip, e[c], o[c])) for c in range(6)]
+        right = [unpack_left(mix(flip, o[c], e[c])) for c in range(6)]
         for half in range(2):
-            rows = [one[t, pl.ds(z * 16 + half * 8, 8), :] for z in range(16)]
-            smooth, detail = lift(rows, left[half:4:2], right[half:4:2], first, last, mix)
-            for z, v in enumerate(interleave(smooth, detail)):
-                out[z, pl.ds(half * 8, 8), lanes] = v
-        rows = [two[t, pl.ds(z * 8, 8), :] for z in range(16)]
+            lifted = []
+            for k, source in enumerate((one_s, one_d)):
+                rows = [source[t, pl.ds(z * 16 + half * 8, 8), :] for z in range(8)]
+                ends = beyond_halves(left[2 * k + half], right[2 * k + half], *edges(rows))
+                lifted.append(interleave(*lift(rows, *ends, first, last, mix)))
+            near, far = separate(*lifted, 1)
+            for z in range(8):
+                out[z, pl.ds(half * 8, 8), lanes] = near[z]
+                out[z + 8, pl.ds(half * 8, 8), lanes] = far[z]
+        rows = [two[t, pl.ds(z * 8, 8), :] for z in range(8)]
         to_right, to_left = edges(rows)
-        smooth, _ = lift(rows, unpack_two(left[4]), unpack_two(right[4]), first, last, mix)
-        left2 = add_pairs(unpack_two(left[5]), own_left(to_left))
-        right2 = add_pairs(unpack_two(right[5]), own_right(to_right))
-        smooth, detail = lift(smooth, left2, right2, first, last, mix)
-        for z, v in enumerate(interleave(smooth, detail)):
+        rows, _ = lift(rows, *beyond_halves(left[4], right[4], to_right, to_left), first, last, mix)
+        left2, right2 = add_pairs(left[5], own_left(to_left)), add_pairs(right[5], own_right(to_right))
+        ends = beyond_halves(left2, right2, *edges(rows))
+        for z, v in enumerate(interleave(*lift(rows, *ends, first, last, mix))):
             fine[pl.ds(z * 8, 8), lanes] = v
 
     times(TILES, stack, TILES)
@@ -416,18 +442,19 @@
     for z in range(1, 16, 2):
         sends[z].start()
     row = lax.broadcasted_iota(jnp.int32, (16, LANES), 0)
-    here = (row % 2 == 0) & (lane_id((16, LANES)) % 2 == 0)
-    for z in (1, 3, 5, 7, 0, 2, 4, 6):
-        v = lift_runs(tiles_of(fine, pl.ds(z * 8, 8)), 2)
-        for t in range(TILES):
-            spread[t, pl.ds(z * 16, 8, stride=2), :] = v[t]
-            w = jnp.where(here, spread[t, pl.ds(z * 16, 16), :], out[2 * z, :, tile(t)])
+    here = (row % 2 == 0) & in_even((16, LANES))
+    for i in (1, 3, 0, 2):
+        v = lift_runs(tiles_of(fine, pl.ds(i * 8, 8)), 2)
+        for z in (i, i + 4):
+            for t in range(TILES):
+                spread[t, pl.ds(z * 16, 8, stride=2), :] = v[t] if z == i else back(v[t])
+                w = jnp.where(here, spread[t, pl.ds(z * 16, 16), :], out[2 * z, :, tile(t)])
+                if z % 2:
+                    out[2 * z, :, tile(t)] = w
+                else:
+                    fourth[z // 2, :, tile(t)] = w
             if z % 2:
-                out[2 * z, :, tile(t)] = w
-            else:
-                fourth[z // 2, :, tile(t)] = w
-        if z % 2:
-            sends[2 * z].start()
+                sends[2 * z].start()
     for send in sends.values():
         send.wait()
 
@@ -541,16 +568,14 @@
     sems = lambda count: pltpu.SemaphoreType.DMA((count,))
     far, here = pl.BlockSpec(memory_space=pltpu.HBM), pl.BlockSpec(memory_space=pltpu.VMEM)
     stay = lambda v: pltpu.with_memory_space_constraint(jnp.asarray(v), pltpu.HBM)
-    tiled = f32(TILES, planes * rows, LANES)
-
-    payload = f32(3, 16, cells)
+    tiled = f32(TILES, planes * rows // 2, LANES)
+    payload = f32(6, 8, cells)
     pay = (ny, 8, cells * 3 // 2)
-    x, pay_e, pay_o, own, pay, z3, z4 = call(
+    smooth, detail, pay_e, pay_o, own, pay, z3, z4 = call(
         along_x,
-        [tiled, payload, payload, f32(16, cells), f32(*pay), bf16(4 * nz, 6 * 16), bf16(4 * nz, 6 * 32)],
+        [tiled, tiled, payload, payload, f32(16, cells), f32(*pay), bf16(4 * nz, 6 * 16), bf16(4 * nz, 6 * 32)],
         [
             vmem(planes * rows, cells),
-            vmem(128, cells),
             vmem(64, cells),
             vmem(32, cells),
             pltpu.VMEM((48, 6 * 64), jnp.bfloat16),
@@ -560,19 +585,18 @@
             sems(5),
         ],
         in_specs=[far] * 5,
-        out_specs=[here, here, here, here, far, here, here],
+        out_specs=[here] * 5 + [far, here, here],
     )(*[stay(w) for w in weights_y(ny) + weights_z(nz)], stay(density.reshape(planes * rows, cells)))
     got_e, got_o = swap(pay_e, "gy", 0), swap(pay_o, "gy", 1)
     got = lax.all_to_all(pay, "gy", 0, 0, tiled=True)
 
-    payload = f32(6, 8, cells)
-    one, two, pay_e, pay_o, third = call(
+    one_s, one_d, two, pay_e, pay_o, third = call(
         along_y,
-        [tiled, f32(TILES, planes * rows // 2, LANES), payload, payload, f32(16, cells)],
+        [tiled, tiled, f32(TILES, planes * rows // 4, LANES), payload, payload, f32(16, cells)],
         [vmem(32, cells)],
         cost=400 << 20,
-        input_output_aliases={0: 0},
-    )(x, got_e, got_o)
+        input_output_aliases={0: 0, 1: 1},
+    )(smooth, detail, got_e, got_o)
     got_e, got_o = swap(pay_e, "gz", 0), swap(pay_o, "gz", 1)
     pay = (nz, 4, cells + LANES)
     pay = call(
@@ -587,10 +611,10 @@
     base, fourth = call(
         along_z,
         [f32(planes, rows, cells), f32(planes // 4, rows, cells)],
-        [vmem(planes, rows, cells), vmem(64, cells), vmem(TILES, 128, LANES), sems(planes)],
+        [vmem(planes, rows, cells), vmem(32, cells), vmem(TILES, 128, LANES), sems(planes)],
         cost=400 << 20,
         out_specs=[far, here],
-    )(one, two, got_e, got_o)
+    )(one_s, one_d, two, got_e, got_o)
     return call(
         join,
         f32(planes, rows, cells),

time: 41.4 us -> 40.8 us (0.986)
  waiting for transfers between devices: 12 us -> 10.8 us
  Pallas kernels: 11.2 us -> 11.7 us
    pallas_call x1, Pallas kernels: 1.8 us -> 3.44 us  [per_device(): call(along_z, [f32(planes, rows, cells), f32(planes // 4, rows, cells)],...]
    all_to_all x1, waiting for transfers between devices: 7.04 us -> 5.4 us  [per_device(): got = lax.all_to_all(pay, 'gz', 0, 0, tiled=True)]
    pallas_call x2, Pallas kernels: 7.02 us -> 5.91 us  [the longest x1 4.62 us: per_device(): call(along_x, [tiled, tiled, payload, payload, f32(16, cells), f32(*pay),...]
    all_to_all x1, waiting for transfers between devices: 4.94 us -> 5.4 us  [per_device(): got = lax.all_to_all(pay, 'gy', 0, 0, tiled=True)]
  transfers between devices with their start and end apart: 6 -> 6, of which waited for: 2 -> 2; matrix products, arithmetic and copies ran while one was open for 0% -> 0% of each run, Pallas kernels for 12% -> 15%
where the time goes in v7:
time: 40.8 us; the launch traced here: 40.5 us
  starting transfers between devices  17.9 us (44%)
  Pallas kernels  11.7 us (29%)
  waiting for transfers between devices  10.8 us (26%)
    all_to_all x1, starting transfers between devices, per_device(): got = lax.all_to_all(pay, 'gy', 0, 0, tiled=True)  7.83 us
    all_to_all x1, starting transfers between devices, per_device(): got = lax.all_to_all(pay, 'gz', 0, 0, tiled=True)  7.05 us
    all_to_all x1, waiting for transfers between devices, per_device(): got = lax.all_to_all(pay, 'gz', 0, 0, tiled=True)  5.4 us
    all_to_all x1, waiting for transfers between devices, per_device(): got = lax.all_to_all(pay, 'gy', 0, 0, tiled=True)  5.4 us
    pallas_call x1, Pallas kernels, per_device(): call(along_x, [tiled, tiled, payload, payload, f32(16, cells), f32(*pay),...  4.62 us
    pallas_call x1, Pallas kernels, per_device(): call(along_z, [f32(planes, rows, cells), f32(planes // 4, rows, cells)],...  3.44 us
    ppermute x4, starting transfers between devices, swap(): return lax.ppermute(values, axis, pairs)  2.99 us
    pallas_call x1, Pallas kernels, per_device(): call(along_y, [tiled, tiled, f32(TILES, planes * rows // 4, LANES), paylo...  1.28 us
  transfers between devices with their start and end apart: 6, of which 2 were waited for; matrix products, arithmetic and copies ran while one was open for 0% of the time, Pallas kernels for 15%

profile of v7, /device:TPU:0, one launch (start us, length us, event | category | flops | bytes accessed | tf_op | source)
XLA Modules:
  0.0 40.5 jit_solution(8168743983945444464)
XLA Ops:
  0.0 4.6 %shard_map.55 = (f32[8,128,128]{2,1,0:T(8,128)S(1)}, f32[8,128,128]{2,1,0:T(8,128)S(1)}, f32[6,8,1024]{2,1,0:T(8,128)S(1)}, f32[6,8,1024]{2,1,0:T(8,128)S(1)}, f...) custom-call(bf16[8,48,384]{2,1,0:T(8,128)(2,1)} %constant.8.clone.y3, ...), custom_call_target="tpu_custom_call" | custom-call | flops 41943040 | bytes 4194304 | tf_op jit(solution)/shard_map/pallas_call | solution.py:574
  4.6 0.1 collective-permute-start
  4.7 0.7 %collective-permute-start.1 = (f32[6,8,1024]{2,1,0:T(8,128)S(1)}, f32[6,8,1024]{2,1,0:T(8,128)S(1)}, u32[]{:S(2)}, u32[]{:S(2)}) collective-permute-start(f32[6,8,1024]{2,1,0:T(8,128)S(1)} %get-tuple-element.26), channel_id=1, source_target_pairs={{1,2},{2,1},{3,4},{4,3},{5,6},{6,5},{9,10},{10,9},{11,12},{12,11},... | collective-permute-start | bytes 589832 | tf_op jit(solution)/shard_map/ppermute | solution.py:542
  5.4 7.8 %all-to-all-start = ((f32[8,8,1536]{2,1,0:T(8,128)}), f32[8,8,1536]{2,1,0:T(8,128)S(1)}, u32[]{:S(2)}, u32[]{:S(2)}) async-start(f32[8,8,1536]{2,1,0:T(8,128)} %get-tuple-element.29), calls=%async_computation | async-start | bytes 786432 | tf_op jit(solution)/shard_map/all_to_all | solution.py:591
  13.2 0.0 collective-permute-done.got_e
  13.2 0.0 collective-permute-done.1.got_o
  13.2 1.3 %shard_map.56 = (f32[8,128,128]{2,1,0:T(8,128)S(1)}, f32[8,128,128]{2,1,0:T(8,128)S(1)}, f32[8,64,128]{2,1,0:T(8,128)S(1)}, f32[6,8,1024]{2,1,0:T(8,128)S(1)}, f...) custom-call(f32[8,128,128]{2,1,0:T(8,128)S(1)} %get-tuple-element.23.smooth, ...), custom_call_target="tpu_custom_call", output_to_operand_aliasing={{0}: (0, {}), {1}: (1, {})} | custom-call | flops 4194304000 | bytes 4194304 | tf_op jit(solution)/shard_map/pallas_call | solution.py:593
  14.5 1.6 %collective-permute-start.2 = (f32[6,8,1024]{2,1,0:T(8,128)S(1)}, f32[6,8,1024]{2,1,0:T(8,128)S(1)}, u32[]{:S(2)}, u32[]{:S(2)}) collective-permute-start(f32[6,8,1024]{2,1,0:T(8,128)S(1)} %get-tuple-element.33), channel_id=1, source_target_pairs={{0,8},{8,0},{16,24},{24,16},{32,40},{40,32},{48,56},{56,48},{64,72... | collective-permute-start | bytes 589832 | tf_op jit(solution)/shard_map/ppermute | solution.py:542
  16.1 0.7 %collective-permute-start.3 = (f32[6,8,1024]{2,1,0:T(8,128)S(1)}, f32[6,8,1024]{2,1,0:T(8,128)S(1)}, u32[]{:S(2)}, u32[]{:S(2)}) collective-permute-start(f32[6,8,1024]{2,1,0:T(8,128)S(1)} %get-tuple-element.34), channel_id=1, source_target_pairs={{8,16},{16,8},{24,32},{32,24},{40,48},{48,40},{56,64},{64,56},{72,... | collective-permute-start | bytes 589832 | tf_op jit(solution)/shard_map/ppermute | solution.py:542
  16.8 5.4 %all-to-all-done.got = f32[8,8,1536]{2,1,0:T(8,128)S(1)} async-done(((f32[8,8,1536]{2,1,0:T(8,128)}), f32[8,8,1536]{2,1,0:T(8,128)S(1)}, u32[]{:S(2)}, u32[]{:S(2)}) %all-to-all-start) | async-done | bytes 393248 | tf_op jit(solution)/shard_map/all_to_all | solution.py:591
  22.2 1.2 %shard_map.57 = f32[16,4,1152]{2,1,0:T(4,128)} custom-call(bf16[64,96]{1,0:T(8,128)(2,1)S(1)} %get-tuple-element.21.w3, bf16[64,192]{1,0:T(8,128)(2,1)S(1)} %get-tuple-element.22.w4, f32[16,1024]{1,0:T(8,128)S(1)} %get-tuple-element.27.cells, f32[16,1024]{1,0:T(8,128)S(1)} %get-tuple-element.28.own, f32[8,8,1536]{2,1,0:T(8,128)S(1)} %all-to-all-done.got), custom_call_target="tpu_custom_call" | custom-call | flops 419430400 | bytes 4194304 | tf_op jit(solution)/shard_map/pallas_call | solution.py:602
  23.4 7.0 %all-to-all-start.1 = ((f32[16,4,1152]{2,1,0:T(4,128)}), f32[16,4,1152]{2,1,0:T(4,128)S(1)}, u32[]{:S(2)}, u32[]{:S(2)}) async-start(f32[16,4,1152]{2,1,0:T(4,128)} %shard_map.57), calls=%async_computation.1 | async-start | bytes 589824 | tf_op jit(solution)/shard_map/all_to_all | solution.py:609
  30.5 0.0 collective-permute-done.2.got_e
  30.5 0.0 collective-permute-done.3.got_o
  30.5 3.4 %shard_map.58 = (f32[16,16,1024]{2,1,0:T(8,128)}, f32[4,16,1024]{2,1,0:T(8,128)S(1)}) custom-call(f32[8,128,128]{2,1,0:T(8,128)S(1)} %get-tuple-element.30.one_s, f32[8,128,128]{2,1,0:T(8,128)S(1)} %get-tuple-element.31.one_d, f32[8,64,128]{2,1,0:T(8,128)S(1)} %get-tuple-element.32.two, f32[6,8,1024]{2,1,0:T(8,128)S(1)} %collective-permute-done.2.got_e, ...), custom_call_target="tpu_custom_call" | custom-call | flops 4194304000 | bytes 4194304 | tf_op jit(solution)/shard_map/pallas_call | solution.py:611
  33.9 5.4 %all-to-all-done.1.got = f32[16,4,1152]{2,1,0:T(4,128)S(1)} async-done(((f32[16,4,1152]{2,1,0:T(4,128)}), f32[16,4,1152]{2,1,0:T(4,128)S(1)}, u32[]{:S(2)}, u32[]{:S(2)}) %all-to-all-start.1) | async-done | bytes 294944 | tf_op jit(solution)/shard_map/all_to_all | solution.py:609
  39.3 1.1 %shard_map.59 = f32[16,16,1024]{2,1,0:T(8,128)} custom-call(f32[16,4,1152]{2,1,0:T(4,128)S(1)} %all-to-all-done.1.got, f32[4,16,1024]{2,1,0:T(8,128)S(1)} %get-tuple-element.35.fourth, f32[16,16,1024]{2,1,0:T(8,128)} %get-tuple-element.36.base), custom_call_target="tpu_custom_call", output_to_operand_aliasing={{}: (2, {})} | custom-call | flops 41943040 | bytes 4194304 | tf_op jit(solution)/shard_map/pallas_call | solution.py:618
Async XLA Ops:
  4.6 8.6 %collective-permute-start = (f32[6,8,1024]{2,1,0:T(8,128)S(1)}, f32[6,8,1024]{2,1,0:T(8,128)S(1)}, u32[]{:S(2)}, u32[]{:S(2)}) collective-permute-start(f32[6,8,1024]{2,1,0:T(8,128)S(1)} %get-tuple-element.25), channel_id=1, source_target_pairs={{0,1},{1,0},{2,3},{3,2},{4,5},{5,4},{6,7},{7,6},{8,9},{9,8},{10,11... | collective-permute-start | bytes 589832 | tf_op jit(solution)/shard_map/ppermute | solution.py:542
  4.7 8.5 %collective-permute-start.1 = (f32[6,8,1024]{2,1,0:T(8,128)S(1)}, f32[6,8,1024]{2,1,0:T(8,128)S(1)}, u32[]{:S(2)}, u32[]{:S(2)}) collective-permute-start(f32[6,8,1024]{2,1,0:T(8,128)S(1)} %get-tuple-element.26), channel_id=1, source_target_pairs={{1,2},{2,1},{3,4},{4,3},{5,6},{6,5},{9,10},{10,9},{11,12},{12,11},... | collective-permute-start | bytes 589832 | tf_op jit(solution)/shard_map/ppermute | solution.py:542
  5.4 16.8 %all-to-all-start = ((f32[8,8,1536]{2,1,0:T(8,128)}), f32[8,8,1536]{2,1,0:T(8,128)S(1)}, u32[]{:S(2)}, u32[]{:S(2)}) async-start(f32[8,8,1536]{2,1,0:T(8,128)} %get-tuple-element.29), calls=%async_computation | async-start | bytes 786432 | tf_op jit(solution)/shard_map/all_to_all | solution.py:591
  14.5 15.9 %collective-permute-start.2 = (f32[6,8,1024]{2,1,0:T(8,128)S(1)}, f32[6,8,1024]{2,1,0:T(8,128)S(1)}, u32[]{:S(2)}, u32[]{:S(2)}) collective-permute-start(f32[6,8,1024]{2,1,0:T(8,128)S(1)} %get-tuple-element.33), channel_id=1, source_target_pairs={{0,8},{8,0},{16,24},{24,16},{32,40},{40,32},{48,56},{56,48},{64,72... | collective-permute-start | bytes 589832 | tf_op jit(solution)/shard_map/ppermute | solution.py:542
  16.1 14.4 %collective-permute-start.3 = (f32[6,8,1024]{2,1,0:T(8,128)S(1)}, f32[6,8,1024]{2,1,0:T(8,128)S(1)}, u32[]{:S(2)}, u32[]{:S(2)}) collective-permute-start(f32[6,8,1024]{2,1,0:T(8,128)S(1)} %get-tuple-element.34), channel_id=1, source_target_pairs={{8,16},{16,8},{24,32},{32,24},{40,48},{48,40},{56,64},{64,56},{72,... | collective-permute-start | bytes 589832 | tf_op jit(solution)/shard_map/ppermute | solution.py:542
  23.4 15.9 %all-to-all-start.1 = ((f32[16,4,1152]{2,1,0:T(4,128)}), f32[16,4,1152]{2,1,0:T(4,128)S(1)}, u32[]{:S(2)}, u32[]{:S(2)}) async-start(f32[16,4,1152]{2,1,0:T(4,128)} %shard_map.57), calls=%async_computation.1 | async-start | bytes 589824 | tf_op jit(solution)/shard_map/all_to_all | solution.py:609

commit v8 on v7

--- a/solution.py
+++ b/solution.py
@@ -190,8 +190,10 @@
     lane = lane_id((a[0].shape[0], LANES))
     here = lane % (2 * phase) < phase
     count, reach = len(a), 2 * phase
-    s = [jnp.where(here, x, pltpu.roll(y, phase, 1)) for x, y in zip(a, b)]
-    d = [jnp.where(here, pltpu.roll(x, LANES - phase, 1), y) for x, y in zip(a, b)]
+    other = jnp.where(here, lane + phase, lane - phase)
+    m = [jnp.take_along_axis(jnp.where(here, y, x), other, axis=1, mode="promise_in_bounds") for x, y in zip(a, b)]
+    s = [jnp.where(here, x, y) for x, y in zip(a, m)]
+    d = [jnp.where(here, y, x) for x, y in zip(b, m)]
 
     def ahead(x):
         r = [pltpu.roll(w, LANES - reach, 1) for w in x]
@@ -209,10 +211,11 @@
 
 
 def separate(s, d, phase):
-    here = lane_id(s[0].shape) % (2 * phase) < phase
-    a = [jnp.where(here, x, pltpu.roll(y, phase, 1)) for x, y in zip(s, d)]
-    b = [jnp.where(here, pltpu.roll(x, LANES - phase, 1), y) for x, y in zip(s, d)]
-    return a, b
+    lane = lane_id(s[0].shape)
+    here = lane % (2 * phase) < phase
+    other = jnp.where(here, lane + phase, lane - phase)
+    m = [jnp.take_along_axis(jnp.where(here, y, x), other, axis=1, mode="promise_in_bounds") for x, y in zip(s, d)]
+    return [jnp.where(here, x, y) for x, y in zip(s, m)], [jnp.where(here, y, x) for x, y in zip(d, m)]
 
 
 def tiles_of(ref, at):

time: 40.8 us -> 40.6 us (level)
  transfers between devices with their start and end apart: 6 -> 6, of which waited for: 2 -> 2; matrix products, arithmetic and copies ran while one was open for 0% -> 0% of each run, Pallas kernels for 15% -> 14%
where the time goes in v8:
time: 40.6 us; the launch traced here: 40.3 us
  starting transfers between devices  17.9 us (44%)
  Pallas kernels  11.3 us (28%)
  waiting for transfers between devices  11 us (27%)
    all_to_all x1, starting transfers between devices, per_device(): got = lax.all_to_all(pay, 'gy', 0, 0, tiled=True)  7.83 us
    all_to_all x1, starting transfers between devices, per_device(): got = lax.all_to_all(pay, 'gz', 0, 0, tiled=True)  7.05 us
    all_to_all x1, waiting for transfers between devices, per_device(): got = lax.all_to_all(pay, 'gz', 0, 0, tiled=True)  5.61 us
    all_to_all x1, waiting for transfers between devices, per_device(): got = lax.all_to_all(pay, 'gy', 0, 0, tiled=True)  5.4 us
    pallas_call x1, Pallas kernels, per_device(): call(along_x, [tiled, tiled, payload, payload, f32(16, cells), f32(*pay),...  4.45 us
    pallas_call x1, Pallas kernels, per_device(): call(along_z, [f32(planes, rows, cells), f32(planes // 4, rows, cells)],...  3.23 us
    ppermute x4, starting transfers between devices, swap(): return lax.ppermute(values, axis, pairs)  2.99 us
    pallas_call x1, Pallas kernels, per_device(): call(along_y, [tiled, tiled, f32(TILES, planes * rows // 4, LANES), paylo...  1.28 us
  transfers between devices with their start and end apart: 6, of which 2 were waited for; matrix products, arithmetic and copies ran while one was open for 0% of the time, Pallas kernels for 14%

profile of v8, /device:TPU:0, one launch (start us, length us, event | category | flops | bytes accessed | tf_op | source)
XLA Modules:
  0.0 40.3 jit_solution(6924205888567821181)
XLA Ops:
  0.0 4.4 %shard_map.55 = (f32[8,128,128]{2,1,0:T(8,128)S(1)}, f32[8,128,128]{2,1,0:T(8,128)S(1)}, f32[6,8,1024]{2,1,0:T(8,128)S(1)}, f32[6,8,1024]{2,1,0:T(8,128)S(1)}, f...) custom-call(bf16[8,48,384]{2,1,0:T(8,128)(2,1)} %constant.8.clone.y3, ...), custom_call_target="tpu_custom_call" | custom-call | flops 41943040 | bytes 4194304 | tf_op jit(solution)/shard_map/pallas_call | solution.py:577
  4.5 0.1 collective-permute-start
  4.5 0.7 %collective-permute-start.1 = (f32[6,8,1024]{2,1,0:T(8,128)S(1)}, f32[6,8,1024]{2,1,0:T(8,128)S(1)}, u32[]{:S(2)}, u32[]{:S(2)}) collective-permute-start(f32[6,8,1024]{2,1,0:T(8,128)S(1)} %get-tuple-element.26), channel_id=1, source_target_pairs={{1,2},{2,1},{3,4},{4,3},{5,6},{6,5},{9,10},{10,9},{11,12},{12,11},... | collective-permute-start | bytes 589832 | tf_op jit(solution)/shard_map/ppermute | solution.py:545
  5.2 7.8 %all-to-all-start = ((f32[8,8,1536]{2,1,0:T(8,128)}), f32[8,8,1536]{2,1,0:T(8,128)S(1)}, u32[]{:S(2)}, u32[]{:S(2)}) async-start(f32[8,8,1536]{2,1,0:T(8,128)} %get-tuple-element.29), calls=%async_computation | async-start | bytes 786432 | tf_op jit(solution)/shard_map/all_to_all | solution.py:594
  13.1 0.0 collective-permute-done.got_e
  13.1 0.0 collective-permute-done.1.got_o
  13.1 1.3 %shard_map.56 = (f32[8,128,128]{2,1,0:T(8,128)S(1)}, f32[8,128,128]{2,1,0:T(8,128)S(1)}, f32[8,64,128]{2,1,0:T(8,128)S(1)}, f32[6,8,1024]{2,1,0:T(8,128)S(1)}, f...) custom-call(f32[8,128,128]{2,1,0:T(8,128)S(1)} %get-tuple-element.23.smooth, ...), custom_call_target="tpu_custom_call", output_to_operand_aliasing={{0}: (0, {}), {1}: (1, {})} | custom-call | flops 4194304000 | bytes 4194304 | tf_op jit(solution)/shard_map/pallas_call | solution.py:596
  14.4 1.6 %collective-permute-start.2 = (f32[6,8,1024]{2,1,0:T(8,128)S(1)}, f32[6,8,1024]{2,1,0:T(8,128)S(1)}, u32[]{:S(2)}, u32[]{:S(2)}) collective-permute-start(f32[6,8,1024]{2,1,0:T(8,128)S(1)} %get-tuple-element.33), channel_id=1, source_target_pairs={{0,8},{8,0},{16,24},{24,16},{32,40},{40,32},{48,56},{56,48},{64,72... | collective-permute-start | bytes 589832 | tf_op jit(solution)/shard_map/ppermute | solution.py:545
  15.9 0.7 %collective-permute-start.3 = (f32[6,8,1024]{2,1,0:T(8,128)S(1)}, f32[6,8,1024]{2,1,0:T(8,128)S(1)}, u32[]{:S(2)}, u32[]{:S(2)}) collective-permute-start(f32[6,8,1024]{2,1,0:T(8,128)S(1)} %get-tuple-element.34), channel_id=1, source_target_pairs={{8,16},{16,8},{24,32},{32,24},{40,48},{48,40},{56,64},{64,56},{72,... | collective-permute-start | bytes 589832 | tf_op jit(solution)/shard_map/ppermute | solution.py:545
  16.6 5.4 %all-to-all-done.got = f32[8,8,1536]{2,1,0:T(8,128)S(1)} async-done(((f32[8,8,1536]{2,1,0:T(8,128)}), f32[8,8,1536]{2,1,0:T(8,128)S(1)}, u32[]{:S(2)}, u32[]{:S(2)}) %all-to-all-start) | async-done | bytes 393248 | tf_op jit(solution)/shard_map/all_to_all | solution.py:594
  22.0 1.2 %shard_map.57 = f32[16,4,1152]{2,1,0:T(4,128)} custom-call(bf16[64,96]{1,0:T(8,128)(2,1)S(1)} %get-tuple-element.21.w3, bf16[64,192]{1,0:T(8,128)(2,1)S(1)} %get-tuple-element.22.w4, f32[16,1024]{1,0:T(8,128)S(1)} %get-tuple-element.27.cells, f32[16,1024]{1,0:T(8,128)S(1)} %get-tuple-element.28.own, f32[8,8,1536]{2,1,0:T(8,128)S(1)} %all-to-all-done.got), custom_call_target="tpu_custom_call" | custom-call | flops 419430400 | bytes 4194304 | tf_op jit(solution)/shard_map/pallas_call | solution.py:605
  23.2 7.0 %all-to-all-start.1 = ((f32[16,4,1152]{2,1,0:T(4,128)}), f32[16,4,1152]{2,1,0:T(4,128)S(1)}, u32[]{:S(2)}, u32[]{:S(2)}) async-start(f32[16,4,1152]{2,1,0:T(4,128)} %shard_map.57), calls=%async_computation.1 | async-start | bytes 589824 | tf_op jit(solution)/shard_map/all_to_all | solution.py:612
  30.3 0.0 collective-permute-done.2.got_e
  30.3 0.0 collective-permute-done.3.got_o
  30.3 3.2 %shard_map.58 = (f32[16,16,1024]{2,1,0:T(8,128)}, f32[4,16,1024]{2,1,0:T(8,128)S(1)}) custom-call(f32[8,128,128]{2,1,0:T(8,128)S(1)} %get-tuple-element.30.one_s, f32[8,128,128]{2,1,0:T(8,128)S(1)} %get-tuple-element.31.one_d, f32[8,64,128]{2,1,0:T(8,128)S(1)} %get-tuple-element.32.two, f32[6,8,1024]{2,1,0:T(8,128)S(1)} %collective-permute-done.2.got_e, ...), custom_call_target="tpu_custom_call" | custom-call | flops 4194304000 | bytes 4194304 | tf_op jit(solution)/shard_map/pallas_call | solution.py:614
  33.5 5.6 %all-to-all-done.1.got = f32[16,4,1152]{2,1,0:T(4,128)S(1)} async-done(((f32[16,4,1152]{2,1,0:T(4,128)}), f32[16,4,1152]{2,1,0:T(4,128)S(1)}, u32[]{:S(2)}, u32[]{:S(2)}) %all-to-all-start.1) | async-done | bytes 294944 | tf_op jit(solution)/shard_map/all_to_all | solution.py:612
  39.2 1.1 %shard_map.59 = f32[16,16,1024]{2,1,0:T(8,128)} custom-call(f32[16,4,1152]{2,1,0:T(4,128)S(1)} %all-to-all-done.1.got, f32[4,16,1024]{2,1,0:T(8,128)S(1)} %get-tuple-element.35.fourth, f32[16,16,1024]{2,1,0:T(8,128)} %get-tuple-element.36.base), custom_call_target="tpu_custom_call", output_to_operand_aliasing={{}: (2, {})} | custom-call | flops 41943040 | bytes 4194304 | tf_op jit(solution)/shard_map/pallas_call | solution.py:621
Async XLA Ops:
  4.5 8.6 %collective-permute-start = (f32[6,8,1024]{2,1,0:T(8,128)S(1)}, f32[6,8,1024]{2,1,0:T(8,128)S(1)}, u32[]{:S(2)}, u32[]{:S(2)}) collective-permute-start(f32[6,8,1024]{2,1,0:T(8,128)S(1)} %get-tuple-element.25), channel_id=1, source_target_pairs={{0,1},{1,0},{2,3},{3,2},{4,5},{5,4},{6,7},{7,6},{8,9},{9,8},{10,11... | collective-permute-start | bytes 589832 | tf_op jit(solution)/shard_map/ppermute | solution.py:545
  4.5 8.5 %collective-permute-start.1 = (f32[6,8,1024]{2,1,0:T(8,128)S(1)}, f32[6,8,1024]{2,1,0:T(8,128)S(1)}, u32[]{:S(2)}, u32[]{:S(2)}) collective-permute-start(f32[6,8,1024]{2,1,0:T(8,128)S(1)} %get-tuple-element.26), channel_id=1, source_target_pairs={{1,2},{2,1},{3,4},{4,3},{5,6},{6,5},{9,10},{10,9},{11,12},{12,11},... | collective-permute-start | bytes 589832 | tf_op jit(solution)/shard_map/ppermute | solution.py:545
  5.2 16.8 %all-to-all-start = ((f32[8,8,1536]{2,1,0:T(8,128)}), f32[8,8,1536]{2,1,0:T(8,128)S(1)}, u32[]{:S(2)}, u32[]{:S(2)}) async-start(f32[8,8,1536]{2,1,0:T(8,128)} %get-tuple-element.29), calls=%async_computation | async-start | bytes 786432 | tf_op jit(solution)/shard_map/all_to_all | solution.py:594
  14.4 15.9 %collective-permute-start.2 = (f32[6,8,1024]{2,1,0:T(8,128)S(1)}, f32[6,8,1024]{2,1,0:T(8,128)S(1)}, u32[]{:S(2)}, u32[]{:S(2)}) collective-permute-start(f32[6,8,1024]{2,1,0:T(8,128)S(1)} %get-tuple-element.33), channel_id=1, source_target_pairs={{0,8},{8,0},{16,24},{24,16},{32,40},{40,32},{48,56},{56,48},{64,72... | collective-permute-start | bytes 589832 | tf_op jit(solution)/shard_map/ppermute | solution.py:545
  15.9 14.4 %collective-permute-start.3 = (f32[6,8,1024]{2,1,0:T(8,128)S(1)}, f32[6,8,1024]{2,1,0:T(8,128)S(1)}, u32[]{:S(2)}, u32[]{:S(2)}) collective-permute-start(f32[6,8,1024]{2,1,0:T(8,128)S(1)} %get-tuple-element.34), channel_id=1, source_target_pairs={{8,16},{16,8},{24,32},{32,24},{40,48},{48,40},{56,64},{64,56},{72,... | collective-permute-start | bytes 589832 | tf_op jit(solution)/shard_map/ppermute | solution.py:545
  23.2 15.9 %all-to-all-start.1 = ((f32[16,4,1152]{2,1,0:T(4,128)}), f32[16,4,1152]{2,1,0:T(4,128)S(1)}, u32[]{:S(2)}, u32[]{:S(2)}) async-start(f32[16,4,1152]{2,1,0:T(4,128)} %shard_map.57), calls=%async_computation.1 | async-start | bytes 589824 | tf_op jit(solution)/shard_map/all_to_all | solution.py:612

commit v9 on v8

--- a/solution.py
+++ b/solution.py
@@ -259,12 +259,13 @@
             detail[t, pl.ds(at, 8), :] = d[t]
 
     def group(k):
-        load(k).wait()
-        load(k + 4).wait()
-        for i in range(4):
-            plane(4 * k + i)
-
-    times(4, group)
+        for j in range(2):
+            load(2 * k + j).wait()
+            load(2 * k + j + 4).wait()
+        for i in range(8):
+            plane(8 * k + i)
+
+    times(2, group)
     for hint in hints:
         hint.wait()
 
@@ -289,10 +290,13 @@
         right = mix(to == me + 1, three[16:24], three[24:32])
         left = mix(to == me - 1, three[32:40], three[40:48])
         pay[to, :, 0:WIDE] = mix(to > me, right, left)
+    parts = [pl.ds(0, WIDE), pl.ds(WIDE, WIDE // 2)]
+    sends = [pltpu.make_async_copy(pay.at[:, :, p], result.at[:, :, p], sem.at[4 + k]) for k, p in enumerate(parts)]
+    sends[0].start()
+    for to in range(pay.shape[0]):
         pay[to, 0:4, WIDE:] = four[to * 4 : to * 4 + 4, : WIDE // 2]
         pay[to, 4:8, WIDE:] = four[to * 4 : to * 4 + 4, WIDE // 2 :]
-    send = pltpu.make_async_copy(pay, result, sem.at[4])
-    send.start()
+    sends[1].start()
     flip = me % 2 == 1
 
     def column(t):
@@ -306,7 +310,8 @@
             pay_o[c, :, lanes] = mix(flip, right, left)
 
     times(TILES, column, 4)
-    send.wait()
+    for send in sends:
+        send.wait()
 
 
 def along_y(smooth, detail, got_e, got_o, one_s, one_d, two, pay_e, pay_o, cells, thick):
@@ -585,7 +590,7 @@
             pltpu.VMEM((4 * ny, 6 * 32), jnp.bfloat16),
             vmem(*pay),
             sems(8),
-            sems(5),
+            sems(6),
         ],
         in_specs=[far] * 5,
         out_specs=[here] * 5 + [far, here, here],

time: 40.6 us -> 40.2 us (level)
  no operation moved by 1% of the time
where the time goes in v9:
time: 40.2 us; the launch traced here: 39.9 us
  starting transfers between devices  17.9 us (45%)
  waiting for transfers between devices  11 us (27%)
  Pallas kernels  10.9 us (27%)
    all_to_all x1, starting transfers between devices, per_device(): got = lax.all_to_all(pay, 'gy', 0, 0, tiled=True)  7.83 us
    all_to_all x1, starting transfers between devices, per_device(): got = lax.all_to_all(pay, 'gz', 0, 0, tiled=True)  7.05 us
    all_to_all x1, waiting for transfers between devices, per_device(): got = lax.all_to_all(pay, 'gz', 0, 0, tiled=True)  5.61 us
    all_to_all x1, waiting for transfers between devices, per_device(): got = lax.all_to_all(pay, 'gy', 0, 0, tiled=True)  5.4 us
    pallas_call x1, Pallas kernels, per_device(): call(along_x, [tiled, tiled, payload, payload, f32(16, cells), f32(*pay),...  4.08 us
    pallas_call x1, Pallas kernels, per_device(): call(along_z, [f32(planes, rows, cells), f32(planes // 4, rows, cells)],...  3.23 us
    ppermute x4, starting transfers between devices, swap(): return lax.ppermute(values, axis, pairs)  2.99 us
    pallas_call x1, Pallas kernels, per_device(): call(along_y, [tiled, tiled, f32(TILES, planes * rows // 4, LANES), paylo...  1.28 us
  transfers between devices with their start and end apart: 6, of which 2 were waited for; matrix products, arithmetic and copies ran while one was open for 0% of the time, Pallas kernels for 14%

profile of v9, /device:TPU:0, one launch (start us, length us, event | category | flops | bytes accessed | tf_op | source)
XLA Modules:
  0.0 39.9 jit_solution(17076627768857774572)
XLA Ops:
  0.0 4.1 %shard_map.55 = (f32[8,128,128]{2,1,0:T(8,128)S(1)}, f32[8,128,128]{2,1,0:T(8,128)S(1)}, f32[6,8,1024]{2,1,0:T(8,128)S(1)}, f32[6,8,1024]{2,1,0:T(8,128)S(1)}, f...) custom-call(bf16[8,48,384]{2,1,0:T(8,128)(2,1)} %constant.8.clone.y3, ...), custom_call_target="tpu_custom_call" | custom-call | flops 41943040 | bytes 4194304 | tf_op jit(solution)/shard_map/pallas_call | solution.py:582
  4.1 0.1 collective-permute-start
  4.2 0.7 %collective-permute-start.1 = (f32[6,8,1024]{2,1,0:T(8,128)S(1)}, f32[6,8,1024]{2,1,0:T(8,128)S(1)}, u32[]{:S(2)}, u32[]{:S(2)}) collective-permute-start(f32[6,8,1024]{2,1,0:T(8,128)S(1)} %get-tuple-element.26), channel_id=1, source_target_pairs={{1,2},{2,1},{3,4},{4,3},{5,6},{6,5},{9,10},{10,9},{11,12},{12,11},... | collective-permute-start | bytes 589832 | tf_op jit(solution)/shard_map/ppermute | solution.py:550
  4.9 7.8 %all-to-all-start = ((f32[8,8,1536]{2,1,0:T(8,128)}), f32[8,8,1536]{2,1,0:T(8,128)S(1)}, u32[]{:S(2)}, u32[]{:S(2)}) async-start(f32[8,8,1536]{2,1,0:T(8,128)} %get-tuple-element.29), calls=%async_computation | async-start | bytes 786432 | tf_op jit(solution)/shard_map/all_to_all | solution.py:599
  12.7 0.0 collective-permute-done.got_e
  12.7 0.0 collective-permute-done.1.got_o
  12.7 1.3 %shard_map.56 = (f32[8,128,128]{2,1,0:T(8,128)S(1)}, f32[8,128,128]{2,1,0:T(8,128)S(1)}, f32[8,64,128]{2,1,0:T(8,128)S(1)}, f32[6,8,1024]{2,1,0:T(8,128)S(1)}, f...) custom-call(f32[8,128,128]{2,1,0:T(8,128)S(1)} %get-tuple-element.23.smooth, ...), custom_call_target="tpu_custom_call", output_to_operand_aliasing={{0}: (0, {}), {1}: (1, {})} | custom-call | flops 4194304000 | bytes 4194304 | tf_op jit(solution)/shard_map/pallas_call | solution.py:601
  14.0 1.6 %collective-permute-start.2 = (f32[6,8,1024]{2,1,0:T(8,128)S(1)}, f32[6,8,1024]{2,1,0:T(8,128)S(1)}, u32[]{:S(2)}, u32[]{:S(2)}) collective-permute-start(f32[6,8,1024]{2,1,0:T(8,128)S(1)} %get-tuple-element.33), channel_id=1, source_target_pairs={{0,8},{8,0},{16,24},{24,16},{32,40},{40,32},{48,56},{56,48},{64,72... | collective-permute-start | bytes 589832 | tf_op jit(solution)/shard_map/ppermute | solution.py:550
  15.6 0.7 %collective-permute-start.3 = (f32[6,8,1024]{2,1,0:T(8,128)S(1)}, f32[6,8,1024]{2,1,0:T(8,128)S(1)}, u32[]{:S(2)}, u32[]{:S(2)}) collective-permute-start(f32[6,8,1024]{2,1,0:T(8,128)S(1)} %get-tuple-element.34), channel_id=1, source_target_pairs={{8,16},{16,8},{24,32},{32,24},{40,48},{48,40},{56,64},{64,56},{72,... | collective-permute-start | bytes 589832 | tf_op jit(solution)/shard_map/ppermute | solution.py:550
  16.2 5.4 %all-to-all-done.got = f32[8,8,1536]{2,1,0:T(8,128)S(1)} async-done(((f32[8,8,1536]{2,1,0:T(8,128)}), f32[8,8,1536]{2,1,0:T(8,128)S(1)}, u32[]{:S(2)}, u32[]{:S(2)}) %all-to-all-start) | async-done | bytes 393248 | tf_op jit(solution)/shard_map/all_to_all | solution.py:599
  21.6 1.2 %shard_map.57 = f32[16,4,1152]{2,1,0:T(4,128)} custom-call(bf16[64,96]{1,0:T(8,128)(2,1)S(1)} %get-tuple-element.21.w3, bf16[64,192]{1,0:T(8,128)(2,1)S(1)} %get-tuple-element.22.w4, f32[16,1024]{1,0:T(8,128)S(1)} %get-tuple-element.27.cells, f32[16,1024]{1,0:T(8,128)S(1)} %get-tuple-element.28.own, f32[8,8,1536]{2,1,0:T(8,128)S(1)} %all-to-all-done.got), custom_call_target="tpu_custom_call" | custom-call | flops 419430400 | bytes 4194304 | tf_op jit(solution)/shard_map/pallas_call | solution.py:610
  22.9 7.0 %all-to-all-start.1 = ((f32[16,4,1152]{2,1,0:T(4,128)}), f32[16,4,1152]{2,1,0:T(4,128)S(1)}, u32[]{:S(2)}, u32[]{:S(2)}) async-start(f32[16,4,1152]{2,1,0:T(4,128)} %shard_map.57), calls=%async_computation.1 | async-start | bytes 589824 | tf_op jit(solution)/shard_map/all_to_all | solution.py:617
  29.9 0.0 collective-permute-done.2.got_e
  29.9 0.0 collective-permute-done.3.got_o
  29.9 3.2 %shard_map.58 = (f32[16,16,1024]{2,1,0:T(8,128)}, f32[4,16,1024]{2,1,0:T(8,128)S(1)}) custom-call(f32[8,128,128]{2,1,0:T(8,128)S(1)} %get-tuple-element.30.one_s, f32[8,128,128]{2,1,0:T(8,128)S(1)} %get-tuple-element.31.one_d, f32[8,64,128]{2,1,0:T(8,128)S(1)} %get-tuple-element.32.two, f32[6,8,1024]{2,1,0:T(8,128)S(1)} %collective-permute-done.2.got_e, ...), custom_call_target="tpu_custom_call" | custom-call | flops 4194304000 | bytes 4194304 | tf_op jit(solution)/shard_map/pallas_call | solution.py:619
  33.2 5.6 %all-to-all-done.1.got = f32[16,4,1152]{2,1,0:T(4,128)S(1)} async-done(((f32[16,4,1152]{2,1,0:T(4,128)}), f32[16,4,1152]{2,1,0:T(4,128)S(1)}, u32[]{:S(2)}, u32[]{:S(2)}) %all-to-all-start.1) | async-done | bytes 294944 | tf_op jit(solution)/shard_map/all_to_all | solution.py:617
  38.8 1.1 %shard_map.59 = f32[16,16,1024]{2,1,0:T(8,128)} custom-call(f32[16,4,1152]{2,1,0:T(4,128)S(1)} %all-to-all-done.1.got, f32[4,16,1024]{2,1,0:T(8,128)S(1)} %get-tuple-element.35.fourth, f32[16,16,1024]{2,1,0:T(8,128)} %get-tuple-element.36.base), custom_call_target="tpu_custom_call", output_to_operand_aliasing={{}: (2, {})} | custom-call | flops 41943040 | bytes 4194304 | tf_op jit(solution)/shard_map/pallas_call | solution.py:626
Async XLA Ops:
  4.1 8.6 %collective-permute-start = (f32[6,8,1024]{2,1,0:T(8,128)S(1)}, f32[6,8,1024]{2,1,0:T(8,128)S(1)}, u32[]{:S(2)}, u32[]{:S(2)}) collective-permute-start(f32[6,8,1024]{2,1,0:T(8,128)S(1)} %get-tuple-element.25), channel_id=1, source_target_pairs={{0,1},{1,0},{2,3},{3,2},{4,5},{5,4},{6,7},{7,6},{8,9},{9,8},{10,11... | collective-permute-start | bytes 589832 | tf_op jit(solution)/shard_map/ppermute | solution.py:550
  4.2 8.5 %collective-permute-start.1 = (f32[6,8,1024]{2,1,0:T(8,128)S(1)}, f32[6,8,1024]{2,1,0:T(8,128)S(1)}, u32[]{:S(2)}, u32[]{:S(2)}) collective-permute-start(f32[6,8,1024]{2,1,0:T(8,128)S(1)} %get-tuple-element.26), channel_id=1, source_target_pairs={{1,2},{2,1},{3,4},{4,3},{5,6},{6,5},{9,10},{10,9},{11,12},{12,11},... | collective-permute-start | bytes 589832 | tf_op jit(solution)/shard_map/ppermute | solution.py:550
  4.9 16.8 %all-to-all-start = ((f32[8,8,1536]{2,1,0:T(8,128)}), f32[8,8,1536]{2,1,0:T(8,128)S(1)}, u32[]{:S(2)}, u32[]{:S(2)}) async-start(f32[8,8,1536]{2,1,0:T(8,128)} %get-tuple-element.29), calls=%async_computation | async-start | bytes 786432 | tf_op jit(solution)/shard_map/all_to_all | solution.py:599
  14.0 15.9 %collective-permute-start.2 = (f32[6,8,1024]{2,1,0:T(8,128)S(1)}, f32[6,8,1024]{2,1,0:T(8,128)S(1)}, u32[]{:S(2)}, u32[]{:S(2)}) collective-permute-start(f32[6,8,1024]{2,1,0:T(8,128)S(1)} %get-tuple-element.33), channel_id=1, source_target_pairs={{0,8},{8,0},{16,24},{24,16},{32,40},{40,32},{48,56},{56,48},{64,72... | collective-permute-start | bytes 589832 | tf_op jit(solution)/shard_map/ppermute | solution.py:550
  15.6 14.4 %collective-permute-start.3 = (f32[6,8,1024]{2,1,0:T(8,128)S(1)}, f32[6,8,1024]{2,1,0:T(8,128)S(1)}, u32[]{:S(2)}, u32[]{:S(2)}) collective-permute-start(f32[6,8,1024]{2,1,0:T(8,128)S(1)} %get-tuple-element.34), channel_id=1, source_target_pairs={{8,16},{16,8},{24,32},{32,24},{40,48},{48,40},{56,64},{64,56},{72,... | collective-permute-start | bytes 589832 | tf_op jit(solution)/shard_map/ppermute | solution.py:550
  22.9 15.9 %all-to-all-start.1 = ((f32[16,4,1152]{2,1,0:T(4,128)}), f32[16,4,1152]{2,1,0:T(4,128)S(1)}, u32[]{:S(2)}, u32[]{:S(2)}) async-start(f32[16,4,1152]{2,1,0:T(4,128)} %shard_map.57), calls=%async_computation.1 | async-start | bytes 589824 | tf_op jit(solution)/shard_map/all_to_all | solution.py:617

commit v10 on v9

--- a/solution.py
+++ b/solution.py
@@ -234,12 +234,12 @@
     me, mz = lax.axis_index("gy"), lax.axis_index("gz")
 
     def load(k):
-        at = pl.ds(pl.multiple_of(k * 32, 32), 32)
+        at = pl.ds(pl.multiple_of(k * 64, 64), 64)
         return pltpu.make_async_copy(density.at[at], x.at[at], load_sem.at[k])
 
-    for k in range(4):
+    for k in range(2):
         load(k).start()
-        load(k + 4).start()
+        load(k + 2).start()
     hints = [
         pltpu.make_async_copy(y3.at[me], w3, sem.at[0]),
         pltpu.make_async_copy(y4.at[me], w4, sem.at[1]),
@@ -259,9 +259,8 @@
             detail[t, pl.ds(at, 8), :] = d[t]
 
     def group(k):
-        for j in range(2):
-            load(2 * k + j).wait()
-            load(2 * k + j + 4).wait()
+        load(k).wait()
+        load(k + 2).wait()
         for i in range(8):
             plane(8 * k + i)
 
@@ -445,7 +444,7 @@
         for z, v in enumerate(interleave(*lift(rows, *ends, first, last, mix))):
             fine[pl.ds(z * 8, 8), lanes] = v
 
-    times(TILES, stack, TILES)
+    times(TILES, stack, 2)
     sends = {z: pltpu.make_async_copy(out.at[z], result.at[z], sem.at[z]) for z in range(16) if z % 4}
     for z in range(1, 16, 2):
         sends[z].start()
@@ -589,7 +588,7 @@
             pltpu.VMEM((48, 6 * 64), jnp.bfloat16),
             pltpu.VMEM((4 * ny, 6 * 32), jnp.bfloat16),
             vmem(*pay),
-            sems(8),
+            sems(4),
             sems(6),
         ],
         in_specs=[far] * 5,

time: 40.2 us -> 40.1 us (level)
  Pallas kernels: 10.9 us -> 9.9 us
  waiting for transfers between devices: 11 us -> 12 us
    all_to_all x1, waiting for transfers between devices: 5.61 us -> 6.54 us  [per_device(): got = lax.all_to_all(pay, 'gz', 0, 0, tiled=True)]
    pallas_call x1, Pallas kernels: 3.23 us -> 2.3 us  [per_device(): call(along_z, [f32(planes, rows, cells), f32(planes // 4, rows, cells)],...]
  transfers between devices with their start and end apart: 6 -> 6, of which waited for: 2 -> 2; matrix products, arithmetic and copies ran while one was open for 0% -> 0% of each run, Pallas kernels for 14% -> 12%
where the time goes in v10:
time: 40.1 us; the launch traced here: 39.8 us
  starting transfers between devices  17.9 us (45%)
  waiting for transfers between devices  12 us (30%)
  Pallas kernels  9.9 us (25%)
    all_to_all x1, starting transfers between devices, per_device(): got = lax.all_to_all(pay, 'gy', 0, 0, tiled=True)  7.83 us
    all_to_all x1, starting transfers between devices, per_device(): got = lax.all_to_all(pay, 'gz', 0, 0, tiled=True)  7.05 us
    all_to_all x1, waiting for transfers between devices, per_device(): got = lax.all_to_all(pay, 'gz', 0, 0, tiled=True)  6.54 us
    all_to_all x1, waiting for transfers between devices, per_device(): got = lax.all_to_all(pay, 'gy', 0, 0, tiled=True)  5.4 us
    pallas_call x1, Pallas kernels, per_device(): call(along_x, [tiled, tiled, payload, payload, f32(16, cells), f32(*pay),...  3.98 us
    ppermute x4, starting transfers between devices, swap(): return lax.ppermute(values, axis, pairs)  2.99 us
    pallas_call x1, Pallas kernels, per_device(): call(along_z, [f32(planes, rows, cells), f32(planes // 4, rows, cells)],...  2.3 us
    pallas_call x1, Pallas kernels, per_device(): call(along_y, [tiled, tiled, f32(TILES, planes * rows // 4, LANES), paylo...  1.28 us
  transfers between devices with their start and end apart: 6, of which 2 were waited for; matrix products, arithmetic and copies ran while one was open for 0% of the time, Pallas kernels for 12%

profile of v10, /device:TPU:0, one launch (start us, length us, event | category | flops | bytes accessed | tf_op | source)
XLA Modules:
  0.0 39.8 jit_solution(7961308732092938804)
XLA Ops:
  0.0 4.0 %shard_map.55 = (f32[8,128,128]{2,1,0:T(8,128)S(1)}, f32[8,128,128]{2,1,0:T(8,128)S(1)}, f32[6,8,1024]{2,1,0:T(8,128)S(1)}, f32[6,8,1024]{2,1,0:T(8,128)S(1)}, f...) custom-call(bf16[8,48,384]{2,1,0:T(8,128)(2,1)} %constant.8.clone.y3, ...), custom_call_target="tpu_custom_call" | custom-call | flops 41943040 | bytes 4194304 | tf_op jit(solution)/shard_map/pallas_call | solution.py:581
  4.0 0.1 collective-permute-start
  4.1 0.7 %collective-permute-start.1 = (f32[6,8,1024]{2,1,0:T(8,128)S(1)}, f32[6,8,1024]{2,1,0:T(8,128)S(1)}, u32[]{:S(2)}, u32[]{:S(2)}) collective-permute-start(f32[6,8,1024]{2,1,0:T(8,128)S(1)} %get-tuple-element.26), channel_id=1, source_target_pairs={{1,2},{2,1},{3,4},{4,3},{5,6},{6,5},{9,10},{10,9},{11,12},{12,11},... | collective-permute-start | bytes 589832 | tf_op jit(solution)/shard_map/ppermute | solution.py:549
  4.8 7.8 %all-to-all-start = ((f32[8,8,1536]{2,1,0:T(8,128)}), f32[8,8,1536]{2,1,0:T(8,128)S(1)}, u32[]{:S(2)}, u32[]{:S(2)}) async-start(f32[8,8,1536]{2,1,0:T(8,128)} %get-tuple-element.29), calls=%async_computation | async-start | bytes 786432 | tf_op jit(solution)/shard_map/all_to_all | solution.py:598
  12.6 0.0 collective-permute-done.got_e
  12.6 0.0 collective-permute-done.1.got_o
  12.6 1.3 %shard_map.56 = (f32[8,128,128]{2,1,0:T(8,128)S(1)}, f32[8,128,128]{2,1,0:T(8,128)S(1)}, f32[8,64,128]{2,1,0:T(8,128)S(1)}, f32[6,8,1024]{2,1,0:T(8,128)S(1)}, f...) custom-call(f32[8,128,128]{2,1,0:T(8,128)S(1)} %get-tuple-element.23.smooth, ...), custom_call_target="tpu_custom_call", output_to_operand_aliasing={{0}: (0, {}), {1}: (1, {})} | custom-call | flops 4194304000 | bytes 4194304 | tf_op jit(solution)/shard_map/pallas_call | solution.py:600
  13.9 1.6 %collective-permute-start.2 = (f32[6,8,1024]{2,1,0:T(8,128)S(1)}, f32[6,8,1024]{2,1,0:T(8,128)S(1)}, u32[]{:S(2)}, u32[]{:S(2)}) collective-permute-start(f32[6,8,1024]{2,1,0:T(8,128)S(1)} %get-tuple-element.33), channel_id=1, source_target_pairs={{0,8},{8,0},{16,24},{24,16},{32,40},{40,32},{48,56},{56,48},{64,72... | collective-permute-start | bytes 589832 | tf_op jit(solution)/shard_map/ppermute | solution.py:549
  15.5 0.7 %collective-permute-start.3 = (f32[6,8,1024]{2,1,0:T(8,128)S(1)}, f32[6,8,1024]{2,1,0:T(8,128)S(1)}, u32[]{:S(2)}, u32[]{:S(2)}) collective-permute-start(f32[6,8,1024]{2,1,0:T(8,128)S(1)} %get-tuple-element.34), channel_id=1, source_target_pairs={{8,16},{16,8},{24,32},{32,24},{40,48},{48,40},{56,64},{64,56},{72,... | collective-permute-start | bytes 589832 | tf_op jit(solution)/shard_map/ppermute | solution.py:549
  16.1 5.4 %all-to-all-done.got = f32[8,8,1536]{2,1,0:T(8,128)S(1)} async-done(((f32[8,8,1536]{2,1,0:T(8,128)}), f32[8,8,1536]{2,1,0:T(8,128)S(1)}, u32[]{:S(2)}, u32[]{:S(2)}) %all-to-all-start) | async-done | bytes 393248 | tf_op jit(solution)/shard_map/all_to_all | solution.py:598
  21.5 1.2 %shard_map.57 = f32[16,4,1152]{2,1,0:T(4,128)} custom-call(bf16[64,96]{1,0:T(8,128)(2,1)S(1)} %get-tuple-element.21.w3, bf16[64,192]{1,0:T(8,128)(2,1)S(1)} %get-tuple-element.22.w4, f32[16,1024]{1,0:T(8,128)S(1)} %get-tuple-element.27.cells, f32[16,1024]{1,0:T(8,128)S(1)} %get-tuple-element.28.own, f32[8,8,1536]{2,1,0:T(8,128)S(1)} %all-to-all-done.got), custom_call_target="tpu_custom_call" | custom-call | flops 419430400 | bytes 4194304 | tf_op jit(solution)/shard_map/pallas_call | solution.py:609
  22.8 7.0 %all-to-all-start.1 = ((f32[16,4,1152]{2,1,0:T(4,128)}), f32[16,4,1152]{2,1,0:T(4,128)S(1)}, u32[]{:S(2)}, u32[]{:S(2)}) async-start(f32[16,4,1152]{2,1,0:T(4,128)} %shard_map.57), calls=%async_computation.1 | async-start | bytes 589824 | tf_op jit(solution)/shard_map/all_to_all | solution.py:616
  29.8 0.0 collective-permute-done.2.got_e
  29.8 0.0 collective-permute-done.3.got_o
  29.8 2.3 %shard_map.58 = (f32[16,16,1024]{2,1,0:T(8,128)}, f32[4,16,1024]{2,1,0:T(8,128)S(1)}) custom-call(f32[8,128,128]{2,1,0:T(8,128)S(1)} %get-tuple-element.30.one_s, f32[8,128,128]{2,1,0:T(8,128)S(1)} %get-tuple-element.31.one_d, f32[8,64,128]{2,1,0:T(8,128)S(1)} %get-tuple-element.32.two, f32[6,8,1024]{2,1,0:T(8,128)S(1)} %collective-permute-done.2.got_e, ...), custom_call_target="tpu_custom_call" | custom-call | flops 4194304000 | bytes 4194304 | tf_op jit(solution)/shard_map/pallas_call | solution.py:618
  32.1 6.5 %all-to-all-done.1.got = f32[16,4,1152]{2,1,0:T(4,128)S(1)} async-done(((f32[16,4,1152]{2,1,0:T(4,128)}), f32[16,4,1152]{2,1,0:T(4,128)S(1)}, u32[]{:S(2)}, u32[]{:S(2)}) %all-to-all-start.1) | async-done | bytes 294944 | tf_op jit(solution)/shard_map/all_to_all | solution.py:616
  38.7 1.1 %shard_map.59 = f32[16,16,1024]{2,1,0:T(8,128)} custom-call(f32[16,4,1152]{2,1,0:T(4,128)S(1)} %all-to-all-done.1.got, f32[4,16,1024]{2,1,0:T(8,128)S(1)} %get-tuple-element.35.fourth, f32[16,16,1024]{2,1,0:T(8,128)} %get-tuple-element.36.base), custom_call_target="tpu_custom_call", output_to_operand_aliasing={{}: (2, {})} | custom-call | flops 41943040 | bytes 4194304 | tf_op jit(solution)/shard_map/pallas_call | solution.py:625
Async XLA Ops:
  4.0 8.6 %collective-permute-start = (f32[6,8,1024]{2,1,0:T(8,128)S(1)}, f32[6,8,1024]{2,1,0:T(8,128)S(1)}, u32[]{:S(2)}, u32[]{:S(2)}) collective-permute-start(f32[6,8,1024]{2,1,0:T(8,128)S(1)} %get-tuple-element.25), channel_id=1, source_target_pairs={{0,1},{1,0},{2,3},{3,2},{4,5},{5,4},{6,7},{7,6},{8,9},{9,8},{10,11... | collective-permute-start | bytes 589832 | tf_op jit(solution)/shard_map/ppermute | solution.py:549
  4.1 8.5 %collective-permute-start.1 = (f32[6,8,1024]{2,1,0:T(8,128)S(1)}, f32[6,8,1024]{2,1,0:T(8,128)S(1)}, u32[]{:S(2)}, u32[]{:S(2)}) collective-permute-start(f32[6,8,1024]{2,1,0:T(8,128)S(1)} %get-tuple-element.26), channel_id=1, source_target_pairs={{1,2},{2,1},{3,4},{4,3},{5,6},{6,5},{9,10},{10,9},{11,12},{12,11},... | collective-permute-start | bytes 589832 | tf_op jit(solution)/shard_map/ppermute | solution.py:549
  4.8 16.8 %all-to-all-start = ((f32[8,8,1536]{2,1,0:T(8,128)}), f32[8,8,1536]{2,1,0:T(8,128)S(1)}, u32[]{:S(2)}, u32[]{:S(2)}) async-start(f32[8,8,1536]{2,1,0:T(8,128)} %get-tuple-element.29), calls=%async_computation | async-start | bytes 786432 | tf_op jit(solution)/shard_map/all_to_all | solution.py:598
  13.9 15.9 %collective-permute-start.2 = (f32[6,8,1024]{2,1,0:T(8,128)S(1)}, f32[6,8,1024]{2,1,0:T(8,128)S(1)}, u32[]{:S(2)}, u32[]{:S(2)}) collective-permute-start(f32[6,8,1024]{2,1,0:T(8,128)S(1)} %get-tuple-element.33), channel_id=1, source_target_pairs={{0,8},{8,0},{16,24},{24,16},{32,40},{40,32},{48,56},{56,48},{64,72... | collective-permute-start | bytes 589832 | tf_op jit(solution)/shard_map/ppermute | solution.py:549
  15.5 14.4 %collective-permute-start.3 = (f32[6,8,1024]{2,1,0:T(8,128)S(1)}, f32[6,8,1024]{2,1,0:T(8,128)S(1)}, u32[]{:S(2)}, u32[]{:S(2)}) collective-permute-start(f32[6,8,1024]{2,1,0:T(8,128)S(1)} %get-tuple-element.34), channel_id=1, source_target_pairs={{8,16},{16,8},{24,32},{32,24},{40,48},{48,40},{56,64},{64,56},{72,... | collective-permute-start | bytes 589832 | tf_op jit(solution)/shard_map/ppermute | solution.py:549
  22.8 15.9 %all-to-all-start.1 = ((f32[16,4,1152]{2,1,0:T(4,128)}), f32[16,4,1152]{2,1,0:T(4,128)S(1)}, u32[]{:S(2)}, u32[]{:S(2)}) async-start(f32[16,4,1152]{2,1,0:T(4,128)} %shard_map.57), calls=%async_computation.1 | async-start | bytes 589824 | tf_op jit(solution)/shard_map/all_to_all | solution.py:616

commit v11 on v9

--- a/solution.py
+++ b/solution.py
@@ -486,7 +486,7 @@
     row = lax.broadcasted_iota(jnp.int32, (16, LANES), 0)
     here = (row % 4 == 0) & (lane_id((16, LANES)) % 4 == 0)
     sends = [pltpu.make_async_copy(planes.at[i], result.at[4 * i], sem.at[i]) for i in range(4)]
-    for i in range(4):
+    for i in (1, 3, 0, 2):
         for t in range(TILES):
             planes[i, :, tile(t)] = jnp.where(here, spread[t, pl.ds(i * 16, 16), :], fourth[i, :, tile(t)])
         sends[i].start()

time: 40.2 us -> 40.2 us (level)
  no operation moved by 1% of the time
where the time goes in v11:
time: 40.2 us; the launch traced here: 39.9 us
  starting transfers between devices  17.9 us (45%)
  waiting for transfers between devices  11 us (27%)
  Pallas kernels  10.9 us (27%)
    all_to_all x1, starting transfers between devices, per_device(): got = lax.all_to_all(pay, 'gy', 0, 0, tiled=True)  7.83 us
    all_to_all x1, starting transfers between devices, per_device(): got = lax.all_to_all(pay, 'gz', 0, 0, tiled=True)  7.05 us
    all_to_all x1, waiting for transfers between devices, per_device(): got = lax.all_to_all(pay, 'gz', 0, 0, tiled=True)  5.61 us
    all_to_all x1, waiting for transfers between devices, per_device(): got = lax.all_to_all(pay, 'gy', 0, 0, tiled=True)  5.4 us
    pallas_call x1, Pallas kernels, per_device(): call(along_x, [tiled, tiled, payload, payload, f32(16, cells), f32(*pay),...  4.08 us
    pallas_call x1, Pallas kernels, per_device(): call(along_z, [f32(planes, rows, cells), f32(planes // 4, rows, cells)],...  3.23 us
    ppermute x4, starting transfers between devices, swap(): return lax.ppermute(values, axis, pairs)  2.99 us
    pallas_call x1, Pallas kernels, per_device(): call(along_y, [tiled, tiled, f32(TILES, planes * rows // 4, LANES), paylo...  1.28 us
  transfers between devices with their start and end apart: 6, of which 2 were waited for; matrix products, arithmetic and copies ran while one was open for 0% of the time, Pallas kernels for 14%

profile of v11, /device:TPU:0, one launch (start us, length us, event | category | flops | bytes accessed | tf_op | source)
XLA Modules:
  0.0 39.9 jit_solution(3856387201878397271)
XLA Ops:
  0.0 4.1 %shard_map.55 = (f32[8,128,128]{2,1,0:T(8,128)S(1)}, f32[8,128,128]{2,1,0:T(8,128)S(1)}, f32[6,8,1024]{2,1,0:T(8,128)S(1)}, f32[6,8,1024]{2,1,0:T(8,128)S(1)}, f...) custom-call(bf16[8,48,384]{2,1,0:T(8,128)(2,1)} %constant.8.clone.y3, ...), custom_call_target="tpu_custom_call" | custom-call | flops 41943040 | bytes 4194304 | tf_op jit(solution)/shard_map/pallas_call | solution.py:582
  4.1 0.1 collective-permute-start
  4.2 0.7 %collective-permute-start.1 = (f32[6,8,1024]{2,1,0:T(8,128)S(1)}, f32[6,8,1024]{2,1,0:T(8,128)S(1)}, u32[]{:S(2)}, u32[]{:S(2)}) collective-permute-start(f32[6,8,1024]{2,1,0:T(8,128)S(1)} %get-tuple-element.26), channel_id=1, source_target_pairs={{1,2},{2,1},{3,4},{4,3},{5,6},{6,5},{9,10},{10,9},{11,12},{12,11},... | collective-permute-start | bytes 589832 | tf_op jit(solution)/shard_map/ppermute | solution.py:550
  4.9 7.8 %all-to-all-start = ((f32[8,8,1536]{2,1,0:T(8,128)}), f32[8,8,1536]{2,1,0:T(8,128)S(1)}, u32[]{:S(2)}, u32[]{:S(2)}) async-start(f32[8,8,1536]{2,1,0:T(8,128)} %get-tuple-element.29), calls=%async_computation | async-start | bytes 786432 | tf_op jit(solution)/shard_map/all_to_all | solution.py:599
  12.7 0.0 collective-permute-done.got_e
  12.7 0.0 collective-permute-done.1.got_o
  12.7 1.3 %shard_map.56 = (f32[8,128,128]{2,1,0:T(8,128)S(1)}, f32[8,128,128]{2,1,0:T(8,128)S(1)}, f32[8,64,128]{2,1,0:T(8,128)S(1)}, f32[6,8,1024]{2,1,0:T(8,128)S(1)}, f...) custom-call(f32[8,128,128]{2,1,0:T(8,128)S(1)} %get-tuple-element.23.smooth, ...), custom_call_target="tpu_custom_call", output_to_operand_aliasing={{0}: (0, {}), {1}: (1, {})} | custom-call | flops 4194304000 | bytes 4194304 | tf_op jit(solution)/shard_map/pallas_call | solution.py:601
  14.0 1.6 %collective-permute-start.2 = (f32[6,8,1024]{2,1,0:T(8,128)S(1)}, f32[6,8,1024]{2,1,0:T(8,128)S(1)}, u32[]{:S(2)}, u32[]{:S(2)}) collective-permute-start(f32[6,8,1024]{2,1,0:T(8,128)S(1)} %get-tuple-element.33), channel_id=1, source_target_pairs={{0,8},{8,0},{16,24},{24,16},{32,40},{40,32},{48,56},{56,48},{64,72... | collective-permute-start | bytes 589832 | tf_op jit(solution)/shard_map/ppermute | solution.py:550
  15.6 0.7 %collective-permute-start.3 = (f32[6,8,1024]{2,1,0:T(8,128)S(1)}, f32[6,8,1024]{2,1,0:T(8,128)S(1)}, u32[]{:S(2)}, u32[]{:S(2)}) collective-permute-start(f32[6,8,1024]{2,1,0:T(8,128)S(1)} %get-tuple-element.34), channel_id=1, source_target_pairs={{8,16},{16,8},{24,32},{32,24},{40,48},{48,40},{56,64},{64,56},{72,... | collective-permute-start | bytes 589832 | tf_op jit(solution)/shard_map/ppermute | solution.py:550
  16.2 5.4 %all-to-all-done.got = f32[8,8,1536]{2,1,0:T(8,128)S(1)} async-done(((f32[8,8,1536]{2,1,0:T(8,128)}), f32[8,8,1536]{2,1,0:T(8,128)S(1)}, u32[]{:S(2)}, u32[]{:S(2)}) %all-to-all-start) | async-done | bytes 393248 | tf_op jit(solution)/shard_map/all_to_all | solution.py:599
  21.6 1.2 %shard_map.57 = f32[16,4,1152]{2,1,0:T(4,128)} custom-call(bf16[64,96]{1,0:T(8,128)(2,1)S(1)} %get-tuple-element.21.w3, bf16[64,192]{1,0:T(8,128)(2,1)S(1)} %get-tuple-element.22.w4, f32[16,1024]{1,0:T(8,128)S(1)} %get-tuple-element.27.cells, f32[16,1024]{1,0:T(8,128)S(1)} %get-tuple-element.28.own, f32[8,8,1536]{2,1,0:T(8,128)S(1)} %all-to-all-done.got), custom_call_target="tpu_custom_call" | custom-call | flops 419430400 | bytes 4194304 | tf_op jit(solution)/shard_map/pallas_call | solution.py:610
  22.9 7.0 %all-to-all-start.1 = ((f32[16,4,1152]{2,1,0:T(4,128)}), f32[16,4,1152]{2,1,0:T(4,128)S(1)}, u32[]{:S(2)}, u32[]{:S(2)}) async-start(f32[16,4,1152]{2,1,0:T(4,128)} %shard_map.57), calls=%async_computation.1 | async-start | bytes 589824 | tf_op jit(solution)/shard_map/all_to_all | solution.py:617
  29.9 0.0 collective-permute-done.2.got_e
  29.9 0.0 collective-permute-done.3.got_o
  29.9 3.2 %shard_map.58 = (f32[16,16,1024]{2,1,0:T(8,128)}, f32[4,16,1024]{2,1,0:T(8,128)S(1)}) custom-call(f32[8,128,128]{2,1,0:T(8,128)S(1)} %get-tuple-element.30.one_s, f32[8,128,128]{2,1,0:T(8,128)S(1)} %get-tuple-element.31.one_d, f32[8,64,128]{2,1,0:T(8,128)S(1)} %get-tuple-element.32.two, f32[6,8,1024]{2,1,0:T(8,128)S(1)} %collective-permute-done.2.got_e, ...), custom_call_target="tpu_custom_call" | custom-call | flops 4194304000 | bytes 4194304 | tf_op jit(solution)/shard_map/pallas_call | solution.py:619
  33.2 5.6 %all-to-all-done.1.got = f32[16,4,1152]{2,1,0:T(4,128)S(1)} async-done(((f32[16,4,1152]{2,1,0:T(4,128)}), f32[16,4,1152]{2,1,0:T(4,128)S(1)}, u32[]{:S(2)}, u32[]{:S(2)}) %all-to-all-start.1) | async-done | bytes 294944 | tf_op jit(solution)/shard_map/all_to_all | solution.py:617
  38.8 1.1 %shard_map.59 = f32[16,16,1024]{2,1,0:T(8,128)} custom-call(f32[16,4,1152]{2,1,0:T(4,128)S(1)} %all-to-all-done.1.got, f32[4,16,1024]{2,1,0:T(8,128)S(1)} %get-tuple-element.35.fourth, f32[16,16,1024]{2,1,0:T(8,128)} %get-tuple-element.36.base), custom_call_target="tpu_custom_call", output_to_operand_aliasing={{}: (2, {})} | custom-call | flops 41943040 | bytes 4194304 | tf_op jit(solution)/shard_map/pallas_call | solution.py:626
Async XLA Ops:
  4.1 8.6 %collective-permute-start = (f32[6,8,1024]{2,1,0:T(8,128)S(1)}, f32[6,8,1024]{2,1,0:T(8,128)S(1)}, u32[]{:S(2)}, u32[]{:S(2)}) collective-permute-start(f32[6,8,1024]{2,1,0:T(8,128)S(1)} %get-tuple-element.25), channel_id=1, source_target_pairs={{0,1},{1,0},{2,3},{3,2},{4,5},{5,4},{6,7},{7,6},{8,9},{9,8},{10,11... | collective-permute-start | bytes 589832 | tf_op jit(solution)/shard_map/ppermute | solution.py:550
  4.2 8.5 %collective-permute-start.1 = (f32[6,8,1024]{2,1,0:T(8,128)S(1)}, f32[6,8,1024]{2,1,0:T(8,128)S(1)}, u32[]{:S(2)}, u32[]{:S(2)}) collective-permute-start(f32[6,8,1024]{2,1,0:T(8,128)S(1)} %get-tuple-element.26), channel_id=1, source_target_pairs={{1,2},{2,1},{3,4},{4,3},{5,6},{6,5},{9,10},{10,9},{11,12},{12,11},... | collective-permute-start | bytes 589832 | tf_op jit(solution)/shard_map/ppermute | solution.py:550
  4.9 16.8 %all-to-all-start = ((f32[8,8,1536]{2,1,0:T(8,128)}), f32[8,8,1536]{2,1,0:T(8,128)S(1)}, u32[]{:S(2)}, u32[]{:S(2)}) async-start(f32[8,8,1536]{2,1,0:T(8,128)} %get-tuple-element.29), calls=%async_computation | async-start | bytes 786432 | tf_op jit(solution)/shard_map/all_to_all | solution.py:599
  14.0 15.9 %collective-permute-start.2 = (f32[6,8,1024]{2,1,0:T(8,128)S(1)}, f32[6,8,1024]{2,1,0:T(8,128)S(1)}, u32[]{:S(2)}, u32[]{:S(2)}) collective-permute-start(f32[6,8,1024]{2,1,0:T(8,128)S(1)} %get-tuple-element.33), channel_id=1, source_target_pairs={{0,8},{8,0},{16,24},{24,16},{32,40},{40,32},{48,56},{56,48},{64,72... | collective-permute-start | bytes 589832 | tf_op jit(solution)/shard_map/ppermute | solution.py:550
  15.6 14.4 %collective-permute-start.3 = (f32[6,8,1024]{2,1,0:T(8,128)S(1)}, f32[6,8,1024]{2,1,0:T(8,128)S(1)}, u32[]{:S(2)}, u32[]{:S(2)}) collective-permute-start(f32[6,8,1024]{2,1,0:T(8,128)S(1)} %get-tuple-element.34), channel_id=1, source_target_pairs={{8,16},{16,8},{24,32},{32,24},{40,48},{48,40},{56,64},{64,56},{72,... | collective-permute-start | bytes 589832 | tf_op jit(solution)/shard_map/ppermute | solution.py:550
  22.9 15.9 %all-to-all-start.1 = ((f32[16,4,1152]{2,1,0:T(4,128)}), f32[16,4,1152]{2,1,0:T(4,128)S(1)}, u32[]{:S(2)}, u32[]{:S(2)}) async-start(f32[16,4,1152]{2,1,0:T(4,128)} %shard_map.57), calls=%async_computation.1 | async-start | bytes 589824 | tf_op jit(solution)/shard_map/all_to_all | solution.py:617

commit v12 on v10

--- a/solution.py
+++ b/solution.py
@@ -291,11 +291,11 @@
         pay[to, :, 0:WIDE] = mix(to > me, right, left)
     parts = [pl.ds(0, WIDE), pl.ds(WIDE, WIDE // 2)]
     sends = [pltpu.make_async_copy(pay.at[:, :, p], result.at[:, :, p], sem.at[4 + k]) for k, p in enumerate(parts)]
-    sends[0].start()
+    sends[0].start(priority=1)
     for to in range(pay.shape[0]):
         pay[to, 0:4, WIDE:] = four[to * 4 : to * 4 + 4, : WIDE // 2]
         pay[to, 4:8, WIDE:] = four[to * 4 : to * 4 + 4, WIDE // 2 :]
-    sends[1].start()
+    sends[1].start(priority=1)
     flip = me % 2 == 1
 
     def column(t):
@@ -401,7 +401,7 @@
     four = product(w4[...], turned4[...])
     for to in range(count):
         pay[to, :, 0:WIDE] = three[to * 4 : to * 4 + 4]
-    sends[0].start()
+    sends[0].start(priority=1)
     lane = lane_id((count, LANES))
     for t in range(TILES // 2):
         v = four[0:count, tile(t)]
@@ -409,7 +409,7 @@
             w = four[k % 4 * count : (k % 4 + 1) * count, tile(t + k // 4 * (TILES // 2))]
             v = jnp.where(lane % 8 == k, pltpu.roll(w, k, 1), v)
         pay[:, t, WIDE:] = v
-    sends[1].start()
+    sends[1].start(priority=1)
     for send in sends:
         send.wait()
 
@@ -444,7 +444,7 @@
         for z, v in enumerate(interleave(*lift(rows, *ends, first, last, mix))):
             fine[pl.ds(z * 8, 8), lanes] = v
 
-    times(TILES, stack, 2)
+    times(TILES, stack, TILES)
     sends = {z: pltpu.make_async_copy(out.at[z], result.at[z], sem.at[z]) for z in range(16) if z % 4}
     for z in range(1, 16, 2):
         sends[z].start()
@@ -485,7 +485,7 @@
     row = lax.broadcasted_iota(jnp.int32, (16, LANES), 0)
     here = (row % 4 == 0) & (lane_id((16, LANES)) % 4 == 0)
     sends = [pltpu.make_async_copy(planes.at[i], result.at[4 * i], sem.at[i]) for i in range(4)]
-    for i in range(4):
+    for i in (1, 3, 0, 2):
         for t in range(TILES):
             planes[i, :, tile(t)] = jnp.where(here, spread[t, pl.ds(i * 16, 16), :], fourth[i, :, tile(t)])
         sends[i].start()

time: 40.1 us -> 40.1 us (level)
  waiting for transfers between devices: 12 us -> 11 us
  Pallas kernels: 9.9 us -> 10.8 us
    all_to_all x1, waiting for transfers between devices: 6.54 us -> 5.61 us  [per_device(): got = lax.all_to_all(pay, 'gz', 0, 0, tiled=True)]
    pallas_call x1, Pallas kernels: 2.3 us -> 3.23 us  [per_device(): call(along_z, [f32(planes, rows, cells), f32(planes // 4, rows, cells)],...]
  transfers between devices with their start and end apart: 6 -> 6, of which waited for: 2 -> 2; matrix products, arithmetic and copies ran while one was open for 0% -> 0% of each run, Pallas kernels for 12% -> 14%
where the time goes in v12:
time: 40.1 us; the launch traced here: 39.8 us
  starting transfers between devices  17.9 us (45%)
  waiting for transfers between devices  11 us (27%)
  Pallas kernels  10.8 us (27%)
    all_to_all x1, starting transfers between devices, per_device(): got = lax.all_to_all(pay, 'gy', 0, 0, tiled=True)  7.83 us
    all_to_all x1, starting transfers between devices, per_device(): got = lax.all_to_all(pay, 'gz', 0, 0, tiled=True)  7.05 us
    all_to_all x1, waiting for transfers between devices, per_device(): got = lax.all_to_all(pay, 'gz', 0, 0, tiled=True)  5.61 us
    all_to_all x1, waiting for transfers between devices, per_device(): got = lax.all_to_all(pay, 'gy', 0, 0, tiled=True)  5.4 us
    pallas_call x1, Pallas kernels, per_device(): call(along_x, [tiled, tiled, payload, payload, f32(16, cells), f32(*pay),...  3.98 us
    pallas_call x1, Pallas kernels, per_device(): call(along_z, [f32(planes, rows, cells), f32(planes // 4, rows, cells)],...  3.23 us
    ppermute x4, starting transfers between devices, swap(): return lax.ppermute(values, axis, pairs)  2.99 us
    pallas_call x1, Pallas kernels, per_device(): call(along_y, [tiled, tiled, f32(TILES, planes * rows // 4, LANES), paylo...  1.28 us
  transfers between devices with their start and end apart: 6, of which 2 were waited for; matrix products, arithmetic and copies ran while one was open for 0% of the time, Pallas kernels for 14%

profile of v12, /device:TPU:0, one launch (start us, length us, event | category | flops | bytes accessed | tf_op | source)
XLA Modules:
  0.0 39.8 jit_solution(13740117636282041063)
XLA Ops:
  0.0 4.0 %shard_map.55 = (f32[8,128,128]{2,1,0:T(8,128)S(1)}, f32[8,128,128]{2,1,0:T(8,128)S(1)}, f32[6,8,1024]{2,1,0:T(8,128)S(1)}, f32[6,8,1024]{2,1,0:T(8,128)S(1)}, f...) custom-call(bf16[8,48,384]{2,1,0:T(8,128)(2,1)} %constant.8.clone.y3, ...), custom_call_target="tpu_custom_call" | custom-call | flops 41943040 | bytes 4194304 | tf_op jit(solution)/shard_map/pallas_call | solution.py:581
  4.0 0.1 collective-permute-start
  4.1 0.7 %collective-permute-start.1 = (f32[6,8,1024]{2,1,0:T(8,128)S(1)}, f32[6,8,1024]{2,1,0:T(8,128)S(1)}, u32[]{:S(2)}, u32[]{:S(2)}) collective-permute-start(f32[6,8,1024]{2,1,0:T(8,128)S(1)} %get-tuple-element.26), channel_id=1, source_target_pairs={{1,2},{2,1},{3,4},{4,3},{5,6},{6,5},{9,10},{10,9},{11,12},{12,11},... | collective-permute-start | bytes 589832 | tf_op jit(solution)/shard_map/ppermute | solution.py:549
  4.8 7.8 %all-to-all-start = ((f32[8,8,1536]{2,1,0:T(8,128)}), f32[8,8,1536]{2,1,0:T(8,128)S(1)}, u32[]{:S(2)}, u32[]{:S(2)}) async-start(f32[8,8,1536]{2,1,0:T(8,128)} %get-tuple-element.29), calls=%async_computation | async-start | bytes 786432 | tf_op jit(solution)/shard_map/all_to_all | solution.py:598
  12.6 0.0 collective-permute-done.got_e
  12.6 0.0 collective-permute-done.1.got_o
  12.6 1.3 %shard_map.56 = (f32[8,128,128]{2,1,0:T(8,128)S(1)}, f32[8,128,128]{2,1,0:T(8,128)S(1)}, f32[8,64,128]{2,1,0:T(8,128)S(1)}, f32[6,8,1024]{2,1,0:T(8,128)S(1)}, f...) custom-call(f32[8,128,128]{2,1,0:T(8,128)S(1)} %get-tuple-element.23.smooth, ...), custom_call_target="tpu_custom_call", output_to_operand_aliasing={{0}: (0, {}), {1}: (1, {})} | custom-call | flops 4194304000 | bytes 4194304 | tf_op jit(solution)/shard_map/pallas_call | solution.py:600
  13.9 1.6 %collective-permute-start.2 = (f32[6,8,1024]{2,1,0:T(8,128)S(1)}, f32[6,8,1024]{2,1,0:T(8,128)S(1)}, u32[]{:S(2)}, u32[]{:S(2)}) collective-permute-start(f32[6,8,1024]{2,1,0:T(8,128)S(1)} %get-tuple-element.33), channel_id=1, source_target_pairs={{0,8},{8,0},{16,24},{24,16},{32,40},{40,32},{48,56},{56,48},{64,72... | collective-permute-start | bytes 589832 | tf_op jit(solution)/shard_map/ppermute | solution.py:549
  15.5 0.7 %collective-permute-start.3 = (f32[6,8,1024]{2,1,0:T(8,128)S(1)}, f32[6,8,1024]{2,1,0:T(8,128)S(1)}, u32[]{:S(2)}, u32[]{:S(2)}) collective-permute-start(f32[6,8,1024]{2,1,0:T(8,128)S(1)} %get-tuple-element.34), channel_id=1, source_target_pairs={{8,16},{16,8},{24,32},{32,24},{40,48},{48,40},{56,64},{64,56},{72,... | collective-permute-start | bytes 589832 | tf_op jit(solution)/shard_map/ppermute | solution.py:549
  16.1 5.4 %all-to-all-done.got = f32[8,8,1536]{2,1,0:T(8,128)S(1)} async-done(((f32[8,8,1536]{2,1,0:T(8,128)}), f32[8,8,1536]{2,1,0:T(8,128)S(1)}, u32[]{:S(2)}, u32[]{:S(2)}) %all-to-all-start) | async-done | bytes 393248 | tf_op jit(solution)/shard_map/all_to_all | solution.py:598
  21.5 1.2 %shard_map.57 = f32[16,4,1152]{2,1,0:T(4,128)} custom-call(bf16[64,96]{1,0:T(8,128)(2,1)S(1)} %get-tuple-element.21.w3, bf16[64,192]{1,0:T(8,128)(2,1)S(1)} %get-tuple-element.22.w4, f32[16,1024]{1,0:T(8,128)S(1)} %get-tuple-element.27.cells, f32[16,1024]{1,0:T(8,128)S(1)} %get-tuple-element.28.own, f32[8,8,1536]{2,1,0:T(8,128)S(1)} %all-to-all-done.got), custom_call_target="tpu_custom_call" | custom-call | flops 419430400 | bytes 4194304 | tf_op jit(solution)/shard_map/pallas_call | solution.py:609
  22.8 7.0 %all-to-all-start.1 = ((f32[16,4,1152]{2,1,0:T(4,128)}), f32[16,4,1152]{2,1,0:T(4,128)S(1)}, u32[]{:S(2)}, u32[]{:S(2)}) async-start(f32[16,4,1152]{2,1,0:T(4,128)} %shard_map.57), calls=%async_computation.1 | async-start | bytes 589824 | tf_op jit(solution)/shard_map/all_to_all | solution.py:616
  29.8 0.0 collective-permute-done.2.got_e
  29.8 0.0 collective-permute-done.3.got_o
  29.8 3.2 %shard_map.58 = (f32[16,16,1024]{2,1,0:T(8,128)}, f32[4,16,1024]{2,1,0:T(8,128)S(1)}) custom-call(f32[8,128,128]{2,1,0:T(8,128)S(1)} %get-tuple-element.30.one_s, f32[8,128,128]{2,1,0:T(8,128)S(1)} %get-tuple-element.31.one_d, f32[8,64,128]{2,1,0:T(8,128)S(1)} %get-tuple-element.32.two, f32[6,8,1024]{2,1,0:T(8,128)S(1)} %collective-permute-done.2.got_e, ...), custom_call_target="tpu_custom_call" | custom-call | flops 4194304000 | bytes 4194304 | tf_op jit(solution)/shard_map/pallas_call | solution.py:618
  33.1 5.6 %all-to-all-done.1.got = f32[16,4,1152]{2,1,0:T(4,128)S(1)} async-done(((f32[16,4,1152]{2,1,0:T(4,128)}), f32[16,4,1152]{2,1,0:T(4,128)S(1)}, u32[]{:S(2)}, u32[]{:S(2)}) %all-to-all-start.1) | async-done | bytes 294944 | tf_op jit(solution)/shard_map/all_to_all | solution.py:616
  38.7 1.1 %shard_map.59 = f32[16,16,1024]{2,1,0:T(8,128)} custom-call(f32[16,4,1152]{2,1,0:T(4,128)S(1)} %all-to-all-done.1.got, f32[4,16,1024]{2,1,0:T(8,128)S(1)} %get-tuple-element.35.fourth, f32[16,16,1024]{2,1,0:T(8,128)} %get-tuple-element.36.base), custom_call_target="tpu_custom_call", output_to_operand_aliasing={{}: (2, {})} | custom-call | flops 41943040 | bytes 4194304 | tf_op jit(solution)/shard_map/pallas_call | solution.py:625
Async XLA Ops:
  4.0 8.6 %collective-permute-start = (f32[6,8,1024]{2,1,0:T(8,128)S(1)}, f32[6,8,1024]{2,1,0:T(8,128)S(1)}, u32[]{:S(2)}, u32[]{:S(2)}) collective-permute-start(f32[6,8,1024]{2,1,0:T(8,128)S(1)} %get-tuple-element.25), channel_id=1, source_target_pairs={{0,1},{1,0},{2,3},{3,2},{4,5},{5,4},{6,7},{7,6},{8,9},{9,8},{10,11... | collective-permute-start | bytes 589832 | tf_op jit(solution)/shard_map/ppermute | solution.py:549
  4.1 8.5 %collective-permute-start.1 = (f32[6,8,1024]{2,1,0:T(8,128)S(1)}, f32[6,8,1024]{2,1,0:T(8,128)S(1)}, u32[]{:S(2)}, u32[]{:S(2)}) collective-permute-start(f32[6,8,1024]{2,1,0:T(8,128)S(1)} %get-tuple-element.26), channel_id=1, source_target_pairs={{1,2},{2,1},{3,4},{4,3},{5,6},{6,5},{9,10},{10,9},{11,12},{12,11},... | collective-permute-start | bytes 589832 | tf_op jit(solution)/shard_map/ppermute | solution.py:549
  4.8 16.8 %all-to-all-start = ((f32[8,8,1536]{2,1,0:T(8,128)}), f32[8,8,1536]{2,1,0:T(8,128)S(1)}, u32[]{:S(2)}, u32[]{:S(2)}) async-start(f32[8,8,1536]{2,1,0:T(8,128)} %get-tuple-element.29), calls=%async_computation | async-start | bytes 786432 | tf_op jit(solution)/shard_map/all_to_all | solution.py:598
  13.9 15.9 %collective-permute-start.2 = (f32[6,8,1024]{2,1,0:T(8,128)S(1)}, f32[6,8,1024]{2,1,0:T(8,128)S(1)}, u32[]{:S(2)}, u32[]{:S(2)}) collective-permute-start(f32[6,8,1024]{2,1,0:T(8,128)S(1)} %get-tuple-element.33), channel_id=1, source_target_pairs={{0,8},{8,0},{16,24},{24,16},{32,40},{40,32},{48,56},{56,48},{64,72... | collective-permute-start | bytes 589832 | tf_op jit(solution)/shard_map/ppermute | solution.py:549
  15.5 14.4 %collective-permute-start.3 = (f32[6,8,1024]{2,1,0:T(8,128)S(1)}, f32[6,8,1024]{2,1,0:T(8,128)S(1)}, u32[]{:S(2)}, u32[]{:S(2)}) collective-permute-start(f32[6,8,1024]{2,1,0:T(8,128)S(1)} %get-tuple-element.34), channel_id=1, source_target_pairs={{8,16},{16,8},{24,32},{32,24},{40,48},{48,40},{56,64},{64,56},{72,... | collective-permute-start | bytes 589832 | tf_op jit(solution)/shard_map/ppermute | solution.py:549
  22.8 15.9 %all-to-all-start.1 = ((f32[16,4,1152]{2,1,0:T(4,128)}), f32[16,4,1152]{2,1,0:T(4,128)S(1)}, u32[]{:S(2)}, u32[]{:S(2)}) async-start(f32[16,4,1152]{2,1,0:T(4,128)} %shard_map.57), calls=%async_computation.1 | async-start | bytes 589824 | tf_op jit(solution)/shard_map/all_to_all | solution.py:616
